TPU v7x, 128 devices: a whole 4x4x4 slice. The times are simulated.
128 devices in a mesh: rep: 2 (over core), shard: 64 (over z, y, x).
Axes of the slice: x: 4, y: 4, z: 4, core: 2. Of those that a mesh axis runs over, the one named last changes fastest.
Arguments:
- gradients: bfloat16 [2, 81920, 1024], P('rep', 'shard')
- owner_table: int32 [80], replicated, may hold values from 0 to 63, as said below
- offsets: int32 [80], replicated, may hold values from 0 to 1264, as said below
- left_root: bfloat16 [128, 1024, 1024], P('shard')
- right_root: bfloat16 [128, 1024, 1024], P('shard', None, 'rep')
Outputs:
- graft_update: bfloat16 [81920, 1024], P('shard', 'rep')
- gram_left: float32 [128, 1024, 1024], P('shard', 'rep')
- gram_right: float32 [128, 1024, 1024], P('shard', 'rep')
Inputs may be any that keep to these rules, and one draw needn't show every extreme that they name: `owner_table`: no owner holds more than 2 blocks, and some owner holds exactly 2. offsets are 16 times a permutation of 0 to 79.
All inputs are finite; a program needn't handle non-finite values.
Results may differ from a plain program's by a relative error of at most 0.0059.
Values may be sent and summed in bfloat16 or wider, within the bound.
No kernel may reach another device: no remote copies, remote signals or barrier semaphores. Data moves between devices by JAX's collectives and lax.ppermute only.
A program may use at most 128 MiB of HBM per device.

v0:
```python
import jax
import jax.numpy as jnp
from jax import lax
from jax.sharding import PartitionSpec as P

EPSILON = 1e-06


def local(gradients, owner_table, offsets, left_root, right_root):
    shard_count = lax.axis_size("shard")
    my_rep = lax.axis_index("rep")
    slot_count = left_root.shape[0]
    block_size = left_root.shape[1]
    strip_size = right_root.shape[2]
    piece_rows = block_size // shard_count
    block_count = offsets.shape[0]
    block_ids = jnp.arange(block_count, dtype=jnp.int32)
    same_owner = owner_table[:, None] == owner_table[None, :]
    before = block_ids[:, None] < block_ids[None, :]
    target = owner_table * slot_count + jnp.sum(
        jnp.where(same_owner & before, 1, 0), axis=0
    ).astype(jnp.int32)
    holder = target[:, None] == jnp.arange(shard_count * slot_count, dtype=jnp.int32)[None, :]
    filled = jnp.any(holder, axis=0)
    first_row = jnp.sum(jnp.where(holder, offsets[:, None], 0), axis=0)
    pick_rows = (first_row[:, None] + jnp.arange(piece_rows, dtype=jnp.int32)[None, :]).reshape(-1)
    summed = lax.psum_scatter(
        gradients[0].astype(jnp.float32).astype(jnp.bfloat16),
        "rep",
        scatter_dimension=1,
        tiled=True,
    )
    picked = jnp.take(summed, pick_rows, axis=0).reshape(
        shard_count * slot_count, piece_rows, summed.shape[1]
    )
    picked = jnp.where(filled[:, None, None], picked, jnp.zeros_like(picked))
    own_strips = lax.all_to_all(
        picked.reshape(shard_count, slot_count, piece_rows, summed.shape[1]),
        "shard",
        split_axis=0,
        concat_axis=2,
        tiled=True,
    ).reshape(slot_count, block_size, strip_size)
    piece_cols = lax.all_gather(own_strips, "rep", axis=2, tiled=True)
    own_rows = lax.dynamic_slice_in_dim(piece_cols, my_rep * strip_size, strip_size, 1)
    left_rows = jnp.einsum("mik,mjk->mij", own_rows, piece_cols, preferred_element_type=jnp.float32)
    cross_term = jnp.einsum(
        "mki,mkj->mij", own_strips, piece_cols, preferred_element_type=jnp.float32
    )
    half_sum = jnp.einsum(
        "mik,mkj->mij", piece_cols, right_root, preferred_element_type=jnp.float32
    )
    gram_left, gram_right, half_sum = (left_rows, cross_term, half_sum)
    precond = jnp.einsum(
        "mik,mkj->mij", left_root, half_sum.astype(jnp.bfloat16), preferred_element_type=jnp.float32
    )
    grad_local = jnp.sum(jnp.square(own_strips.astype(jnp.float32)), axis=(1, 2))
    pre_local = jnp.sum(precond * precond, axis=(1, 2))
    grad_sq, pre_sq = lax.psum((grad_local, pre_local), "rep")
    entries = float(block_size * block_size)
    graft_scale = jnp.sqrt(grad_sq / entries / (pre_sq / entries + EPSILON))
    outgoing = (precond * graft_scale[:, None, None]).astype(jnp.bfloat16)
    outgoing = outgoing.reshape(slot_count, shard_count, piece_rows, strip_size)
    returned = lax.all_to_all(outgoing, "shard", split_axis=1, concat_axis=0, tiled=True)
    returned = returned.reshape(shard_count * slot_count * piece_rows, strip_size)
    position = offsets // piece_rows
    at_position = position[None, :] == block_ids[:, None]
    source_slot = jnp.sum(jnp.where(at_position, target[None, :], 0), axis=1)
    row_index = (
        source_slot[:, None] * piece_rows + jnp.arange(piece_rows, dtype=jnp.int32)[None, :]
    ).reshape(-1)
    graft_update = jnp.take(returned, row_index, axis=0)
    return (graft_update, gram_left, gram_right)


def solution(mesh):
    in_specs = (P("rep", "shard", None), P(), P(), P("shard", None, None), P("shard", None, "rep"))
    out_specs = (P("shard", "rep"), P("shard", "rep", None), P("shard", "rep", None))
    return jax.shard_map(local, mesh=mesh, in_specs=in_specs, out_specs=out_specs, check_vma=False)
```

profile of v0, /device:TPU:1, one launch (start us, length us, event | category | flops | bytes accessed | tf_op | source)
XLA Modules:
  0.0 173.0 jit_solution(13019763180372696962)
XLA Ops:
  7.2 0.0 copy-start
  7.2 0.0 copy-start.3
  7.2 0.0 copy-start.4
  7.2 0.0 reduce-scatter.2.cloned.1.call-start
  7.2 0.7 reduce-scatter.2.cloned.1.call-update
  7.9 0.0 all-gather.2.cloned.1.call-start
  8.0 0.0 copy-done.3
  8.0 0.1 select_reduce_fusion.2
  8.1 0.0 copy-done.4
  8.1 0.1 select_reduce_fusion
  8.2 0.1 add.130
  8.4 0.1 iota_add_fusion
  8.4 0.1 add.139
  8.5 0.1 fusion.7
  8.6 0.2 broadcast_in_dim.83
  8.8 0.2 compare_and_fusion
  9.0 18.0 %reduce-scatter.2.cloned.1.call-done = bf16[1280,512]{1,0:T(8,128)(2,1)} async-done(((bf16[1280,1024]{1,0:T(8,128)(2,1)}), bf16[1280,512]{1,0:T(8,128)(2,1)}) %reduce-scatter.2.cloned.1.call-update) | async-done | bytes 1310736 | tf_op jit(solution)/shard_map/reduce_scatter | solution.py:27
  26.9 10.7 %gather_fusion = bf16[2048,512]{1,0:T(8,128)(2,1)} fusion(bf16[1280,512]{1,0:T(8,128)(2,1)} %reduce-scatter.2.cloned.1.call-done, s32[2048]{0:T(1024)S(1)} %broadcast_clamp_fusion), kind=kCustom, calls=%fused_computation | custom fusion | bytes 4202496 | tf_op jit(solution)/shard_map/jit(_take)/gather | solution.py:33
  37.7 1.8 %select_select_fusion = bf16[64,2,16,512]{3,2,1,0:T(8,128)(2,1)S(1)} fusion(bf16[64,2,16,512]{3,2,1,0:T(8,128)(2,1)} %bitcast.23, pred[64,2,16]{2,1,0:T(4,128)(4,1)S(1)} %compare_and_fusion, pred[64,2]{1,0:T(8,128)(4,1)S(1)} %broadcast_in_dim.83), kind=kLoop, calls=%fused_computation.10 | loop fusion | flops 2097152 | bytes 4196480 | tf_op jit(solution)/shard_map/jit(_where)/select_n | solution.py:36
  39.5 39.0 %all_to_all.30 = bf16[64,2,16,512]{3,2,1,0:T(8,128)(2,1)S(1)} all-to-all(bf16[64,2,16,512]{3,2,1,0:T(8,128)(2,1)S(1)} %select_select_fusion), channel_id=1, replica_groups=mesh['rep'=2,'shard'=64] {'shard'}, dimensions={0} | all-to-all | bytes 4194304 | tf_op jit(solution)/shard_map/all_to_all | solution.py:37
  78.6 0.0 copy-start.1
  78.6 1.7 copy.24
  80.2 0.4 copy-done.1
  80.6 0.0 all-gather.2.cloned.1.call-update
  80.6 0.1 select_reduce_fusion.1
  80.7 2.3 %multiply_reduce_fusion.1 = f32[2]{0:T(128)S(1)} fusion(bf16[64,2,16,512]{3,2,1,0:T(8,128)(2,1)} %copy-done.1), kind=kLoop, calls=%fused_computation.4 | loop fusion | flops 3145726 | bytes 2097160 | tf_op jit(solution)/shard_map/reduce_sum | solution.py:57
  83.0 12.5 %all-gather.2.cloned.1.call-done = bf16[2,1024,1024]{2,1,0:T(8,128)(2,1)} async-done(((bf16[2,1024,512]{2,1,0:T(8,128)(2,1)}), bf16[2,1024,1024]{2,1,0:T(8,128)(2,1)}) %all-gather.2.cloned.1.call-update) | async-done | bytes 4194320 | tf_op jit(solution)/shard_map/all_gather | solution.py:44
  95.4 0.0 copy-done
  95.4 10.1 %multiply_reduce_fusion = (f32[2]{0:T(128)S(1)}, f32[2,512,1024]{2,1,0:T(8,128)}) fusion(bf16[2,1024,1024]{2,1,0:T(8,128)(2,1)} %param.8, bf16[2,1024,1024]{2,1,0:T(8,128)(2,1)} %all-gather.2.cloned.1.call-done, bf16[2,1024,512]{2,1,0:T(8,128)(2,1)S(1)} %copy-done), kind=kOutput, calls=%fused_computation.3 | convolution fusion | flops 4298113024 | bytes 14680072 | tf_op jit(solution)/shard_map/mik,mkj->mij/dot_general | solution.py:54
  105.5 2.5 %all-reduce = (f32[2]{0:T(128)S(1)}, f32[2]{0:T(128)S(1)}) all-reduce(f32[2]{0:T(128)S(1)} %get-tuple-element.5, f32[2]{0:T(128)S(1)} %multiply_reduce_fusion.1), channel_id=1, replica_groups=mesh['rep'=2,'shard'=64] {'rep'}, use_global_device_ids=true, to_apply=%region_8.9 | all-reduce | flops 4 | bytes 32 | tf_op jit(solution)/shard_map/psum | solution.py:59
  108.0 4.1 %fusion = bf16[2,1024,512]{1,2,0:T(8,128)(2,1)} fusion(f32[2,512,1024]{2,1,0:T(8,128)} %get-tuple-element.6, f32[2]{0:T(128)S(1)} %fusion.10), kind=kLoop, calls=%fused_computation.5 | loop fusion | flops 2097152 | bytes 6291464 | tf_op jit(solution)/shard_map/convert_element_type | solution.py:62
  112.1 3.9 %copy.26 = bf16[2,1024,512]{2,1,0:T(8,128)(2,1)} copy(bf16[2,1024,512]{1,2,0:T(8,128)(2,1)} %fusion) | data formatting | bytes 4194304 | tf_op jit(solution)/shard_map/convert_element_type | solution.py:62
  116.1 3.2 %copy.27 = bf16[2,64,16,512]{3,2,0,1:T(8,128)(2,1)} copy(bf16[2,64,16,512]{3,2,1,0:T(8,128)(2,1)} %bitcast.26) | data formatting | bytes 4194304 | tf_op jit(solution)/shard_map/reshape | solution.py:63
  119.3 10.6 %all-to-all-start.1 = ((bf16[2,64,16,512]{3,2,0,1:T(8,128)(2,1)}), bf16[2,64,16,512]{3,2,0,1:T(8,128)(2,1)}, u32[]{:S(2)}, u32[]{:S(2)}) async-start(bf16[2,64,16,512]{3,2,0,1:T(8,128)(2,1)} %copy.27), calls=%async_computation.2 | async-start | bytes 4194304 | tf_op jit(solution)/shard_map/all_to_all | solution.py:64
  129.9 0.1 iota_add_fusion.1
  129.9 0.1 add.143
  130.0 0.1 add.127
  130.2 0.0 copy-start.2
  130.2 0.0 copy-start.5
  130.2 7.4 %fusion.1 = f32[2,512,1024]{2,1,0:T(8,128)} fusion(bf16[2,1024,1024]{2,1,0:T(8,128)(2,1)} %all-gather.2.cloned.1.call-done, s32[]{:T(128)S(6)} %select_n.79), kind=kOutput, calls=%fused_computation.6 | convolution fusion | flops 2147483648 | bytes 10485764 | tf_op jit(solution)/shard_map/mik,mjk->mij/dot_general | solution.py:46
  137.6 0.0 copy-done.2
  137.6 0.0 copy-done.5
  137.6 4.4 %fusion.12 = f32[2,512,1024]{2,1,0:T(8,128)} fusion(bf16[2,1024,512]{2,1,0:T(8,128)(2,1)S(1)} %bitcast.25, bf16[2,1024,1024]{2,1,0:T(8,128)(2,1)S(1)} %copy-done.5), kind=kOutput, calls=%fused_computation.41 | convolution fusion | flops 2147483648 | bytes 10485760 | tf_op jit(solution)/shard_map/mki,mkj->mij/dot_general | solution.py:47
  142.0 16.9 %all-to-all-done.1 = bf16[2,64,16,512]{3,2,0,1:T(8,128)(2,1)} async-done(((bf16[2,64,16,512]{3,2,0,1:T(8,128)(2,1)}), bf16[2,64,16,512]{3,2,0,1:T(8,128)(2,1)}, u32[]{:S(2)}, u32[]{:S(2)}) %all-to-all-start.1) | async-done | bytes 2097184 | tf_op jit(solution)/shard_map/all_to_all | solution.py:64
  158.9 6.0 %gather_fusion.1 = bf16[1280,512]{1,0:T(8,128)(2,1)S(1)} fusion(bf16[2048,512]{1,0:T(8,128)(2,1)} %bitcast.11, s32[2048]{0:T(1024)S(1)} %pad_clamp_fusion), kind=kCustom, calls=%fused_computation.1 | custom fusion | bytes 2626560 | tf_op jit(solution)/shard_map/jit(_take)/gather | solution.py:72
  164.9 1.3 broadcast_select_fusion
  (8 shorter events, 0.1 us)
Async XLA Ops:
  7.2 88.3 %copy-start = (bf16[2,1024,512]{2,1,0:T(8,128)(2,1)S(1)}, bf16[2,1024,512]{2,1,0:T(8,128)(2,1)}, u32[]{:S(2)}) copy-start(bf16[2,1024,512]{2,1,0:T(8,128)(2,1)} %param.9) | copy-start | bytes 6291460
  7.2 0.8 copy-start.3
  7.2 0.9 copy-start.4
  7.2 19.7 %reduce-scatter.2.cloned.1.call-start = ((), (), s32[]{:S(2)}) async-start(), calls=%async_computation.3 | async-start | bytes 3932160 | tf_op jit(solution)/shard_map/reduce_scatter | solution.py:27
  7.9 87.5 %all-gather.2.cloned.1.call-start = ((), (), s32[]{:S(2)}) async-start(), calls=%async_computation.4 | async-start | bytes 6291456 | tf_op jit(solution)/shard_map/all_gather | solution.py:44
  78.6 2.0 %copy-start.1 = (bf16[64,2,16,512]{3,2,1,0:T(8,128)(2,1)}, bf16[64,2,16,512]{3,2,1,0:T(8,128)(2,1)S(1)}, u32[]{:S(2)}) copy-start(bf16[64,2,16,512]{3,2,1,0:T(8,128)(2,1)S(1)} %all_to_all.30) | copy-start | bytes 6291460
  119.3 39.6 %all-to-all-start.1 = ((bf16[2,64,16,512]{3,2,0,1:T(8,128)(2,1)}), bf16[2,64,16,512]{3,2,0,1:T(8,128)(2,1)}, u32[]{:S(2)}, u32[]{:S(2)}) async-start(bf16[2,64,16,512]{3,2,0,1:T(8,128)(2,1)} %copy.27), calls=%async_computation.2 | async-start | bytes 4194304 | tf_op jit(solution)/shard_map/all_to_all | solution.py:64
  130.2 7.4 %copy-start.2 = (bf16[1,2,64,16,512]{4,3,2,1,0:T(8,128)(2,1)S(1)}, bf16[1,2,64,16,512]{4,3,2,1,0:T(8,128)(2,1)}, u32[]{:S(2)}) copy-start(bf16[1,2,64,16,512]{4,3,2,1,0:T(8,128)(2,1)} %copy.24) | copy-start | bytes 6291460
  130.2 7.4 %copy-start.5 = (bf16[2,1024,1024]{2,1,0:T(8,128)(2,1)S(1)}, bf16[2,1024,1024]{2,1,0:T(8,128)(2,1)}, u32[]{:S(2)}) copy-start(bf16[2,1024,1024]{2,1,0:T(8,128)(2,1)} %all-gather.2.cloned.1.call-done) | copy-start | bytes 12582916
Sparse Core Ops, SparseCore 0:
  10.4 16.5 reduce-scatter.1
  80.7 14.6 all-gather.1
where the time goes:
time: 174 us; the launch traced here: 173 us
  waiting for transfers between devices  48 us (28%)
  blocking collectives  41.5 us (24%)
  local copies, waits for them, and re-layouts  26.5 us (15%)
  matrix products  21.9 us (13%)
  between operations  14.2 us (8%)
  starting transfers between devices  10.6 us (6%)
  other arithmetic  10.3 us (6%)
    all_to_all x1, blocking collectives, local(): lax.all_to_all(picked.reshape(shard_count, slot_count, piece_rows, summed...  39 us
    reduce_scatter x1, waiting for transfers between devices, local(): lax.psum_scatter(gradients[0].astype(jnp.float32).astype(jnp.bfloat16), '...  18 us
    all_to_all x1, waiting for transfers between devices, local(): lax.all_to_all(outgoing, 'shard', split_axis=1, concat_axis=0, tiled=True)  16.9 us
    all_gather x1, waiting for transfers between devices, local(): piece_cols = lax.all_gather(own_strips, 'rep', axis=2, tiled=True)  12.5 us
    gather x1, local copies, waits for them, and re-layouts, local(): jnp.take(summed, pick_rows, axis=0)  10.7 us
    all_to_all x1, starting transfers between devices, local(): lax.all_to_all(outgoing, 'shard', split_axis=1, concat_axis=0, tiled=True)  10.6 us
    dot_general x1, matrix products, local(): jnp.einsum('mik,mkj->mij', left_root, half_sum.astype(jnp.bfloat16), pref...  10.1 us
    dot_general x1, matrix products, local(): jnp.einsum('mik,mjk->mij', own_rows, piece_cols, preferred_element_type=j...  7.36 us
  transfers between devices with their start and end apart: 3, of which 3 were waited for; matrix products, arithmetic and copies ran while one was open for 9% of the time, Pallas kernels for 0%

commit v1 on v0

v1 whole, which is shorter than its diff:
```python
import functools

import jax
import jax.numpy as jnp
from jax import lax
from jax.experimental import pallas as pl
from jax.experimental.pallas import tpu as pltpu
from jax.sharding import PartitionSpec as P

EPSILON = 1e-06
VMEM_BYTES = 48 * 1024 * 1024
NT = (((1,), (1,)), ((), ()))
TN = (((0,), (0,)), ((), ()))
SWAP = [(0, 1), (1, 0)]


def cost(flops, nbytes):
    return pl.CostEstimate(flops=flops, bytes_accessed=nbytes, transcendentals=0)


def params():
    return pltpu.CompilerParams(vmem_limit_bytes=VMEM_BYTES)


def pack_kernel(slot, slots, piece, place_ref, rep_ref, mine_ref, theirs_ref, out_ref):
    def step(owner, carry):
        where = place_ref[owner * slots + slot]
        row = pl.multiple_of(jnp.maximum(where, 0) * piece, piece)
        total = mine_ref[pl.ds(row, piece), :].astype(jnp.float32) + theirs_ref[
            pl.ds(row, piece), :
        ].astype(jnp.float32)
        total = jnp.where(where >= 0, total, 0.0).astype(out_ref.dtype)
        out_ref[pl.ds(pl.multiple_of(owner * piece, piece), piece), :] = total
        return carry

    lax.fori_loop(0, out_ref.shape[0] // piece, step, 0, unroll=8)


def pack(slot, slots, piece, block, place, rep, mine, theirs):
    rows, strip = theirs.shape
    return pl.pallas_call(
        functools.partial(pack_kernel, slot, slots, piece),
        grid_spec=pltpu.PrefetchScalarGridSpec(
            num_scalar_prefetch=2,
            grid=(1,),
            in_specs=[
                pl.BlockSpec((rows, strip), lambda i, place, rep: (0, rep[0])),
                pl.BlockSpec((rows, strip), lambda i, place, rep: (0, 0)),
            ],
            out_specs=pl.BlockSpec((block, strip), lambda i, place, rep: (0, 0)),
        ),
        out_shape=jax.ShapeDtypeStruct((block, strip), theirs.dtype),
        compiler_params=params(),
        cost_estimate=cost(rows * strip, 2 * (2 * rows + block) * strip),
        name="pack",
    )(place, rep, mine, theirs)


def root_kernel(steps, rep_ref, own_ref, oth_ref, right_own, right_oth, left_ref, pre_ref, sums_ref, half):
    i = pl.program_id(0)
    tile = own_ref.shape[0]

    @pl.when(i == 0)
    def _():
        sums_ref[...] = jnp.zeros_like(sums_ref)

    @pl.when(i < steps)
    def _():
        own = own_ref[...]
        acc = jnp.dot(own, right_own[0], preferred_element_type=jnp.float32)
        acc += jnp.dot(oth_ref[...], right_oth[0], preferred_element_type=jnp.float32)
        half[pl.ds(pl.multiple_of(i * tile, tile), tile), :] = acc.astype(half.dtype)
        wide = own.astype(jnp.float32)
        sums_ref[0:1, :] += jnp.sum(wide * wide, axis=0, keepdims=True)

    @pl.when(i >= steps)
    def _():
        pre = jnp.dot(left_ref[0], half[...], preferred_element_type=jnp.float32)
        pre_ref[...] = pre
        sums_ref[1:2, :] += jnp.sum(pre * pre, axis=0, keepdims=True)


def apply_roots(slot, rep, own, oth, left_root, right_root):
    block, strip = own.shape
    steps = 2
    tile = block // steps
    return pl.pallas_call(
        functools.partial(root_kernel, steps),
        grid_spec=pltpu.PrefetchScalarGridSpec(
            num_scalar_prefetch=1,
            grid=(2 * steps,),
            in_specs=[
                pl.BlockSpec((tile, strip), lambda i, rep: (jnp.minimum(i, steps - 1), 0)),
                pl.BlockSpec((tile, strip), lambda i, rep: (jnp.minimum(i, steps - 1), 0)),
                pl.BlockSpec((1, strip, strip), lambda i, rep: (slot, rep[0], 0)),
                pl.BlockSpec((1, strip, strip), lambda i, rep: (slot, 1 - rep[0], 0)),
                pl.BlockSpec((1, tile, block), lambda i, rep: (slot, jnp.maximum(i - steps, 0), 0)),
            ],
            out_specs=[
                pl.BlockSpec((tile, strip), lambda i, rep: (jnp.maximum(i - steps, 0), 0)),
                pl.BlockSpec((8, strip), lambda i, rep: (0, 0)),
            ],
            scratch_shapes=[pltpu.VMEM((block, strip), jnp.bfloat16)],
        ),
        out_shape=[
            jax.ShapeDtypeStruct((block, strip), jnp.float32),
            jax.ShapeDtypeStruct((8, strip), jnp.float32),
        ],
        compiler_params=params(),
        cost_estimate=cost(4 * block * block * strip, 2 * block * (5 * strip + block)),
        name="roots",
    )(rep, own, oth, right_root, right_root, left_root)


def scale_kernel(entries, pre_ref, mine_ref, theirs_ref, out_ref):
    grad_sq = jnp.sum(mine_ref[0:1, :]) + jnp.sum(theirs_ref[0:1, :])
    pre_sq = jnp.sum(mine_ref[1:2, :]) + jnp.sum(theirs_ref[1:2, :])
    top = jnp.full((8, 128), grad_sq, jnp.float32) / entries
    bottom = jnp.full((8, 128), pre_sq, jnp.float32) / entries + EPSILON
    scale = jnp.sqrt(top / bottom)[0:1, 0:1]
    out_ref[...] = (pre_ref[...] * scale).astype(out_ref.dtype)


def apply_scale(pre, mine, theirs):
    block, strip = pre.shape
    steps = 4
    tile = block // steps
    return pl.pallas_call(
        functools.partial(scale_kernel, float(block * block)),
        grid=(steps,),
        in_specs=[
            pl.BlockSpec((tile, strip), lambda i: (i, 0)),
            pl.BlockSpec(mine.shape, lambda i: (0, 0)),
            pl.BlockSpec(mine.shape, lambda i: (0, 0)),
        ],
        out_specs=pl.BlockSpec((tile, strip), lambda i: (i, 0)),
        out_shape=jax.ShapeDtypeStruct((block, strip), jnp.bfloat16),
        compiler_params=params(),
        cost_estimate=cost(2 * block * strip, 6 * block * strip),
        name="graft",
    )(pre, mine, theirs)


def gram_kernel(steps, rep_ref, own_ref, oth_ref, *rest):
    left_out, right_out = rest[-2:]
    i = pl.program_id(0)
    rep = rep_ref[0]
    strip = own_ref.shape[1]
    tile = strip // steps
    row = pl.multiple_of(rep * strip + i * tile, tile)
    left = lax.dot_general(
        own_ref[pl.ds(row, tile), :], own_ref[...], NT, preferred_element_type=jnp.float32
    )
    left += lax.dot_general(
        oth_ref[pl.ds(row, tile), :], oth_ref[...], NT, preferred_element_type=jnp.float32
    )
    left_out[0] = left
    col = pl.multiple_of(i * tile, tile)
    mine = own_ref[:, pl.ds(col, tile)]
    here = pl.multiple_of(rep * strip, strip)
    there = pl.multiple_of((1 - rep) * strip, strip)
    right_out[0, :, pl.ds(here, strip)] = lax.dot_general(
        mine, own_ref[...], TN, preferred_element_type=jnp.float32
    )
    right_out[0, :, pl.ds(there, strip)] = lax.dot_general(
        mine, oth_ref[...], TN, preferred_element_type=jnp.float32
    )


def grams(slot, slots, rep, own, oth, previous):
    block, strip = own.shape
    steps = 2
    tile = strip // steps
    out = jax.ShapeDtypeStruct((slots, strip, block), jnp.float32)
    return pl.pallas_call(
        functools.partial(gram_kernel, steps),
        grid_spec=pltpu.PrefetchScalarGridSpec(
            num_scalar_prefetch=1,
            grid=(steps,),
            in_specs=[
                pl.BlockSpec((block, strip), lambda i, rep: (0, 0)),
                pl.BlockSpec((block, strip), lambda i, rep: (0, 0)),
            ]
            + [pl.BlockSpec(memory_space=pl.ANY)] * len(previous),
            out_specs=[pl.BlockSpec((1, tile, block), lambda i, rep: (slot, i, 0))] * 2,
        ),
        out_shape=[out, out],
        input_output_aliases={3 + k: k for k in range(len(previous))},
        compiler_params=params(),
        cost_estimate=cost(4 * block * block * strip, 4 * block * strip + 8 * block * strip),
        name="grams",
    )(rep, own, oth, *previous)


def place_kernel(slot, slots, piece, place_ref, blocks_ref, *rest):
    out_ref, sems = rest[-2:]
    count = blocks_ref.shape[0]

    def copy(owner):
        where = place_ref[owner * slots + slot]
        row = pl.multiple_of(jnp.maximum(where, 0) * piece, piece)
        return where, pltpu.make_async_copy(
            blocks_ref.at[owner], out_ref.at[pl.ds(row, piece), :], sems.at[owner]
        )

    def start(owner, carry):
        where, move = copy(owner)

        @pl.when(where >= 0)
        def _():
            move.start()

        return carry

    def finish(owner, carry):
        where, move = copy(owner)

        @pl.when(where >= 0)
        def _():
            move.wait()

        return carry

    lax.fori_loop(0, count, start, 0, unroll=4)
    lax.fori_loop(0, count, finish, 0, unroll=4)


def place_rows(slot, slots, rows, place, blocks, previous):
    count, piece, strip = blocks.shape
    return pl.pallas_call(
        functools.partial(place_kernel, slot, slots, piece),
        grid_spec=pltpu.PrefetchScalarGridSpec(
            num_scalar_prefetch=1,
            grid=(1,),
            in_specs=[pl.BlockSpec(memory_space=pl.ANY)] * (1 + len(previous)),
            out_specs=pl.BlockSpec(memory_space=pl.ANY),
            scratch_shapes=[pltpu.SemaphoreType.DMA((count,))],
        ),
        out_shape=jax.ShapeDtypeStruct((rows, strip), blocks.dtype),
        input_output_aliases={2 + k: k for k in range(len(previous))},
        compiler_params=params(),
        cost_estimate=cost(0, 4 * count * piece * strip),
        name="place",
    )(place, blocks, *previous)


def local(gradients, owner_table, offsets, left_root, right_root):
    shard_count = lax.axis_size("shard")
    slots, block = left_root.shape[:2]
    strip = right_root.shape[2]
    piece = block // shard_count
    rows = gradients.shape[1]
    block_ids = jnp.arange(offsets.shape[0], dtype=jnp.int32)
    me = lax.axis_index("rep").astype(jnp.int32)
    rep = me.reshape(1)

    mine = gradients[0]
    theirs = lax.ppermute(
        lax.dynamic_slice_in_dim(mine, (1 - me) * strip, strip, 1), "rep", SWAP
    )
    same_owner = owner_table[:, None] == owner_table[None, :]
    before = block_ids[:, None] < block_ids[None, :]
    rank = jnp.sum(jnp.where(same_owner & before, 1, 0), axis=0).astype(jnp.int32)
    target = owner_table * slots + rank
    slot_ids = jnp.arange(shard_count * slots, dtype=jnp.int32)
    holder = target[:, None] == slot_ids[None, :]
    place = jnp.sum(jnp.where(holder, (offsets // piece)[:, None] + 1, 0), axis=0) - 1
    place = place.astype(jnp.int32)

    def exchange(x):
        x = x.reshape(shard_count, piece, strip)
        return lax.all_to_all(x, "shard", split_axis=0, concat_axis=0, tiled=True)

    own = [
        exchange(pack(slot, slots, piece, block, place, rep, mine, theirs)).reshape(block, strip)
        for slot in range(slots)
    ]
    oth = [lax.ppermute(x, "rep", SWAP) for x in own]
    back = []
    for slot in range(slots):
        pre, sums = apply_roots(slot, rep, own[slot], oth[slot], left_root, right_root)
        other_sums = lax.ppermute(sums, "rep", SWAP)
        back.append(exchange(apply_scale(pre, sums, other_sums)))
    gram = ()
    update = ()
    for slot in range(slots):
        gram = tuple(grams(slot, slots, rep, own[slot], oth[slot], gram))
        update = (place_rows(slot, slots, rows, place, back[slot], update),)
    return (update[0], *gram)


def solution(mesh):
    in_specs = (P("rep", "shard", None), P(), P(), P("shard", None, None), P("shard", None, "rep"))
    out_specs = (P("shard", "rep"), P("shard", "rep", None), P("shard", "rep", None))
    return jax.shard_map(local, mesh=mesh, in_specs=in_specs, out_specs=out_specs, check_vma=False)
```

time: 174 us -> 122 us (0.70)
  Pallas kernels: 0 us -> 29.4 us
  matrix products: 21.9 us -> 0 us
  local copies, waits for them, and re-layouts: 26.5 us -> 6.05 us
  blocking collectives: 41.5 us -> 23.3 us
  starting transfers between devices: 10.6 us -> 26 us
  waiting for transfers between devices: 48 us -> 34.2 us
  between operations: 14.2 us -> 0.84 us
  other arithmetic: 10.3 us -> 0.21 us
    pallas_call x0 -> x10, Pallas kernels: none -> 29.4 us  [the longest x2 10.9 us: apply_roots(): pl.pallas_call(functools.partial(root_kernel, steps), grid_spec=pltpu.Pre...]
    dot_general x3 -> x0, matrix products: 21.9 us -> none  [the longest x1 10.1 us: local(): jnp.einsum('mik,mkj->mij', left_root, half_sum.astype(jnp.bfloat16), pref...]
    reduce_scatter x1 -> x0, waiting for transfers between devices: 18 us -> none  [local(): lax.psum_scatter(gradients[0].astype(jnp.float32).astype(jnp.bfloat16), '...]
    gather x2 -> x0, local copies, waits for them, and re-layouts: 16.7 us -> none  [the longest x1 10.7 us: local(): jnp.take(summed, pick_rows, axis=0)]
    all_to_all x1, blocking collectives: 39 us -> 23.3 us  [exchange(): return lax.all_to_all(x, 'shard', split_axis=0, concat_axis=0, tiled=True)]
    all_to_all x1 -> x3, waiting for transfers between devices: 16.9 us -> 29.7 us  [exchange(): return lax.all_to_all(x, 'shard', split_axis=0, concat_axis=0, tiled=True)]
    all_gather x1 -> x0, waiting for transfers between devices: 12.5 us -> none  [local(): piece_cols = lax.all_gather(own_strips, 'rep', axis=2, tiled=True)]
    all_to_all x1 -> x3, starting transfers between devices: 10.6 us -> 21 us  [exchange(): return lax.all_to_all(x, 'shard', split_axis=0, concat_axis=0, tiled=True)]
  transfers between devices with their start and end apart: 3 -> 8, of which waited for: 3 -> 6; matrix products, arithmetic and copies ran while one was open for 9% -> 0% of each run, Pallas kernels for 0% -> 22%
where the time goes in v1:
time: 122 us; the launch traced here: 120 us
  waiting for transfers between devices  34.2 us (28%)
  Pallas kernels  29.4 us (24%)
  starting transfers between devices  26 us (21%)
  blocking collectives  23.3 us (19%)
  local copies, waits for them, and re-layouts  6.05 us (5%)
    all_to_all x3, waiting for transfers between devices, exchange(): return lax.all_to_all(x, 'shard', split_axis=0, concat_axis=0, tiled=True)  29.7 us
    all_to_all x1, blocking collectives, exchange(): return lax.all_to_all(x, 'shard', split_axis=0, concat_axis=0, tiled=True)  23.3 us
    all_to_all x3, starting transfers between devices, exchange(): return lax.all_to_all(x, 'shard', split_axis=0, concat_axis=0, tiled=True)  21 us
    pallas_call x2, Pallas kernels, apply_roots(): pl.pallas_call(functools.partial(root_kernel, steps), grid_spec=pltpu.Pre...  10.9 us
    pallas_call x2, Pallas kernels, grams(): pl.pallas_call(functools.partial(gram_kernel, steps), grid_spec=pltpu.Pre...  8.43 us
    unnamed x22, local copies, waits for them, and re-layouts  4.49 us
    pallas_call x2, Pallas kernels, place_rows(): pl.pallas_call(functools.partial(place_kernel, slot, slots, piece), grid_...  4.11 us
    pallas_call x2, Pallas kernels, apply_scale(): pl.pallas_call(functools.partial(scale_kernel, float(block * block)), gri...  3.93 us
  transfers between devices with their start and end apart: 8, of which 6 were waited for; matrix products, arithmetic and copies ran while one was open for 0% of the time, Pallas kernels for 22%

profile of v1, /device:TPU:1, one launch (start us, length us, event | category | flops | bytes accessed | tf_op | source)
XLA Modules:
  0.0 120.1 jit_solution(798888419619802461)
XLA Ops:
  0.6 0.0 copy-start
  0.6 0.0 copy-start.10
  0.7 0.0 copy-start.9
  0.7 1.6 %dynamic-slice_bitcast_fusion = bf16[1280,512]{1,0:T(8,128)(2,1)S(1)} fusion(bf16[1,1280,1024]{2,1,0:T(8,128)(2,1)} %param.5, s32[]{:T(128)S(6)} %select_n.19), kind=kLoop, calls=%fused_computation | loop fusion | bytes 2621444 | tf_op jit(solution)/shard_map/dynamic_slice | solution.py:259
  2.2 1.5 %collective-permute-start = (bf16[1280,512]{1,0:T(8,128)(2,1)S(1)}, bf16[1280,512]{1,0:T(8,128)(2,1)S(1)}, u32[]{:S(2)}, u32[]{:S(2)}) collective-permute-start(bf16[1280,512]{1,0:T(8,128)(2,1)S(1)} %dynamic-slice_bitcast_fusion), channel_id=1, source_target_pairs={{0,64},{64,0},{1,65},{65,1},{2,66},{66,2},{3,67},{67,3},{4,68},{68... | collective-permute-start | bytes 3932168 | tf_op jit(solution)/shard_map/ppermute | solution.py:258
  3.7 0.0 copy-done.10
  3.7 0.1 select_reduce_fusion.1
  3.8 0.0 copy-done.9
  3.8 0.1 select_reduce_fusion
  4.0 2.4 %collective-permute-done.theirs_ref = bf16[1280,512]{1,0:T(8,128)(2,1)S(1)} collective-permute-done((bf16[1280,512]{1,0:T(8,128)(2,1)S(1)}, bf16[1280,512]{1,0:T(8,128)(2,1)S(1)}, u32[]{:S(2)}, u32[]{:S(2)}) %collective-permute-start) | collective-permute-done | bytes 1310752 | tf_op jit(solution)/shard_map/ppermute | solution.py:258
  6.4 0.0 copy-start.1
  6.4 0.0 copy-done
  6.4 1.0 pack.3
  7.5 0.0 copy-done.1
  7.5 0.0 copy-start.4
  7.5 1.0 copy-done.4
  8.4 11.5 %all-to-all-start.2 = ((bf16[64,16,512]{2,1,0:T(8,128)(2,1)}), bf16[64,16,512]{2,1,0:T(8,128)(2,1)}, u32[]{:S(2)}, u32[]{:S(2)}) async-start(bf16[64,16,512]{2,1,0:T(8,128)(2,1)} %bitcast.16), calls=%async_computation.2 | async-start | bytes 2097152 | tf_op jit(solution)/shard_map/all_to_all | solution.py:272
  19.9 0.0 copy-start.2
  19.9 1.3 %copy-done.2 = bf16[1280,512]{1,0:T(8,128)(2,1)S(1)} copy-done((bf16[1280,512]{1,0:T(8,128)(2,1)S(1)}, bf16[1280,512]{1,0:T(8,128)(2,1)}, u32[]{:S(2)}) %copy-start.2) | copy-done | bytes 1310744
  21.2 1.0 pack.2
  22.3 0.0 copy-start.3
  22.3 1.0 copy-done.3
  23.3 14.6 %all-to-all-done.2 = bf16[64,16,512]{2,1,0:T(8,128)(2,1)} async-done(((bf16[64,16,512]{2,1,0:T(8,128)(2,1)}), bf16[64,16,512]{2,1,0:T(8,128)(2,1)}, u32[]{:S(2)}, u32[]{:S(2)}) %all-to-all-start.2) | async-done | bytes 1048608 | tf_op jit(solution)/shard_map/all_to_all | solution.py:272
  37.9 1.8 %collective-permute-start.3 = (bf16[1024,512]{1,0:T(8,128)(2,1)}, bf16[1024,512]{1,0:T(8,128)(2,1)S(1)}, u32[]{:S(2)}, u32[]{:S(2)}) collective-permute-start(bf16[1024,512]{1,0:T(8,128)(2,1)} %bitcast.7.own_ref), channel_id=1, source_target_pairs={{0,64},{64,0},{1,65},{65,1},{2,66},{66,2},{3,67},{67,3},{4,68},{68... | collective-permute-start | bytes 3145736 | tf_op jit(solution)/shard_map/ppermute | solution.py:278
  39.6 23.3 %all_to_all.20 = bf16[64,16,512]{2,1,0:T(8,128)(2,1)S(1)} all-to-all(bf16[64,16,512]{2,1,0:T(8,128)(2,1)} %bitcast.15), channel_id=1, replica_groups=mesh['rep'=2,'shard'=64] {'shard'}, dimensions={0} | all-to-all | bytes 2097152 | tf_op jit(solution)/shard_map/all_to_all | solution.py:272
  62.9 1.3 %collective-permute-start.1 = (bf16[1024,512]{1,0:T(8,128)(2,1)S(1)}, bf16[1024,512]{1,0:T(8,128)(2,1)S(1)}, u32[]{:S(2)}, u32[]{:S(2)}) collective-permute-start(bf16[1024,512]{1,0:T(8,128)(2,1)S(1)} %bitcast.12), channel_id=1, source_target_pairs={{0,64},{64,0},{1,65},{65,1},{2,66},{66,2},{3,67},{67,3},{4,68},{68... | collective-permute-start | bytes 3145736 | tf_op jit(solution)/shard_map/ppermute | solution.py:278
  64.2 0.0 collective-permute-done.3.oth_ref
  64.2 0.0 copy-start.7
  64.2 5.5 %roots.3 = (f32[1024,512]{1,0:T(8,128)S(1)}, f32[8,512]{1,0:T(8,128)S(1)}) custom-call(s32[1]{0:T(128)} %bitcast.rep_ref, bf16[1024,512]{1,0:T(8,128)(2,1)} %bitcast.7.own_ref, bf16[1024,512]{1,0:T(8,128)(2,1)S(1)} %collective-permute-done.3.oth_ref, bf16[2,1024,512]{2,1,0:T(8,128)(2,1)} %right_oth.3, bf16[2,1024,512]{2,1,0:T(8,128)(2,1)} %right_oth.3, ...), custom_call_target="tpu_custom_call" | custom-call | flops 2147483648 | bytes 7340032 | tf_op jit(solution)/shard_map/roots/pallas_call | solution.py:87
  69.7 0.0 copy-done.7
  69.7 0.1 collective-permute-start.4
  69.8 1.2 collective-permute-done.4.theirs_ref
  71.0 2.0 %graft.3 = bf16[1024,512]{1,0:T(8,128)(2,1)} custom-call(f32[1024,512]{1,0:T(8,128)S(1)} %get-tuple-element.13.pre_ref, f32[8,512]{1,0:T(8,128)S(1)} %get-tuple-element.14.mine_ref, f32[8,512]{1,0:T(8,128)S(1)} %collective-permute-done.4.theirs_ref), custom_call_target="tpu_custom_call" | custom-call | flops 1048576 | bytes 3145728 | tf_op jit(solution)/shard_map/graft/pallas_call | solution.py:128
  73.0 4.7 %all-to-all-start.3 = ((bf16[64,16,512]{2,1,0:T(8,128)(2,1)}), bf16[64,16,512]{2,1,0:T(8,128)(2,1)S(1)}, u32[]{:S(2)}, u32[]{:S(2)}) async-start(bf16[64,16,512]{2,1,0:T(8,128)(2,1)} %bitcast.8), calls=%async_computation.3 | async-start | bytes 2097152 | tf_op jit(solution)/shard_map/all_to_all | solution.py:272
  77.6 0.0 collective-permute-done.1.oth_ref
  77.6 0.0 copy-start.5
  77.7 5.3 %roots.2 = (f32[1024,512]{1,0:T(8,128)S(1)}, f32[8,512]{1,0:T(8,128)S(1)}) custom-call(s32[1]{0:T(128)} %bitcast.rep_ref, bf16[1024,512]{1,0:T(8,128)(2,1)S(1)} %bitcast.13, bf16[1024,512]{1,0:T(8,128)(2,1)S(1)} %collective-permute-done.1.oth_ref, bf16[2,1024,512]{2,1,0:T(8,128)(2,1)} %right_oth.3, bf16[2,1024,512]{2,1,0:T(8,128)(2,1)} %right_oth.3, ...), custom_call_target="tpu_custom_call" | custom-call | flops 2147483648 | bytes 7340032 | tf_op jit(solution)/shard_map/roots/pallas_call | solution.py:87
  83.0 0.0 copy-done.5
  83.0 0.4 collective-permute-start.2
  83.4 0.9 collective-permute-done.2.theirs_ref
  84.3 2.0 %graft.2 = bf16[1024,512]{1,0:T(8,128)(2,1)} custom-call(f32[1024,512]{1,0:T(8,128)S(1)} %get-tuple-element.11.pre_ref, f32[8,512]{1,0:T(8,128)S(1)} %get-tuple-element.12.mine_ref, f32[8,512]{1,0:T(8,128)S(1)} %collective-permute-done.2.theirs_ref), custom_call_target="tpu_custom_call" | custom-call | flops 1048576 | bytes 3145728 | tf_op jit(solution)/shard_map/graft/pallas_call | solution.py:128
  86.2 9.7 %all-to-all-done.3.blocks_ref = bf16[64,16,512]{2,1,0:T(8,128)(2,1)S(1)} async-done(((bf16[64,16,512]{2,1,0:T(8,128)(2,1)}), bf16[64,16,512]{2,1,0:T(8,128)(2,1)S(1)}, u32[]{:S(2)}, u32[]{:S(2)}) %all-to-all-start.3) | async-done | bytes 1048608 | tf_op jit(solution)/shard_map/all_to_all | solution.py:272
  95.9 4.9 %all-to-all-start.1 = ((bf16[64,16,512]{2,1,0:T(8,128)(2,1)}), bf16[64,16,512]{2,1,0:T(8,128)(2,1)S(1)}, u32[]{:S(2)}, u32[]{:S(2)}) async-start(bf16[64,16,512]{2,1,0:T(8,128)(2,1)} %bitcast.5), calls=%async_computation.1 | async-start | bytes 2097152 | tf_op jit(solution)/shard_map/all_to_all | solution.py:272
  100.8 0.0 copy-start.8
  100.9 1.2 %copy-done.8 = bf16[1024,512]{1,0:T(8,128)(2,1)S(1)} copy-done((bf16[1024,512]{1,0:T(8,128)(2,1)S(1)}, bf16[1024,512]{1,0:T(8,128)(2,1)}, u32[]{:S(2)}) %copy-start.8) | copy-done | bytes 1048600
  102.1 0.0 copy-start.6
  102.1 4.9 %grams.2 = (f32[2,512,1024]{2,1,0:T(8,128)}, f32[2,512,1024]{2,1,0:T(8,128)}) custom-call(s32[1]{0:T(128)} %bitcast.rep_ref, bf16[1024,512]{1,0:T(8,128)(2,1)} %bitcast.7.own_ref, bf16[1024,512]{1,0:T(8,128)(2,1)S(1)} %copy-done.8), custom_call_target="tpu_custom_call" | custom-call | flops 2147483648 | bytes 6291456 | tf_op jit(solution)/shard_map/grams/pallas_call | solution.py:175
  106.9 0.0 copy-done.6
  106.9 3.6 %grams.3 = (f32[2,512,1024]{2,1,0:T(8,128)}, f32[2,512,1024]{2,1,0:T(8,128)}) custom-call(s32[1]{0:T(128)} %bitcast.rep_ref, bf16[1024,512]{1,0:T(8,128)(2,1)S(1)} %bitcast.14, bf16[1024,512]{1,0:T(8,128)(2,1)S(1)} %copy-done.6, f32[2,512,1024]{2,1,0:T(8,128)} %get-tuple-element.15.rest_0_, ...), custom_call_target="tpu_custom_call", output_to_operand_aliasing={{0}: (3, {}), {1}: (4, {})} | custom-call | flops 2147483648 | bytes 6291456 | tf_op jit(solution)/shard_map/grams/pallas_call | solution.py:175
  110.5 2.0 %place.2.rest_0_ = bf16[1280,512]{1,0:T(8,128)(2,1)} custom-call(s32[128]{0:T(128)S(1)} %broadcast_add_fusion.place_ref, bf16[64,16,512]{2,1,0:T(8,128)(2,1)S(1)} %all-to-all-done.3.blocks_ref), custom_call_target="tpu_custom_call" | custom-call | bytes 2097152 | tf_op jit(solution)/shard_map/place/pallas_call | solution.py:230
  112.6 5.5 %all-to-all-done.1.blocks_ref = bf16[64,16,512]{2,1,0:T(8,128)(2,1)S(1)} async-done(((bf16[64,16,512]{2,1,0:T(8,128)(2,1)}), bf16[64,16,512]{2,1,0:T(8,128)(2,1)S(1)}, u32[]{:S(2)}, u32[]{:S(2)}) %all-to-all-start.1) | async-done | bytes 1048608 | tf_op jit(solution)/shard_map/all_to_all | solution.py:272
  118.0 2.1 %place.3 = bf16[1280,512]{1,0:T(8,128)(2,1)} custom-call(s32[128]{0:T(128)S(1)} %broadcast_add_fusion.place_ref, bf16[64,16,512]{2,1,0:T(8,128)(2,1)S(1)} %all-to-all-done.1.blocks_ref, bf16[1280,512]{1,0:T(8,128)(2,1)} %place.2.rest_0_), custom_call_target="tpu_custom_call", output_to_operand_aliasing={{}: (2, {})} | custom-call | bytes 2097152 | tf_op jit(solution)/shard_map/place/pallas_call | solution.py:230
  (2 shorter events, 0.0 us)
Async XLA Ops:
  0.6 5.8 %copy-start = (bf16[1,1280,1024]{2,1,0:T(8,128)(2,1)S(1)}, bf16[1,1280,1024]{2,1,0:T(8,128)(2,1)}, u32[]{:S(2)}) copy-start(bf16[1,1280,1024]{2,1,0:T(8,128)(2,1)} %param.5) | copy-start | bytes 7864324
  0.6 3.1 %copy-start.10 = (s32[80]{0:T(128)S(1)}, s32[80]{0:T(128)}, u32[]{:S(2)}) copy-start(s32[80]{0:T(128)} %param.6) | copy-start | bytes 964
  0.7 3.2 %copy-start.9 = (s32[80]{0:T(128)S(1)}, s32[80]{0:T(128)}, u32[]{:S(2)}) copy-start(s32[80]{0:T(128)} %param.7) | copy-start | bytes 964
  2.2 4.2 %collective-permute-start = (bf16[1280,512]{1,0:T(8,128)(2,1)S(1)}, bf16[1280,512]{1,0:T(8,128)(2,1)S(1)}, u32[]{:S(2)}, u32[]{:S(2)}) collective-permute-start(bf16[1280,512]{1,0:T(8,128)(2,1)S(1)} %dynamic-slice_bitcast_fusion), channel_id=1, source_target_pairs={{0,64},{64,0},{1,65},{65,1},{2,66},{66,2},{3,67},{67,3},{4,68},{68... | collective-permute-start | bytes 3932168 | tf_op jit(solution)/shard_map/ppermute | solution.py:258
  6.4 1.1 copy-start.1
  7.5 1.0 copy-start.4
  8.4 29.4 %all-to-all-start.2 = ((bf16[64,16,512]{2,1,0:T(8,128)(2,1)}), bf16[64,16,512]{2,1,0:T(8,128)(2,1)}, u32[]{:S(2)}, u32[]{:S(2)}) async-start(bf16[64,16,512]{2,1,0:T(8,128)(2,1)} %bitcast.16), calls=%async_computation.2 | async-start | bytes 2097152 | tf_op jit(solution)/shard_map/all_to_all | solution.py:272
  19.9 1.3 %copy-start.2 = (bf16[1280,512]{1,0:T(8,128)(2,1)S(1)}, bf16[1280,512]{1,0:T(8,128)(2,1)}, u32[]{:S(2)}) copy-start(bf16[1280,512]{1,0:T(8,128)(2,1)} %copy-done.1) | copy-start | bytes 3932164
  22.3 1.0 copy-start.3
  37.9 26.3 %collective-permute-start.3 = (bf16[1024,512]{1,0:T(8,128)(2,1)}, bf16[1024,512]{1,0:T(8,128)(2,1)S(1)}, u32[]{:S(2)}, u32[]{:S(2)}) collective-permute-start(bf16[1024,512]{1,0:T(8,128)(2,1)} %bitcast.7.own_ref), channel_id=1, source_target_pairs={{0,64},{64,0},{1,65},{65,1},{2,66},{66,2},{3,67},{67,3},{4,68},{68... | collective-permute-start | bytes 3145736 | tf_op jit(solution)/shard_map/ppermute | solution.py:278
  62.9 14.7 %collective-permute-start.1 = (bf16[1024,512]{1,0:T(8,128)(2,1)S(1)}, bf16[1024,512]{1,0:T(8,128)(2,1)S(1)}, u32[]{:S(2)}, u32[]{:S(2)}) collective-permute-start(bf16[1024,512]{1,0:T(8,128)(2,1)S(1)} %bitcast.12), channel_id=1, source_target_pairs={{0,64},{64,0},{1,65},{65,1},{2,66},{66,2},{3,67},{67,3},{4,68},{68... | collective-permute-start | bytes 3145736 | tf_op jit(solution)/shard_map/ppermute | solution.py:278
  64.2 5.6 %copy-start.7 = (bf16[1024,512]{1,0:T(8,128)(2,1)}, bf16[1024,512]{1,0:T(8,128)(2,1)S(1)}, u32[]{:S(2)}) copy-start(bf16[1024,512]{1,0:T(8,128)(2,1)S(1)} %collective-permute-done.3.oth_ref) | copy-start | bytes 3145732
  69.7 1.3 %collective-permute-start.4 = (f32[8,512]{1,0:T(8,128)S(1)}, f32[8,512]{1,0:T(8,128)S(1)}, u32[]{:S(2)}, u32[]{:S(2)}) collective-permute-start(f32[8,512]{1,0:T(8,128)S(1)} %get-tuple-element.14.mine_ref), channel_id=1, source_target_pairs={{0,64},{64,0},{1,65},{65,1},{2,66},{66,2},{3,67},{67,3},{4,68},{68... | collective-permute-start | bytes 49160 | tf_op jit(solution)/shard_map/ppermute | solution.py:282
  73.0 23.0 %all-to-all-start.3 = ((bf16[64,16,512]{2,1,0:T(8,128)(2,1)}), bf16[64,16,512]{2,1,0:T(8,128)(2,1)S(1)}, u32[]{:S(2)}, u32[]{:S(2)}) async-start(bf16[64,16,512]{2,1,0:T(8,128)(2,1)} %bitcast.8), calls=%async_computation.3 | async-start | bytes 2097152 | tf_op jit(solution)/shard_map/all_to_all | solution.py:272
  77.6 5.4 %copy-start.5 = (bf16[1024,512]{1,0:T(8,128)(2,1)}, bf16[1024,512]{1,0:T(8,128)(2,1)S(1)}, u32[]{:S(2)}) copy-start(bf16[1024,512]{1,0:T(8,128)(2,1)S(1)} %collective-permute-done.1.oth_ref) | copy-start | bytes 3145732
  83.0 1.3 %collective-permute-start.2 = (f32[8,512]{1,0:T(8,128)S(1)}, f32[8,512]{1,0:T(8,128)S(1)}, u32[]{:S(2)}, u32[]{:S(2)}) collective-permute-start(f32[8,512]{1,0:T(8,128)S(1)} %get-tuple-element.12.mine_ref), channel_id=1, source_target_pairs={{0,64},{64,0},{1,65},{65,1},{2,66},{66,2},{3,67},{67,3},{4,68},{68... | collective-permute-start | bytes 49160 | tf_op jit(solution)/shard_map/ppermute | solution.py:282
  95.9 22.1 %all-to-all-start.1 = ((bf16[64,16,512]{2,1,0:T(8,128)(2,1)}), bf16[64,16,512]{2,1,0:T(8,128)(2,1)S(1)}, u32[]{:S(2)}, u32[]{:S(2)}) async-start(bf16[64,16,512]{2,1,0:T(8,128)(2,1)} %bitcast.5), calls=%async_computation.1 | async-start | bytes 2097152 | tf_op jit(solution)/shard_map/all_to_all | solution.py:272
  100.8 1.2 %copy-start.8 = (bf16[1024,512]{1,0:T(8,128)(2,1)S(1)}, bf16[1024,512]{1,0:T(8,128)(2,1)}, u32[]{:S(2)}) copy-start(bf16[1024,512]{1,0:T(8,128)(2,1)} %copy-done.7) | copy-start | bytes 3145732
  102.1 4.9 %copy-start.6 = (bf16[1024,512]{1,0:T(8,128)(2,1)S(1)}, bf16[1024,512]{1,0:T(8,128)(2,1)}, u32[]{:S(2)}) copy-start(bf16[1024,512]{1,0:T(8,128)(2,1)} %copy-done.5) | copy-start | bytes 3145732

commit v2 on v0

v2 whole, which is shorter than its diff:
```python
import functools

import jax
import jax.numpy as jnp
from jax import lax
from jax.experimental import pallas as pl
from jax.experimental.pallas import tpu as pltpu
from jax.sharding import PartitionSpec as P

EPSILON = 1e-06
VMEM_BYTES = 48 * 1024 * 1024
NT = (((1,), (1,)), ((), ()))
TN = (((0,), (0,)), ((), ()))
SWAP = [(0, 1), (1, 0)]
BOTH = ("rep", "shard")


def cost(flops, nbytes):
    return pl.CostEstimate(flops=flops, bytes_accessed=nbytes, transcendentals=0)


def params():
    return pltpu.CompilerParams(vmem_limit_bytes=VMEM_BYTES)


def pack_kernel(place_ref, rep_ref, mine_ref, theirs_ref, out_ref):
    piece = out_ref.shape[1]
    base = pl.program_id(0) * out_ref.shape[0]

    def step(i, carry):
        where = place_ref[base + i]
        row = pl.multiple_of(jnp.maximum(where, 0) * piece, piece)
        total = mine_ref[pl.ds(row, piece), :].astype(jnp.float32) + theirs_ref[
            pl.ds(row, piece), :
        ].astype(jnp.float32)
        out_ref[i] = jnp.where(where >= 0, total, 0.0).astype(out_ref.dtype)
        return carry

    lax.fori_loop(0, out_ref.shape[0], step, 0, unroll=8)


def pack(pieces, piece, place, rep, mine, theirs):
    rows, strip = theirs.shape
    steps = 4
    return pl.pallas_call(
        pack_kernel,
        grid_spec=pltpu.PrefetchScalarGridSpec(
            num_scalar_prefetch=2,
            grid=(steps,),
            in_specs=[
                pl.BlockSpec((rows, strip), lambda i, place, rep: (0, rep[0])),
                pl.BlockSpec((rows, strip), lambda i, place, rep: (0, 0)),
            ],
            out_specs=pl.BlockSpec((pieces // steps, piece, strip), lambda i, place, rep: (i, 0, 0)),
        ),
        out_shape=jax.ShapeDtypeStruct((pieces, piece, strip), theirs.dtype),
        compiler_params=params(),
        cost_estimate=cost(rows * strip, 2 * (2 * rows + pieces * piece) * strip),
        name="pack",
    )(place, rep, mine, theirs)


def root_kernel(steps, rep_ref, grad_ref, right_own, right_oth, left_ref, out_ref, half, pre, sums):
    i = pl.program_id(0)
    rep = rep_ref[0]
    tile, strip = grad_ref.shape[1:]
    block = half.shape[1]

    @pl.when(i == 0)
    def _():
        sums[...] = jnp.zeros_like(sums)

    @pl.when(i < steps)
    def _():
        rows = pl.ds(pl.multiple_of(i * tile, tile), tile)
        first, second = grad_ref[0], grad_ref[1]
        for k, right in ((rep, right_own), (1 - rep, right_oth)):
            acc = jnp.dot(first, right[0, :strip, :], preferred_element_type=jnp.float32)
            acc += jnp.dot(second, right[0, strip:, :], preferred_element_type=jnp.float32)
            half[k, rows, :] = acc.astype(half.dtype)
        first, second = first.astype(jnp.float32), second.astype(jnp.float32)
        sums[0:1, :] += jnp.sum(first * first + second * second, axis=0, keepdims=True)

    @pl.when(i >= steps)
    def _():
        rows = pl.ds(pl.multiple_of((i - steps) * tile, tile), tile)
        for k in range(2):
            value = jnp.dot(left_ref[0], half[k], preferred_element_type=jnp.float32)
            pre[k, rows, :] = value
            sums[1:2, :] += jnp.sum(value * value, axis=0, keepdims=True)

    @pl.when(i == 2 * steps - 1)
    def _():
        entries = float(block * block)
        top = jnp.full((8, 128), jnp.sum(sums[0:1, :]), jnp.float32) / entries
        bottom = jnp.full((8, 128), jnp.sum(sums[1:2, :]), jnp.float32) / entries + EPSILON
        scale = jnp.sqrt(top / bottom)[0:1, 0:1]
        for k in range(2):
            out_ref[k] = (pre[k] * scale).astype(out_ref.dtype)


def apply_roots(rep, grad, left_root, right_root, right_other):
    strips, block, strip = grad.shape
    steps = 2
    tile = block // steps
    return pl.pallas_call(
        functools.partial(root_kernel, steps),
        grid_spec=pltpu.PrefetchScalarGridSpec(
            num_scalar_prefetch=1,
            grid=(2 * steps,),
            in_specs=[
                pl.BlockSpec((strips, tile, strip), lambda i, rep: (0, jnp.minimum(i, steps - 1), 0)),
                pl.BlockSpec((1, block, strip), lambda i, rep: (rep[0], 0, 0)),
                pl.BlockSpec((1, block, strip), lambda i, rep: (0, 0, 0)),
                pl.BlockSpec(
                    (1, tile, block), lambda i, rep: (rep[0], jnp.maximum(i - steps, 0), 0)
                ),
            ],
            out_specs=pl.BlockSpec(grad.shape, lambda i, rep: (0, 0, 0)),
            scratch_shapes=[
                pltpu.VMEM(grad.shape, jnp.bfloat16),
                pltpu.VMEM(grad.shape, jnp.float32),
                pltpu.VMEM((8, strip), jnp.float32),
            ],
        ),
        out_shape=jax.ShapeDtypeStruct(grad.shape, jnp.bfloat16),
        compiler_params=params(),
        cost_estimate=cost(4 * block**3, 8 * block * block),
        name="roots",
    )(rep, grad, right_root, right_other, left_root)


def gram_kernel(steps, rep_ref, own_ref, oth_ref, left_out, right_out):
    i = pl.program_id(0)
    rep = rep_ref[0]

    def form(grad_ref):
        strips, _, strip = grad_ref.shape
        tile = strip // steps
        begin = pl.multiple_of((i % steps) * tile, tile)
        rows = pl.ds(pl.multiple_of(rep * strip + begin, tile), tile)
        left = lax.dot_general(
            grad_ref[0, rows, :], grad_ref[0], NT, preferred_element_type=jnp.float32
        )
        for k in range(1, strips):
            left += lax.dot_general(
                grad_ref[k, rows, :], grad_ref[k], NT, preferred_element_type=jnp.float32
            )
        left_out[0] = left
        columns = grad_ref[rep, :, pl.ds(begin, tile)]
        for k in range(strips):
            right_out[0, :, k * strip : (k + 1) * strip] = lax.dot_general(
                columns, grad_ref[k], TN, preferred_element_type=jnp.float32
            )

    pl.when(i < steps)(lambda: form(own_ref))
    pl.when(i >= steps)(lambda: form(oth_ref))


def grams(rep, own, oth):
    slots, block, strip = own.shape
    steps = 2
    tile = strip // steps
    out = jax.ShapeDtypeStruct((slots, strip, block), jnp.float32)

    def where(i, rep):
        return (jnp.where(i < steps, rep[0], 1 - rep[0]), i % steps, 0)

    return pl.pallas_call(
        functools.partial(gram_kernel, steps),
        grid_spec=pltpu.PrefetchScalarGridSpec(
            num_scalar_prefetch=1,
            grid=(2 * steps,),
            in_specs=[pl.BlockSpec(own.shape, lambda i, rep: (0, 0, 0))] * 2,
            out_specs=[pl.BlockSpec((1, tile, block), where)] * 2,
        ),
        out_shape=[out, out],
        compiler_params=params(),
        cost_estimate=cost(8 * block * block * strip, 24 * block * strip),
        name="grams",
    )(rep, own, oth)


def place_kernel(source_ref, row_ref, pieces_ref, out_ref, sem):
    piece = pieces_ref.shape[1]

    def start(b, carry):
        row = pl.multiple_of(row_ref[b], piece)
        pltpu.make_async_copy(
            pieces_ref.at[source_ref[b]], out_ref.at[pl.ds(row, piece), :], sem
        ).start()
        return carry

    lax.fori_loop(0, row_ref.shape[0], start, 0, unroll=4)
    pltpu.make_async_copy(out_ref, out_ref, sem).wait()


def place_rows(rows, source, row, pieces):
    _, piece, strip = pieces.shape
    return pl.pallas_call(
        place_kernel,
        grid_spec=pltpu.PrefetchScalarGridSpec(
            num_scalar_prefetch=2,
            grid=(1,),
            in_specs=[pl.BlockSpec(memory_space=pl.ANY)],
            out_specs=pl.BlockSpec(memory_space=pl.ANY),
            scratch_shapes=[pltpu.SemaphoreType.DMA],
        ),
        out_shape=jax.ShapeDtypeStruct((rows, strip), pieces.dtype),
        compiler_params=params(),
        cost_estimate=cost(0, 4 * rows * strip),
        name="place",
    )(source, row, pieces)


def local(gradients, owner_table, offsets, left_root, right_root):
    shard_count = lax.axis_size("shard")
    slots, block = left_root.shape[:2]
    strip = right_root.shape[2]
    piece = block // shard_count
    rows = gradients.shape[1]
    block_ids = jnp.arange(offsets.shape[0], dtype=jnp.int32)
    me = lax.axis_index("rep").astype(jnp.int32)
    rep = me.reshape(1)

    mine = gradients[0]
    theirs = lax.ppermute(
        lax.dynamic_slice_in_dim(mine, (1 - me) * strip, strip, 1), "rep", SWAP
    )
    same_owner = owner_table[:, None] == owner_table[None, :]
    before = block_ids[:, None] < block_ids[None, :]
    rank = jnp.sum(jnp.where(same_owner & before, 1, 0), axis=0).astype(jnp.int32)
    holder_id = rank * shard_count + owner_table
    holder_ids = jnp.arange(slots * shard_count, dtype=jnp.int32)
    held = holder_id[:, None] == holder_ids[None, :]
    place = jnp.sum(jnp.where(held, (offsets // piece)[:, None] + 1, 0), axis=0) - 1
    place = place.astype(jnp.int32)

    def exchange(x):
        return lax.all_to_all(x, BOTH, split_axis=0, concat_axis=0, tiled=True)

    packed = pack(slots * shard_count, piece, place, rep, mine, theirs)
    packed, right_root = lax.optimization_barrier((packed, right_root))
    right_other = lax.ppermute(
        lax.dynamic_slice_in_dim(right_root, 1 - me, 1, 0), "rep", SWAP
    )
    grad = exchange(packed).reshape(slots, block, strip)
    update = apply_roots(rep, grad, left_root, right_root, right_other)
    update, grad = lax.optimization_barrier((update, grad))
    back = exchange(update.reshape(packed.shape))
    grad_other = lax.ppermute(grad, "rep", SWAP)
    gram_left, gram_right = grams(rep, grad, grad_other)
    holder_id, gram_left = lax.optimization_barrier((holder_id, gram_left))
    return place_rows(rows, holder_id, offsets, back), gram_left, gram_right


def solution(mesh):
    in_specs = (P("rep", "shard", None), P(), P(), P("shard", None, None), P("shard", None, "rep"))
    out_specs = (P("shard", "rep"), P("shard", "rep", None), P("shard", "rep", None))
    return jax.shard_map(local, mesh=mesh, in_specs=in_specs, out_specs=out_specs, check_vma=False)
```

time: 174 us -> 94.1 us (0.54)
  blocking collectives: 41.5 us -> 0 us
  local copies, waits for them, and re-layouts: 26.5 us -> 2.99 us
  matrix products: 21.9 us -> 0 us
  Pallas kernels: 0 us -> 21 us
  between operations: 14.2 us -> 0.74 us
  other arithmetic: 10.3 us -> 0.21 us
  starting transfers between devices: 10.6 us -> 19.8 us
    all_to_all x1 -> x0, blocking collectives: 39 us -> none  [local(): lax.all_to_all(picked.reshape(shard_count, slot_count, piece_rows, summed...]
    all_to_all x1 -> x2, waiting for transfers between devices: 16.9 us -> 44.4 us  [exchange(): return lax.all_to_all(x, BOTH, split_axis=0, concat_axis=0, tiled=True)]
    dot_general x3 -> x0, matrix products: 21.9 us -> none  [the longest x1 10.1 us: local(): jnp.einsum('mik,mkj->mij', left_root, half_sum.astype(jnp.bfloat16), pref...]
    pallas_call x0 -> x4, Pallas kernels: none -> 21 us  [the longest x1 8.87 us: grams(): pl.pallas_call(functools.partial(gram_kernel, steps), grid_spec=pltpu.Pre...]
    reduce_scatter x1 -> x0, waiting for transfers between devices: 18 us -> none  [local(): lax.psum_scatter(gradients[0].astype(jnp.float32).astype(jnp.bfloat16), '...]
    gather x2 -> x0, local copies, waits for them, and re-layouts: 16.7 us -> none  [the longest x1 10.7 us: local(): jnp.take(summed, pick_rows, axis=0)]
    all_gather x1 -> x0, waiting for transfers between devices: 12.5 us -> none  [local(): piece_cols = lax.all_gather(own_strips, 'rep', axis=2, tiled=True)]
    all_to_all x1 -> x2, starting transfers between devices: 10.6 us -> 16 us  [exchange(): return lax.all_to_all(x, BOTH, split_axis=0, concat_axis=0, tiled=True)]
  transfers between devices with their start and end apart: 3 -> 5, of which waited for: 3 -> 4; matrix products, arithmetic and copies ran while one was open for 9% -> 0% of each run, Pallas kernels for 0% -> 9%
where the time goes in v2:
time: 94.1 us; the launch traced here: 93.8 us
  waiting for transfers between devices  49.1 us (52%)
  Pallas kernels  21 us (22%)
  starting transfers between devices  19.8 us (21%)
  local copies, waits for them, and re-layouts  2.99 us (3%)
    all_to_all x2, waiting for transfers between devices, exchange(): return lax.all_to_all(x, BOTH, split_axis=0, concat_axis=0, tiled=True)  44.4 us
    all_to_all x2, starting transfers between devices, exchange(): return lax.all_to_all(x, BOTH, split_axis=0, concat_axis=0, tiled=True)  16 us
    pallas_call x1, Pallas kernels, grams(): pl.pallas_call(functools.partial(gram_kernel, steps), grid_spec=pltpu.Pre...  8.87 us
    pallas_call x1, Pallas kernels, apply_roots(): pl.pallas_call(functools.partial(root_kernel, steps), grid_spec=pltpu.Pre...  7.67 us
    pallas_call x1, Pallas kernels, pack(): pl.pallas_call(pack_kernel, grid_spec=pltpu.PrefetchScalarGridSpec(num_sc...  2.87 us
    ppermute x1, waiting for transfers between devices, local(): lax.ppermute(lax.dynamic_slice_in_dim(mine, (1 - me) * strip, strip, 1),...  2.43 us
    ppermute x1, waiting for transfers between devices, local(): lax.ppermute(lax.dynamic_slice_in_dim(right_root, 1 - me, 1, 0), 'rep', S...  2.29 us
  transfers between devices with their start and end apart: 5, of which 4 were waited for; matrix products, arithmetic and copies ran while one was open for 0% of the time, Pallas kernels for 9%

profile of v2, /device:TPU:1, one launch (start us, length us, event | category | flops | bytes accessed | tf_op | source)
XLA Modules:
  0.0 93.8 jit_solution(6970150099295116101)
XLA Ops:
  0.6 0.0 copy-start
  0.6 0.0 copy-start.4
  0.7 0.0 copy-start.2
  0.7 1.6 %dynamic-slice_bitcast_fusion = bf16[1280,512]{1,0:T(8,128)(2,1)S(1)} fusion(bf16[1,1280,1024]{2,1,0:T(8,128)(2,1)} %param.5, s32[]{:T(128)S(6)} %select_n.22), kind=kLoop, calls=%fused_computation | loop fusion | bytes 2621444 | tf_op jit(solution)/shard_map/dynamic_slice | solution.py:228
  2.2 1.5 %collective-permute-start = (bf16[1280,512]{1,0:T(8,128)(2,1)S(1)}, bf16[1280,512]{1,0:T(8,128)(2,1)S(1)}, u32[]{:S(2)}, u32[]{:S(2)}) collective-permute-start(bf16[1280,512]{1,0:T(8,128)(2,1)S(1)} %dynamic-slice_bitcast_fusion), channel_id=1, source_target_pairs={{0,64},{64,0},{1,65},{65,1},{2,66},{66,2},{3,67},{67,3},{4,68},{68... | collective-permute-start | bytes 3932168 | tf_op jit(solution)/shard_map/ppermute | solution.py:227
  3.7 0.0 copy-done.4
  3.7 0.1 select_reduce_fusion.1
  3.8 0.0 copy-done.2
  3.8 0.1 select_reduce_fusion
  4.0 2.4 %collective-permute-done.theirs_ref = bf16[1280,512]{1,0:T(8,128)(2,1)S(1)} collective-permute-done((bf16[1280,512]{1,0:T(8,128)(2,1)S(1)}, bf16[1280,512]{1,0:T(8,128)(2,1)S(1)}, u32[]{:S(2)}, u32[]{:S(2)}) %collective-permute-start) | collective-permute-done | bytes 1310752 | tf_op jit(solution)/shard_map/ppermute | solution.py:227
  6.4 0.0 copy-done
  6.4 2.9 %pack.1 = bf16[128,16,512]{2,1,0:T(8,128)(2,1)} custom-call(s32[128]{0:T(128)S(1)} %broadcast_add_fusion.place_ref, s32[1]{0:T(128)} %bitcast.rep_ref, bf16[1280,1024]{1,0:T(8,128)(2,1)S(1)} %bitcast.6, bf16[1280,512]{1,0:T(8,128)(2,1)S(1)} %collective-permute-done.theirs_ref), custom_call_target="tpu_custom_call" | custom-call | flops 655360 | bytes 4718592 | tf_op jit(solution)/shard_map/pack/pallas_call | solution.py:45
  9.3 0.0 copy-start.3
  9.3 10.9 %all-to-all-start = ((bf16[128,16,512]{2,1,0:T(8,128)(2,1)}), bf16[128,16,512]{2,1,0:T(8,128)(2,1)}, u32[]{:S(2)}, u32[]{:S(2)}) async-start(bf16[128,16,512]{2,1,0:T(8,128)(2,1)} %pack.1), calls=%async_computation | async-start | bytes 4194304 | tf_op jit(solution)/shard_map/all_to_all | solution.py:240
  20.2 0.0 copy-done.3
  20.2 0.1 constant_dynamic-slice_fusion
  20.3 1.2 %collective-permute-start.1 = (bf16[1,1024,512]{2,1,0:T(8,128)(2,1)S(1)}, bf16[1,1024,512]{2,1,0:T(8,128)(2,1)S(1)}, u32[]{:S(2)}, u32[]{:S(2)}) collective-permute-start(bf16[1,1024,512]{2,1,0:T(8,128)(2,1)S(1)} %constant_dynamic-slice_fusion), channel_id=1, source_target_pairs={{0,64},{64,0},{1,65},{65,1},{2,66},{66,2},{3,67},{67,3},{4,68},{68... | collective-permute-start | bytes 3145736 | tf_op jit(solution)/shard_map/ppermute | solution.py:244
  21.5 2.3 %collective-permute-done.1.right_oth = bf16[1,1024,512]{2,1,0:T(8,128)(2,1)S(1)} collective-permute-done((bf16[1,1024,512]{2,1,0:T(8,128)(2,1)S(1)}, bf16[1,1024,512]{2,1,0:T(8,128)(2,1)S(1)}, u32[]{:S(2)}, u32[]{:S(2)}) %collective-permute-start.1) | collective-permute-done | bytes 1048608 | tf_op jit(solution)/shard_map/ppermute | solution.py:244
  23.8 24.6 %all-to-all-done = bf16[128,16,512]{2,1,0:T(8,128)(2,1)} async-done(((bf16[128,16,512]{2,1,0:T(8,128)(2,1)}), bf16[128,16,512]{2,1,0:T(8,128)(2,1)}, u32[]{:S(2)}, u32[]{:S(2)}) %all-to-all-start) | async-done | bytes 2097184 | tf_op jit(solution)/shard_map/all_to_all | solution.py:240
  48.4 7.7 %roots.1 = bf16[2,1024,512]{2,1,0:T(8,128)(2,1)S(1)} custom-call(s32[1]{0:T(128)} %bitcast.rep_ref, bf16[2,1024,512]{2,1,0:T(8,128)(2,1)} %bitcast.3.grad_ref.own_ref, bf16[2,1024,512]{2,1,0:T(8,128)(2,1)} %right_own, bf16[1,1024,512]{2,1,0:T(8,128)(2,1)S(1)} %collective-permute-done.1.right_oth, bf16[2,1024,1024]{2,1,0:T(8,128)(2,1)} %left_ref.1), custom_call_target="tpu_custom_call" | custom-call | flops 4294967296 | bytes 8388608 | tf_op jit(solution)/shard_map/roots/pallas_call | solution.py:106
  56.1 0.0 copy-start.1
  56.1 1.3 %copy-done.1 = bf16[2,1024,512]{2,1,0:T(8,128)(2,1)} copy-done((bf16[2,1024,512]{2,1,0:T(8,128)(2,1)}, bf16[2,1024,512]{2,1,0:T(8,128)(2,1)S(1)}, u32[]{:S(2)}) %copy-start.1) | copy-done | bytes 2097176
  57.5 1.1 %collective-permute-start.2 = (bf16[2,1024,512]{2,1,0:T(8,128)(2,1)}, bf16[2,1024,512]{2,1,0:T(8,128)(2,1)}, u32[]{:S(2)}, u32[]{:S(2)}) collective-permute-start(bf16[2,1024,512]{2,1,0:T(8,128)(2,1)} %bitcast.3.grad_ref.own_ref), channel_id=1, source_target_pairs={{0,64},{64,0},{1,65},{65,1},{2,66},{66,2},{3,67},{67,3},{4,68},{68... | collective-permute-start | bytes 6291464 | tf_op jit(solution)/shard_map/ppermute | solution.py:251
  58.6 5.0 %all-to-all-start.1 = ((bf16[128,16,512]{2,1,0:T(8,128)(2,1)}), bf16[128,16,512]{2,1,0:T(8,128)(2,1)S(1)}, u32[]{:S(2)}, u32[]{:S(2)}) async-start(bf16[128,16,512]{2,1,0:T(8,128)(2,1)} %bitcast.7), calls=%async_computation.1 | async-start | bytes 4194304 | tf_op jit(solution)/shard_map/all_to_all | solution.py:240
  63.6 0.0 collective-permute-done.2.oth_ref
  63.6 8.9 %grams.1 = (f32[2,512,1024]{2,1,0:T(8,128)}, f32[2,512,1024]{2,1,0:T(8,128)}) custom-call(s32[1]{0:T(128)} %bitcast.rep_ref, bf16[2,1024,512]{2,1,0:T(8,128)(2,1)} %bitcast.3.grad_ref.own_ref, bf16[2,1024,512]{2,1,0:T(8,128)(2,1)} %collective-permute-done.2.oth_ref), custom_call_target="tpu_custom_call" | custom-call | flops 4294967296 | bytes 12582912 | tf_op jit(solution)/shard_map/grams/pallas_call | solution.py:169
  72.5 19.7 %all-to-all-done.1.pieces_ref = bf16[128,16,512]{2,1,0:T(8,128)(2,1)S(1)} async-done(((bf16[128,16,512]{2,1,0:T(8,128)(2,1)}), bf16[128,16,512]{2,1,0:T(8,128)(2,1)S(1)}, u32[]{:S(2)}, u32[]{:S(2)}) %all-to-all-start.1) | async-done | bytes 2097184 | tf_op jit(solution)/shard_map/all_to_all | solution.py:240
  92.2 1.6 %place.1 = bf16[1280,512]{1,0:T(8,128)(2,1)} custom-call(s32[80]{0:T(128)S(1)} %get-tuple-element.15.source_ref, s32[80]{0:T(128)S(1)} %copy-done.2, bf16[128,16,512]{2,1,0:T(8,128)(2,1)S(1)} %all-to-all-done.1.pieces_ref), custom_call_target="tpu_custom_call" | custom-call | bytes 2621440 | tf_op jit(solution)/shard_map/place/pallas_call | solution.py:200
  (2 shorter events, 0.0 us)
Async XLA Ops:
  0.6 5.8 %copy-start = (bf16[1,1280,1024]{2,1,0:T(8,128)(2,1)S(1)}, bf16[1,1280,1024]{2,1,0:T(8,128)(2,1)}, u32[]{:S(2)}) copy-start(bf16[1,1280,1024]{2,1,0:T(8,128)(2,1)} %param.5) | copy-start | bytes 7864324
  0.6 3.1 %copy-start.4 = (s32[80]{0:T(128)S(1)}, s32[80]{0:T(128)}, u32[]{:S(2)}) copy-start(s32[80]{0:T(128)} %param.6) | copy-start | bytes 964
  0.7 3.2 %copy-start.2 = (s32[80]{0:T(128)S(1)}, s32[80]{0:T(128)}, u32[]{:S(2)}) copy-start(s32[80]{0:T(128)} %row_ref.1) | copy-start | bytes 964
  2.2 4.2 %collective-permute-start = (bf16[1280,512]{1,0:T(8,128)(2,1)S(1)}, bf16[1280,512]{1,0:T(8,128)(2,1)S(1)}, u32[]{:S(2)}, u32[]{:S(2)}) collective-permute-start(bf16[1280,512]{1,0:T(8,128)(2,1)S(1)} %dynamic-slice_bitcast_fusion), channel_id=1, source_target_pairs={{0,64},{64,0},{1,65},{65,1},{2,66},{66,2},{3,67},{67,3},{4,68},{68... | collective-permute-start | bytes 3932168 | tf_op jit(solution)/shard_map/ppermute | solution.py:227
  9.3 10.9 %copy-start.3 = (bf16[2,1024,512]{2,1,0:T(8,128)(2,1)S(1)}, bf16[2,1024,512]{2,1,0:T(8,128)(2,1)}, u32[]{:S(2)}) copy-start(bf16[2,1024,512]{2,1,0:T(8,128)(2,1)} %right_own) | copy-start | bytes 6291460
  9.3 39.2 %all-to-all-start = ((bf16[128,16,512]{2,1,0:T(8,128)(2,1)}), bf16[128,16,512]{2,1,0:T(8,128)(2,1)}, u32[]{:S(2)}, u32[]{:S(2)}) async-start(bf16[128,16,512]{2,1,0:T(8,128)(2,1)} %pack.1), calls=%async_computation | async-start | bytes 4194304 | tf_op jit(solution)/shard_map/all_to_all | solution.py:240
  20.3 3.5 %collective-permute-start.1 = (bf16[1,1024,512]{2,1,0:T(8,128)(2,1)S(1)}, bf16[1,1024,512]{2,1,0:T(8,128)(2,1)S(1)}, u32[]{:S(2)}, u32[]{:S(2)}) collective-permute-start(bf16[1,1024,512]{2,1,0:T(8,128)(2,1)S(1)} %constant_dynamic-slice_fusion), channel_id=1, source_target_pairs={{0,64},{64,0},{1,65},{65,1},{2,66},{66,2},{3,67},{67,3},{4,68},{68... | collective-permute-start | bytes 3145736 | tf_op jit(solution)/shard_map/ppermute | solution.py:244
  56.1 1.3 %copy-start.1 = (bf16[2,1024,512]{2,1,0:T(8,128)(2,1)}, bf16[2,1024,512]{2,1,0:T(8,128)(2,1)S(1)}, u32[]{:S(2)}) copy-start(bf16[2,1024,512]{2,1,0:T(8,128)(2,1)S(1)} %roots.1) | copy-start | bytes 6291460
  57.5 6.2 %collective-permute-start.2 = (bf16[2,1024,512]{2,1,0:T(8,128)(2,1)}, bf16[2,1024,512]{2,1,0:T(8,128)(2,1)}, u32[]{:S(2)}, u32[]{:S(2)}) collective-permute-start(bf16[2,1024,512]{2,1,0:T(8,128)(2,1)} %bitcast.3.grad_ref.own_ref), channel_id=1, source_target_pairs={{0,64},{64,0},{1,65},{65,1},{2,66},{66,2},{3,67},{67,3},{4,68},{68... | collective-permute-start | bytes 6291464 | tf_op jit(solution)/shard_map/ppermute | solution.py:251
  58.6 33.7 %all-to-all-start.1 = ((bf16[128,16,512]{2,1,0:T(8,128)(2,1)}), bf16[128,16,512]{2,1,0:T(8,128)(2,1)S(1)}, u32[]{:S(2)}, u32[]{:S(2)}) async-start(bf16[128,16,512]{2,1,0:T(8,128)(2,1)} %bitcast.7), calls=%async_computation.1 | async-start | bytes 4194304 | tf_op jit(solution)/shard_map/all_to_all | solution.py:240

commit v3 on v2

v3 whole, which is shorter than its diff:
```python
import functools

import jax
import jax.numpy as jnp
from jax import lax
from jax.experimental import pallas as pl
from jax.experimental.pallas import tpu as pltpu
from jax.sharding import PartitionSpec as P

EPSILON = 1e-06
VMEM_BYTES = 24 * 1024 * 1024
NT = (((1,), (1,)), ((), ()))
TN = (((0,), (0,)), ((), ()))
SWAP = [(0, 1), (1, 0)]
BOTH = ("rep", "shard")


def cost(flops, nbytes):
    return pl.CostEstimate(flops=flops, bytes_accessed=nbytes, transcendentals=0)


def params():
    return pltpu.CompilerParams(vmem_limit_bytes=VMEM_BYTES)


def in_vmem(x):
    return pltpu.with_memory_space_constraint(x, pltpu.VMEM)


def in_hbm(x):
    return pltpu.with_memory_space_constraint(x, pltpu.HBM)


def strip_kernel(steps, which_ref, rows_ref, strip_ref, sems):
    rows, strip = strip_ref.shape
    columns = pl.ds(pl.multiple_of(which_ref[0] * strip, strip), strip)
    moves = []
    for k in range(steps):
        here = pl.ds(k * (rows // steps), rows // steps)
        move = pltpu.make_async_copy(rows_ref.at[here, columns], strip_ref.at[here], sems.at[k])
        move.start()
        moves.append(move)
    for move in moves:
        move.wait()


def take_strip(strip, which, gradients):
    rows = gradients.shape[0]
    steps = 4
    return pl.pallas_call(
        functools.partial(strip_kernel, steps),
        grid_spec=pltpu.PrefetchScalarGridSpec(
            num_scalar_prefetch=1,
            grid=(1,),
            in_specs=[pl.BlockSpec(memory_space=pltpu.HBM)],
            out_specs=pl.BlockSpec(memory_space=pltpu.VMEM),
            scratch_shapes=[pltpu.SemaphoreType.DMA((steps,))],
        ),
        out_shape=pltpu.VMEM((rows, strip), gradients.dtype),
        compiler_params=params(),
        cost_estimate=cost(0, 4 * rows * strip),
        name="strip",
    )(which, in_hbm(gradients))


def fetch_kernel(which_ref, left_ref, left_out, sems):
    moves = []
    for k in range(4):
        rows = pl.ds(k * (left_out.shape[0] // 4), left_out.shape[0] // 4)
        move = pltpu.make_async_copy(
            left_ref.at[which_ref[0], rows], left_out.at[rows], sems.at[k]
        )
        move.start()
        moves.append(move)
    for move in moves:
        move.wait()


def fetch_root(which, left_root):
    return pl.pallas_call(
        fetch_kernel,
        grid_spec=pltpu.PrefetchScalarGridSpec(
            num_scalar_prefetch=1,
            grid=(1,),
            in_specs=[pl.BlockSpec(memory_space=pltpu.HBM)],
            out_specs=pl.BlockSpec(memory_space=pltpu.VMEM),
            scratch_shapes=[pltpu.SemaphoreType.DMA((4,))],
        ),
        out_shape=pltpu.VMEM(left_root.shape[1:], left_root.dtype),
        compiler_params=params(),
        cost_estimate=cost(0, 4 * left_root[0].size),
        name="fetch",
    )(which, in_hbm(left_root))


def pack_kernel(steps, place_ref, mine_ref, theirs_ref, out_ref, total, sems):
    pieces, piece, _ = total.shape
    chunk = pieces // steps
    moves = []
    for k in range(steps):

        def step(i, carry, k=k):
            where = place_ref[k * chunk + i]
            rows = pl.ds(pl.multiple_of(jnp.maximum(where, 0) * piece, piece), piece)
            both = mine_ref[rows, :] + theirs_ref[rows, :]
            total[k * chunk + i] = jnp.where(where >= 0, both, jnp.zeros_like(both))
            return carry

        lax.fori_loop(0, chunk, step, 0, unroll=8)
        here = pl.ds(k * chunk, chunk)
        move = pltpu.make_async_copy(total.at[here], out_ref.at[here], sems.at[k])
        move.start()
        moves.append(move)
    for move in moves:
        move.wait()


def pack(pieces, piece, place, mine, theirs):
    rows, strip = theirs.shape
    steps = 8
    return pl.pallas_call(
        functools.partial(pack_kernel, steps),
        grid_spec=pltpu.PrefetchScalarGridSpec(
            num_scalar_prefetch=1,
            grid=(1,),
            in_specs=[pl.BlockSpec(memory_space=pltpu.VMEM)] * 2,
            out_specs=pl.BlockSpec(memory_space=pltpu.HBM),
            scratch_shapes=[
                pltpu.VMEM((pieces, piece, strip), theirs.dtype),
                pltpu.SemaphoreType.DMA((steps,)),
            ],
        ),
        out_shape=pltpu.HBM((pieces, piece, strip), theirs.dtype),
        compiler_params=params(),
        cost_estimate=cost(rows * strip, 2 * pieces * piece * strip),
        name="pack",
    )(place, in_vmem(mine), in_vmem(theirs))


def root_kernel(
    tiles,
    steps,
    rep_ref,
    grad_ref,
    right_ref,
    right_oth,
    left_ref,
    out_ref,
    kept_ref,
    grad,
    right_own,
    half,
    pre,
    ready,
    sems,
    own_sem,
    kept_sem,
):
    rep = rep_ref[0]
    strips, block, strip = grad.shape
    arrivals = []
    for i in range(tiles):
        rows = pl.ds(i * (block // tiles), block // tiles)
        for k in range(strips):
            move = pltpu.make_async_copy(
                grad_ref.at[k, rows], grad.at[k, rows], sems.at[len(arrivals)]
            )
            move.start()
            arrivals.append(move)
        if i == 0:
            own = pltpu.make_async_copy(right_ref.at[rep], right_own, own_sem)
            own.start()
    grad_sq = jnp.zeros((1, strip), jnp.float32)
    for i in range(tiles):
        rows = pl.ds(i * (block // tiles), block // tiles)
        for k in range(strips):
            arrivals[strips * i + k].wait()
        wide = jnp.concatenate([grad[k, rows, :] for k in range(strips)], axis=1)
        for k, right in ((1, right_oth.at[0]), (0, right_own)):
            if i == 0 and k == 0:
                own.wait()
            acc = jnp.dot(wide, right[...], preferred_element_type=jnp.float32)
            half[k, rows, :] = acc.astype(half.dtype)
        for k in range(strips):
            value = grad[k, rows, :].astype(jnp.float32)
            grad_sq += jnp.sum(value * value, axis=0, keepdims=True)
    keep = pltpu.make_async_copy(grad, kept_ref, kept_sem)
    keep.start()
    pre_sq = jnp.zeros((1, strip), jnp.float32)
    for k in range(strips):
        value = jnp.dot(left_ref[...], half[k], preferred_element_type=jnp.float32)
        pre[k] = value
        pre_sq += jnp.sum(value * value, axis=0, keepdims=True)
    entries = float(block * block)
    top = jnp.full((8, 128), jnp.sum(grad_sq), jnp.float32) / entries
    bottom = jnp.full((8, 128), jnp.sum(pre_sq), jnp.float32) / entries + EPSILON
    scale = jnp.sqrt(top / bottom)[0:1, 0:1]
    moves = [keep]
    for k, c in ((0, rep), (1, 1 - rep)):
        for j in range(steps):
            rows = pl.ds(j * (block // steps), block // steps)
            ready[k, rows, :] = (pre[k, rows, :] * scale).astype(ready.dtype)
            move = pltpu.make_async_copy(
                ready.at[k, rows], out_ref.at[c, rows], sems.at[strips * tiles + len(moves) - 1]
            )
            move.start()
            moves.append(move)
    for move in moves:
        move.wait()


def apply_roots(rep, grad, left, right_root, right_oth):
    strips, block, strip = grad.shape
    tiles = 2
    steps = 4
    out = pltpu.HBM(grad.shape, jnp.bfloat16)
    return pl.pallas_call(
        functools.partial(root_kernel, tiles, steps),
        grid_spec=pltpu.PrefetchScalarGridSpec(
            num_scalar_prefetch=1,
            grid=(1,),
            in_specs=[
                pl.BlockSpec(memory_space=pl.ANY),
                pl.BlockSpec(memory_space=pltpu.HBM),
                pl.BlockSpec(memory_space=pltpu.VMEM),
                pl.BlockSpec(memory_space=pltpu.VMEM),
            ],
            out_specs=[pl.BlockSpec(memory_space=pltpu.HBM)] * 2,
            scratch_shapes=[
                pltpu.VMEM(grad.shape, jnp.bfloat16),
                pltpu.VMEM((block, strip), jnp.bfloat16),
                pltpu.VMEM(grad.shape, jnp.bfloat16),
                pltpu.VMEM(grad.shape, jnp.float32),
                pltpu.VMEM(grad.shape, jnp.bfloat16),
                pltpu.SemaphoreType.DMA((strips * (steps + tiles),)),
                pltpu.SemaphoreType.DMA,
                pltpu.SemaphoreType.DMA,
            ],
        ),
        out_shape=[out, out],
        compiler_params=params(),
        cost_estimate=cost(4 * block**3, 4 * block * block),
        name="roots",
    )(rep, grad, in_hbm(right_root), in_vmem(right_oth), in_vmem(left))


def gram_kernel(steps, rep_ref, own_ref, oth_ref, left_out, right_out):
    i = pl.program_id(0)
    rep = rep_ref[0]

    def form(grad_ref):
        strips, _, strip = grad_ref.shape
        tile = strip // steps
        begin = pl.multiple_of((i % steps) * tile, tile)
        rows = pl.ds(pl.multiple_of(rep * strip + begin, tile), tile)
        left = lax.dot_general(
            grad_ref[0, rows, :], grad_ref[0], NT, preferred_element_type=jnp.float32
        )
        for k in range(1, strips):
            left += lax.dot_general(
                grad_ref[k, rows, :], grad_ref[k], NT, preferred_element_type=jnp.float32
            )
        left_out[0] = left
        columns = grad_ref[rep, :, pl.ds(begin, tile)]
        for k in range(strips):
            right_out[0, :, k * strip : (k + 1) * strip] = lax.dot_general(
                columns, grad_ref[k], TN, preferred_element_type=jnp.float32
            )

    pl.when(i < steps)(lambda: form(own_ref))
    pl.when(i >= steps)(lambda: form(oth_ref))


def grams(rep, own, oth):
    slots, block, strip = own.shape
    steps = 2
    tile = strip // steps
    out = jax.ShapeDtypeStruct((slots, strip, block), jnp.float32)

    def where(i, rep):
        return (jnp.where(i < steps, rep[0], 1 - rep[0]), i % steps, 0)

    return pl.pallas_call(
        functools.partial(gram_kernel, steps),
        grid_spec=pltpu.PrefetchScalarGridSpec(
            num_scalar_prefetch=1,
            grid=(2 * steps,),
            in_specs=[pl.BlockSpec(own.shape, lambda i, rep: (0, 0, 0))] * 2,
            out_specs=[pl.BlockSpec((1, tile, block), where)] * 2,
        ),
        out_shape=[out, out],
        compiler_params=params(),
        cost_estimate=cost(8 * block * block * strip, 24 * block * strip),
        name="grams",
    )(rep, own, oth)


def place_kernel(source_ref, row_ref, pieces_ref, out_ref, sem):
    piece = pieces_ref.shape[1]

    def start(b, carry):
        row = pl.multiple_of(row_ref[b], piece)
        pltpu.make_async_copy(
            pieces_ref.at[source_ref[b]], out_ref.at[pl.ds(row, piece), :], sem
        ).start()
        return carry

    lax.fori_loop(0, row_ref.shape[0], start, 0, unroll=4)
    pltpu.make_async_copy(out_ref, out_ref, sem).wait()


def place_rows(rows, source, row, pieces):
    _, piece, strip = pieces.shape
    return pl.pallas_call(
        place_kernel,
        grid_spec=pltpu.PrefetchScalarGridSpec(
            num_scalar_prefetch=2,
            grid=(1,),
            in_specs=[pl.BlockSpec(memory_space=pl.ANY)],
            out_specs=pl.BlockSpec(memory_space=pl.ANY),
            scratch_shapes=[pltpu.SemaphoreType.DMA],
        ),
        out_shape=jax.ShapeDtypeStruct((rows, strip), pieces.dtype),
        compiler_params=params(),
        cost_estimate=cost(0, 4 * rows * strip),
        name="place",
    )(source, row, pieces)


def local(gradients, owner_table, offsets, left_root, right_root):
    shard_count = lax.axis_size("shard")
    slots, block = left_root.shape[:2]
    strip = right_root.shape[2]
    piece = block // shard_count
    rows = gradients.shape[1]
    block_ids = jnp.arange(offsets.shape[0], dtype=jnp.int32)
    me = lax.axis_index("rep").astype(jnp.int32)
    rep = me.reshape(1)

    send = take_strip(strip, 1 - rep, gradients[0])
    theirs = lax.ppermute(send, "rep", SWAP)
    send, whole = lax.optimization_barrier((send, gradients[0]))
    mine = take_strip(strip, rep, whole)
    same_owner = owner_table[:, None] == owner_table[None, :]
    before = block_ids[:, None] < block_ids[None, :]
    rank = jnp.sum(jnp.where(same_owner & before, 1, 0), axis=0).astype(jnp.int32)
    holder_id = rank * shard_count + owner_table
    holder_ids = jnp.arange(slots * shard_count, dtype=jnp.int32)
    held = holder_id[:, None] == holder_ids[None, :]
    place = jnp.sum(jnp.where(held, (offsets // piece)[:, None] + 1, 0), axis=0) - 1
    place = place.astype(jnp.int32)

    def exchange(x):
        return lax.all_to_all(x, BOTH, split_axis=0, concat_axis=0, tiled=True)

    packed = pack(slots * shard_count, piece, place, mine, theirs)
    packed, left_root, right_root = lax.optimization_barrier((packed, left_root, right_root))
    right_oth = lax.ppermute(
        lax.dynamic_slice_in_dim(right_root, 1 - me, 1, 0), "rep", SWAP
    )
    left = fetch_root(rep, left_root)
    grad = exchange(packed).reshape(slots, block, strip)
    update, grad = apply_roots(rep, grad, left, right_root, right_oth)
    update, grad = lax.optimization_barrier((update, grad))
    back = exchange(update.reshape(packed.shape))
    grad_other = lax.ppermute(grad, "rep", SWAP)
    gram_left, gram_right = grams(rep, grad, grad_other)
    holder_id, gram_left = lax.optimization_barrier((holder_id, gram_left))
    return place_rows(rows, holder_id, offsets, back), gram_left, gram_right


def solution(mesh):
    in_specs = (P("rep", "shard", None), P(), P(), P("shard", None, None), P("shard", None, "rep"))
    out_specs = (P("shard", "rep"), P("shard", "rep", None), P("shard", "rep", None))
    return jax.shard_map(local, mesh=mesh, in_specs=in_specs, out_specs=out_specs, check_vma=False)
```

time: 94.1 us -> 92.1 us (0.979)
  waiting for transfers between devices: 49.1 us -> 45.3 us
  Pallas kernels: 21 us -> 23.8 us
  local copies, waits for them, and re-layouts: 2.99 us -> 1.68 us
    pallas_call x2 -> x5, Pallas kernels: 10.5 us -> 14.1 us  [the longest x1 7.94 us: apply_roots(): pl.pallas_call(functools.partial(root_kernel, tiles, steps), grid_spec=pl...]
    dynamic_slice x1 -> x0, local copies, waits for them, and re-layouts: 1.56 us -> none  [local(): lax.dynamic_slice_in_dim(mine, (1 - me) * strip, strip, 1)]
    ppermute x1, waiting for transfers between devices: 2.29 us -> 0.73 us  [local(): lax.ppermute(lax.dynamic_slice_in_dim(right_root, 1 - me, 1, 0), 'rep', S...]
    ppermute x1, waiting for transfers between devices: 2.43 us -> 1.11 us  [local(): theirs = lax.ppermute(send, 'rep', SWAP)]
  transfers between devices with their start and end apart: 5 -> 5, of which waited for: 4 -> 4; matrix products, arithmetic and copies ran while one was open for 0% -> 0% of each run, Pallas kernels for 9% -> 12%
where the time goes in v3:
time: 92.1 us; the launch traced here: 91.7 us
  waiting for transfers between devices  45.3 us (49%)
  Pallas kernels  23.8 us (26%)
  starting transfers between devices  19.9 us (22%)
  local copies, waits for them, and re-layouts  1.68 us (2%)
    all_to_all x2, waiting for transfers between devices, exchange(): return lax.all_to_all(x, BOTH, split_axis=0, concat_axis=0, tiled=True)  43.5 us
    all_to_all x2, starting transfers between devices, exchange(): return lax.all_to_all(x, BOTH, split_axis=0, concat_axis=0, tiled=True)  16 us
    pallas_call x1, Pallas kernels, grams(): pl.pallas_call(functools.partial(gram_kernel, steps), grid_spec=pltpu.Pre...  8.17 us
    pallas_call x1, Pallas kernels, apply_roots(): pl.pallas_call(functools.partial(root_kernel, tiles, steps), grid_spec=pl...  7.94 us
    pallas_call x2, Pallas kernels, take_strip(): pl.pallas_call(functools.partial(strip_kernel, steps), grid_spec=pltpu.Pr...  2.61 us
    pallas_call x1, Pallas kernels, pack(): pl.pallas_call(functools.partial(pack_kernel, steps), grid_spec=pltpu.Pre...  1.98 us
  transfers between devices with their start and end apart: 5, of which 4 were waited for; matrix products, arithmetic and copies ran while one was open for 0% of the time, Pallas kernels for 12%

profile of v3, /device:TPU:1, one launch (start us, length us, event | category | flops | bytes accessed | tf_op | source)
XLA Modules:
  0.0 91.7 jit_solution(2095690015374528947)
XLA Ops:
  0.6 1.3 %strip.2 = bf16[1280,512]{1,0:T(8,128)(2,1)S(1)} custom-call(s32[1]{0:T(128)S(6)} %sub.18.which_ref, bf16[1280,1024]{1,0:T(8,128)(2,1)} %bitcast.4), custom_call_target="tpu_custom_call" | custom-call | bytes 2621440 | tf_op jit(solution)/shard_map/strip/pallas_call | solution.py:50
  1.9 0.0 copy-start.3
  2.0 0.0 copy-start
  2.0 1.5 %collective-permute-start = (bf16[1280,512]{1,0:T(8,128)(2,1)S(1)}, bf16[1280,512]{1,0:T(8,128)(2,1)S(1)}, u32[]{:S(2)}, u32[]{:S(2)}) collective-permute-start(bf16[1280,512]{1,0:T(8,128)(2,1)S(1)} %strip.2), channel_id=1, source_target_pairs={{0,64},{64,0},{1,65},{65,1},{2,66},{66,2},{3,67},{67,3},{4,68},{68... | collective-permute-start | bytes 3932168 | tf_op jit(solution)/shard_map/ppermute | solution.py:341
  3.5 1.3 %strip.3.mine_ref = bf16[1280,512]{1,0:T(8,128)(2,1)S(1)} custom-call(s32[1]{0:T(128)} %bitcast.which_ref.rep_ref, bf16[1280,1024]{1,0:T(8,128)(2,1)} %bitcast.5), custom_call_target="tpu_custom_call" | custom-call | bytes 2621440 | tf_op jit(solution)/shard_map/strip/pallas_call | solution.py:50
  4.8 0.0 copy-done.3
  4.8 0.1 select_reduce_fusion.1
  4.9 0.0 copy-done
  4.9 0.1 select_reduce_fusion
  5.0 1.1 %collective-permute-done.theirs_ref = bf16[1280,512]{1,0:T(8,128)(2,1)S(1)} collective-permute-done((bf16[1280,512]{1,0:T(8,128)(2,1)S(1)}, bf16[1280,512]{1,0:T(8,128)(2,1)S(1)}, u32[]{:S(2)}, u32[]{:S(2)}) %collective-permute-start) | collective-permute-done | bytes 1310752 | tf_op jit(solution)/shard_map/ppermute | solution.py:341
  6.1 2.0 %pack.1 = bf16[128,16,512]{2,1,0:T(8,128)(2,1)} custom-call(s32[128]{0:T(128)S(1)} %broadcast_add_fusion.place_ref, bf16[1280,512]{1,0:T(8,128)(2,1)S(1)} %strip.3.mine_ref, bf16[1280,512]{1,0:T(8,128)(2,1)S(1)} %collective-permute-done.theirs_ref), custom_call_target="tpu_custom_call" | custom-call | flops 655360 | bytes 2097152 | tf_op jit(solution)/shard_map/pack/pallas_call | solution.py:121
  8.1 0.0 copy-start.2
  8.1 10.9 %all-to-all-start = ((bf16[128,16,512]{2,1,0:T(8,128)(2,1)}), bf16[128,16,512]{2,1,0:T(8,128)(2,1)}, u32[]{:S(2)}, u32[]{:S(2)}) async-start(bf16[128,16,512]{2,1,0:T(8,128)(2,1)} %pack.1), calls=%async_computation | async-start | bytes 4194304 | tf_op jit(solution)/shard_map/all_to_all | solution.py:354
  19.1 0.0 copy-done.2
  19.1 0.1 constant_dynamic-slice_fusion
  19.2 1.2 %collective-permute-start.1 = (bf16[1,1024,512]{2,1,0:T(8,128)(2,1)S(1)}, bf16[1,1024,512]{2,1,0:T(8,128)(2,1)S(1)}, u32[]{:S(2)}, u32[]{:S(2)}) collective-permute-start(bf16[1,1024,512]{2,1,0:T(8,128)(2,1)S(1)} %constant_dynamic-slice_fusion), channel_id=1, source_target_pairs={{0,64},{64,0},{1,65},{65,1},{2,66},{66,2},{3,67},{67,3},{4,68},{68... | collective-permute-start | bytes 3145736 | tf_op jit(solution)/shard_map/ppermute | solution.py:358
  20.4 1.5 %fetch.1.left_ref = bf16[1024,1024]{1,0:T(8,128)(2,1)S(1)} custom-call(s32[1]{0:T(128)} %bitcast.which_ref.rep_ref, bf16[2,1024,1024]{2,1,0:T(8,128)(2,1)} %left_ref), custom_call_target="tpu_custom_call" | custom-call | bytes 4194304 | tf_op jit(solution)/shard_map/fetch/pallas_call | solution.py:80
  21.9 0.7 collective-permute-done.1.right_oth
  22.7 24.6 %all-to-all-done = bf16[128,16,512]{2,1,0:T(8,128)(2,1)} async-done(((bf16[128,16,512]{2,1,0:T(8,128)(2,1)}), bf16[128,16,512]{2,1,0:T(8,128)(2,1)}, u32[]{:S(2)}, u32[]{:S(2)}) %all-to-all-start) | async-done | bytes 2097184 | tf_op jit(solution)/shard_map/all_to_all | solution.py:354
  47.3 7.9 %roots.1 = (bf16[2,1024,512]{2,1,0:T(8,128)(2,1)}, bf16[2,1024,512]{2,1,0:T(8,128)(2,1)}) custom-call(s32[1]{0:T(128)} %bitcast.which_ref.rep_ref, bf16[2,1024,512]{2,1,0:T(8,128)(2,1)} %bitcast.2.grad_ref, bf16[2,1024,512]{2,1,0:T(8,128)(2,1)} %right_ref, bf16[1,1024,512]{2,1,0:T(8,128)(2,1)S(1)} %collective-permute-done.1.right_oth, ...), custom_call_target="tpu_custom_call" | custom-call | flops 4294967296 | bytes 4194304 | tf_op jit(solution)/shard_map/roots/pallas_call | solution.py:217
  55.3 1.2 %collective-permute-start.2 = (bf16[2,1024,512]{2,1,0:T(8,128)(2,1)}, bf16[2,1024,512]{2,1,0:T(8,128)(2,1)}, u32[]{:S(2)}, u32[]{:S(2)}) collective-permute-start(bf16[2,1024,512]{2,1,0:T(8,128)(2,1)} %get-tuple-element.17.own_ref), channel_id=1, source_target_pairs={{0,64},{64,0},{1,65},{65,1},{2,66},{66,2},{3,67},{67,3},{4,68},{68... | collective-permute-start | bytes 6291464 | tf_op jit(solution)/shard_map/ppermute | solution.py:366
  56.5 5.0 %all-to-all-start.1 = ((bf16[128,16,512]{2,1,0:T(8,128)(2,1)}), bf16[128,16,512]{2,1,0:T(8,128)(2,1)S(1)}, u32[]{:S(2)}, u32[]{:S(2)}) async-start(bf16[128,16,512]{2,1,0:T(8,128)(2,1)} %bitcast.6), calls=%async_computation.1 | async-start | bytes 4194304 | tf_op jit(solution)/shard_map/all_to_all | solution.py:354
  61.5 0.0 collective-permute-done.2.oth_ref
  61.5 0.0 copy-start.1
  61.6 1.6 %copy-done.1 = bf16[2,1024,512]{2,1,0:T(8,128)(2,1)S(1)} copy-done((bf16[2,1024,512]{2,1,0:T(8,128)(2,1)S(1)}, bf16[2,1024,512]{2,1,0:T(8,128)(2,1)}, u32[]{:S(2)}) %copy-start.1) | copy-done | bytes 2097176
  63.1 8.2 %grams.1 = (f32[2,512,1024]{2,1,0:T(8,128)}, f32[2,512,1024]{2,1,0:T(8,128)}) custom-call(s32[1]{0:T(128)} %bitcast.which_ref.rep_ref, bf16[2,1024,512]{2,1,0:T(8,128)(2,1)S(1)} %copy-done.1, bf16[2,1024,512]{2,1,0:T(8,128)(2,1)} %collective-permute-done.2.oth_ref), custom_call_target="tpu_custom_call" | custom-call | flops 4294967296 | bytes 12582912 | tf_op jit(solution)/shard_map/grams/pallas_call | solution.py:283
  71.3 18.8 %all-to-all-done.1.pieces_ref = bf16[128,16,512]{2,1,0:T(8,128)(2,1)S(1)} async-done(((bf16[128,16,512]{2,1,0:T(8,128)(2,1)}), bf16[128,16,512]{2,1,0:T(8,128)(2,1)S(1)}, u32[]{:S(2)}, u32[]{:S(2)}) %all-to-all-start.1) | async-done | bytes 2097184 | tf_op jit(solution)/shard_map/all_to_all | solution.py:354
  90.1 1.6 %place.1 = bf16[1280,512]{1,0:T(8,128)(2,1)} custom-call(s32[80]{0:T(128)S(1)} %get-tuple-element.19.source_ref, s32[80]{0:T(128)S(1)} %copy-done, bf16[128,16,512]{2,1,0:T(8,128)(2,1)S(1)} %all-to-all-done.1.pieces_ref), custom_call_target="tpu_custom_call" | custom-call | bytes 2621440 | tf_op jit(solution)/shard_map/place/pallas_call | solution.py:314
  (2 shorter events, 0.0 us)
Async XLA Ops:
  1.9 2.8 %copy-start.3 = (s32[80]{0:T(128)S(1)}, s32[80]{0:T(128)}, u32[]{:S(2)}) copy-start(s32[80]{0:T(128)} %param.6) | copy-start | bytes 964
  2.0 2.9 %copy-start = (s32[80]{0:T(128)S(1)}, s32[80]{0:T(128)}, u32[]{:S(2)}) copy-start(s32[80]{0:T(128)} %row_ref.1) | copy-start | bytes 964
  2.0 4.2 %collective-permute-start = (bf16[1280,512]{1,0:T(8,128)(2,1)S(1)}, bf16[1280,512]{1,0:T(8,128)(2,1)S(1)}, u32[]{:S(2)}, u32[]{:S(2)}) collective-permute-start(bf16[1280,512]{1,0:T(8,128)(2,1)S(1)} %strip.2), channel_id=1, source_target_pairs={{0,64},{64,0},{1,65},{65,1},{2,66},{66,2},{3,67},{67,3},{4,68},{68... | collective-permute-start | bytes 3932168 | tf_op jit(solution)/shard_map/ppermute | solution.py:341
  8.1 10.9 %copy-start.2 = (bf16[2,1024,512]{2,1,0:T(8,128)(2,1)S(1)}, bf16[2,1024,512]{2,1,0:T(8,128)(2,1)}, u32[]{:S(2)}) copy-start(bf16[2,1024,512]{2,1,0:T(8,128)(2,1)} %right_ref) | copy-start | bytes 6291460
  8.1 39.2 %all-to-all-start = ((bf16[128,16,512]{2,1,0:T(8,128)(2,1)}), bf16[128,16,512]{2,1,0:T(8,128)(2,1)}, u32[]{:S(2)}, u32[]{:S(2)}) async-start(bf16[128,16,512]{2,1,0:T(8,128)(2,1)} %pack.1), calls=%async_computation | async-start | bytes 4194304 | tf_op jit(solution)/shard_map/all_to_all | solution.py:354
  19.2 3.5 %collective-permute-start.1 = (bf16[1,1024,512]{2,1,0:T(8,128)(2,1)S(1)}, bf16[1,1024,512]{2,1,0:T(8,128)(2,1)S(1)}, u32[]{:S(2)}, u32[]{:S(2)}) collective-permute-start(bf16[1,1024,512]{2,1,0:T(8,128)(2,1)S(1)} %constant_dynamic-slice_fusion), channel_id=1, source_target_pairs={{0,64},{64,0},{1,65},{65,1},{2,66},{66,2},{3,67},{67,3},{4,68},{68... | collective-permute-start | bytes 3145736 | tf_op jit(solution)/shard_map/ppermute | solution.py:358
  55.3 6.3 %collective-permute-start.2 = (bf16[2,1024,512]{2,1,0:T(8,128)(2,1)}, bf16[2,1024,512]{2,1,0:T(8,128)(2,1)}, u32[]{:S(2)}, u32[]{:S(2)}) collective-permute-start(bf16[2,1024,512]{2,1,0:T(8,128)(2,1)} %get-tuple-element.17.own_ref), channel_id=1, source_target_pairs={{0,64},{64,0},{1,65},{65,1},{2,66},{66,2},{3,67},{67,3},{4,68},{68... | collective-permute-start | bytes 6291464 | tf_op jit(solution)/shard_map/ppermute | solution.py:366
  56.5 33.7 %all-to-all-start.1 = ((bf16[128,16,512]{2,1,0:T(8,128)(2,1)}), bf16[128,16,512]{2,1,0:T(8,128)(2,1)S(1)}, u32[]{:S(2)}, u32[]{:S(2)}) async-start(bf16[128,16,512]{2,1,0:T(8,128)(2,1)} %bitcast.6), calls=%async_computation.1 | async-start | bytes 4194304 | tf_op jit(solution)/shard_map/all_to_all | solution.py:354
  61.5 1.6 %copy-start.1 = (bf16[2,1024,512]{2,1,0:T(8,128)(2,1)S(1)}, bf16[2,1024,512]{2,1,0:T(8,128)(2,1)}, u32[]{:S(2)}) copy-start(bf16[2,1024,512]{2,1,0:T(8,128)(2,1)} %get-tuple-element.17.own_ref) | copy-start | bytes 6291460

commit v4 on v3

--- a/solution.py
+++ b/solution.py
@@ -63,34 +63,29 @@
     )(which, in_hbm(gradients))
 
 
-def fetch_kernel(which_ref, left_ref, left_out, sems):
+def fetch_kernel(right_ref, right_out, sems):
     moves = []
-    for k in range(4):
-        rows = pl.ds(k * (left_out.shape[0] // 4), left_out.shape[0] // 4)
-        move = pltpu.make_async_copy(
-            left_ref.at[which_ref[0], rows], left_out.at[rows], sems.at[k]
-        )
+    for k in range(sems.shape[0]):
+        count = right_out.shape[0] // sems.shape[0]
+        rows = pl.ds(k * count, count)
+        move = pltpu.make_async_copy(right_ref.at[0, rows], right_out.at[rows], sems.at[k])
         move.start()
         moves.append(move)
     for move in moves:
         move.wait()
 
 
-def fetch_root(which, left_root):
+def fetch(right):
     return pl.pallas_call(
         fetch_kernel,
-        grid_spec=pltpu.PrefetchScalarGridSpec(
-            num_scalar_prefetch=1,
-            grid=(1,),
-            in_specs=[pl.BlockSpec(memory_space=pltpu.HBM)],
-            out_specs=pl.BlockSpec(memory_space=pltpu.VMEM),
-            scratch_shapes=[pltpu.SemaphoreType.DMA((4,))],
-        ),
-        out_shape=pltpu.VMEM(left_root.shape[1:], left_root.dtype),
-        compiler_params=params(),
-        cost_estimate=cost(0, 4 * left_root[0].size),
+        in_specs=[pl.BlockSpec(memory_space=pltpu.HBM)],
+        out_specs=pl.BlockSpec(memory_space=pltpu.VMEM),
+        scratch_shapes=[pltpu.SemaphoreType.DMA((2,))],
+        out_shape=pltpu.VMEM(right.shape[1:], right.dtype),
+        compiler_params=params(),
+        cost_estimate=cost(0, 4 * right.size),
         name="fetch",
-    )(which, in_hbm(left_root))
+    )(in_hbm(right))
 
 
 def pack_kernel(steps, place_ref, mine_ref, theirs_ref, out_ref, total, sems):
@@ -138,7 +133,6 @@
 
 
 def root_kernel(
-    tiles,
     steps,
     rep_ref,
     grad_ref,
@@ -147,48 +141,37 @@
     left_ref,
     out_ref,
     kept_ref,
-    grad,
     right_own,
+    left,
     half,
     pre,
     ready,
     sems,
-    own_sem,
+    in_sems,
     kept_sem,
 ):
     rep = rep_ref[0]
-    strips, block, strip = grad.shape
-    arrivals = []
-    for i in range(tiles):
-        rows = pl.ds(i * (block // tiles), block // tiles)
-        for k in range(strips):
-            move = pltpu.make_async_copy(
-                grad_ref.at[k, rows], grad.at[k, rows], sems.at[len(arrivals)]
-            )
-            move.start()
-            arrivals.append(move)
-        if i == 0:
-            own = pltpu.make_async_copy(right_ref.at[rep], right_own, own_sem)
-            own.start()
+    strips, block, strip = half.shape
+    fetch_right = pltpu.make_async_copy(right_ref.at[rep], right_own, in_sems.at[0])
+    fetch_left = pltpu.make_async_copy(left_ref.at[rep], left, in_sems.at[1])
+    keep = pltpu.make_async_copy(grad_ref, kept_ref, kept_sem)
+    fetch_right.start()
+    fetch_left.start()
+    for k, right in ((1, right_oth), (0, right_own)):
+        if k == 0:
+            fetch_right.wait()
+        wide = jnp.concatenate([grad_ref[j] for j in range(strips)], axis=1)
+        acc = jnp.dot(wide, right[...], preferred_element_type=jnp.float32)
+        half[k] = acc.astype(half.dtype)
     grad_sq = jnp.zeros((1, strip), jnp.float32)
-    for i in range(tiles):
-        rows = pl.ds(i * (block // tiles), block // tiles)
-        for k in range(strips):
-            arrivals[strips * i + k].wait()
-        wide = jnp.concatenate([grad[k, rows, :] for k in range(strips)], axis=1)
-        for k, right in ((1, right_oth.at[0]), (0, right_own)):
-            if i == 0 and k == 0:
-                own.wait()
-            acc = jnp.dot(wide, right[...], preferred_element_type=jnp.float32)
-            half[k, rows, :] = acc.astype(half.dtype)
-        for k in range(strips):
-            value = grad[k, rows, :].astype(jnp.float32)
-            grad_sq += jnp.sum(value * value, axis=0, keepdims=True)
-    keep = pltpu.make_async_copy(grad, kept_ref, kept_sem)
+    for k in range(strips):
+        value = grad_ref[k].astype(jnp.float32)
+        grad_sq += jnp.sum(value * value, axis=0, keepdims=True)
+    fetch_left.wait()
     keep.start()
     pre_sq = jnp.zeros((1, strip), jnp.float32)
     for k in range(strips):
-        value = jnp.dot(left_ref[...], half[k], preferred_element_type=jnp.float32)
+        value = jnp.dot(left[...], half[k], preferred_element_type=jnp.float32)
         pre[k] = value
         pre_sq += jnp.sum(value * value, axis=0, keepdims=True)
     entries = float(block * block)
@@ -201,7 +184,7 @@
             rows = pl.ds(j * (block // steps), block // steps)
             ready[k, rows, :] = (pre[k, rows, :] * scale).astype(ready.dtype)
             move = pltpu.make_async_copy(
-                ready.at[k, rows], out_ref.at[c, rows], sems.at[strips * tiles + len(moves) - 1]
+                ready.at[k, rows], out_ref.at[c, rows], sems.at[steps * k + j]
             )
             move.start()
             moves.append(move)
@@ -209,39 +192,38 @@
         move.wait()
 
 
-def apply_roots(rep, grad, left, right_root, right_oth):
+def apply_roots(rep, grad, left_root, right_root, right_oth):
     strips, block, strip = grad.shape
-    tiles = 2
     steps = 4
     out = pltpu.HBM(grad.shape, jnp.bfloat16)
     return pl.pallas_call(
-        functools.partial(root_kernel, tiles, steps),
+        functools.partial(root_kernel, steps),
         grid_spec=pltpu.PrefetchScalarGridSpec(
             num_scalar_prefetch=1,
             grid=(1,),
             in_specs=[
-                pl.BlockSpec(memory_space=pl.ANY),
+                pl.BlockSpec(memory_space=pltpu.VMEM),
                 pl.BlockSpec(memory_space=pltpu.HBM),
                 pl.BlockSpec(memory_space=pltpu.VMEM),
-                pl.BlockSpec(memory_space=pltpu.VMEM),
+                pl.BlockSpec(memory_space=pltpu.HBM),
             ],
             out_specs=[pl.BlockSpec(memory_space=pltpu.HBM)] * 2,
             scratch_shapes=[
-                pltpu.VMEM(grad.shape, jnp.bfloat16),
                 pltpu.VMEM((block, strip), jnp.bfloat16),
+                pltpu.VMEM((block, block), jnp.bfloat16),
                 pltpu.VMEM(grad.shape, jnp.bfloat16),
                 pltpu.VMEM(grad.shape, jnp.float32),
                 pltpu.VMEM(grad.shape, jnp.bfloat16),
-                pltpu.SemaphoreType.DMA((strips * (steps + tiles),)),
-                pltpu.SemaphoreType.DMA,
+                pltpu.SemaphoreType.DMA((strips * steps,)),
+                pltpu.SemaphoreType.DMA((2,)),
                 pltpu.SemaphoreType.DMA,
             ],
         ),
         out_shape=[out, out],
         compiler_params=params(),
-        cost_estimate=cost(4 * block**3, 4 * block * block),
+        cost_estimate=cost(4 * block**3, 8 * block * block),
         name="roots",
-    )(rep, grad, in_hbm(right_root), in_vmem(right_oth), in_vmem(left))
+    )(rep, in_vmem(grad), in_hbm(right_root), in_vmem(right_oth), in_hbm(left_root))
 
 
 def gram_kernel(steps, rep_ref, own_ref, oth_ref, left_out, right_out):
@@ -354,13 +336,13 @@
         return lax.all_to_all(x, BOTH, split_axis=0, concat_axis=0, tiled=True)
 
     packed = pack(slots * shard_count, piece, place, mine, theirs)
-    packed, left_root, right_root = lax.optimization_barrier((packed, left_root, right_root))
+    packed, right_later = lax.optimization_barrier((packed, right_root))
     right_oth = lax.ppermute(
-        lax.dynamic_slice_in_dim(right_root, 1 - me, 1, 0), "rep", SWAP
+        lax.dynamic_slice_in_dim(right_later, 1 - me, 1, 0), "rep", SWAP
     )
-    left = fetch_root(rep, left_root)
+    right_oth = fetch(right_oth)
     grad = exchange(packed).reshape(slots, block, strip)
-    update, grad = apply_roots(rep, grad, left, right_root, right_oth)
+    update, grad = apply_roots(rep, grad, left_root, right_root, right_oth)
     update, grad = lax.optimization_barrier((update, grad))
     back = exchange(update.reshape(packed.shape))
     grad_other = lax.ppermute(grad, "rep", SWAP)

time: 92.1 us -> 90.8 us (0.986)
  local copies, waits for them, and re-layouts: 1.68 us -> 3.87 us
  Pallas kernels: 23.8 us -> 22.2 us
  waiting for transfers between devices: 45.3 us -> 43.9 us
    all_to_all x2, waiting for transfers between devices: 43.5 us -> 40.5 us  [exchange(): return lax.all_to_all(x, BOTH, split_axis=0, concat_axis=0, tiled=True)]
    pallas_call x2, Pallas kernels: 9.49 us -> 7.88 us  [the longest x1 6.67 us: apply_roots(): pl.pallas_call(functools.partial(root_kernel, steps), grid_spec=pltpu.Pre...]
    ppermute x1, waiting for transfers between devices: 0.73 us -> 2.29 us  [local(): lax.ppermute(lax.dynamic_slice_in_dim(right_later, 1 - me, 1, 0), 'rep',...]
    dynamic_slice x1, local copies, waits for them, and re-layouts: 0.07 us -> 1.3 us  [local(): lax.dynamic_slice_in_dim(right_later, 1 - me, 1, 0)]
    unnamed x8, local copies, waits for them, and re-layouts: 1.61 us -> 2.57 us
  transfers between devices with their start and end apart: 5 -> 5, of which waited for: 4 -> 4; matrix products, arithmetic and copies ran while one was open for 0% -> 2% of each run, Pallas kernels for 12% -> 12%
where the time goes in v4:
time: 90.8 us; the launch traced here: 90.3 us
  waiting for transfers between devices  43.9 us (48%)
  Pallas kernels  22.2 us (24%)
  starting transfers between devices  19.4 us (21%)
  local copies, waits for them, and re-layouts  3.87 us (4%)
    all_to_all x2, waiting for transfers between devices, exchange(): return lax.all_to_all(x, BOTH, split_axis=0, concat_axis=0, tiled=True)  40.5 us
    all_to_all x2, starting transfers between devices, exchange(): return lax.all_to_all(x, BOTH, split_axis=0, concat_axis=0, tiled=True)  15.5 us
    pallas_call x1, Pallas kernels, grams(): pl.pallas_call(functools.partial(gram_kernel, steps), grid_spec=pltpu.Pre...  8.17 us
    pallas_call x1, Pallas kernels, apply_roots(): pl.pallas_call(functools.partial(root_kernel, steps), grid_spec=pltpu.Pre...  6.67 us
    pallas_call x2, Pallas kernels, take_strip(): pl.pallas_call(functools.partial(strip_kernel, steps), grid_spec=pltpu.Pr...  2.61 us
    unnamed x8, local copies, waits for them, and re-layouts  2.57 us
    ppermute x1, waiting for transfers between devices, local(): lax.ppermute(lax.dynamic_slice_in_dim(right_later, 1 - me, 1, 0), 'rep',...  2.29 us
    pallas_call x1, Pallas kernels, pack(): pl.pallas_call(functools.partial(pack_kernel, steps), grid_spec=pltpu.Pre...  1.98 us
  transfers between devices with their start and end apart: 5, of which 4 were waited for; matrix products, arithmetic and copies ran while one was open for 2% of the time, Pallas kernels for 12%

profile of v4, /device:TPU:1, one launch (start us, length us, event | category | flops | bytes accessed | tf_op | source)
XLA Modules:
  0.0 90.3 jit_solution(18278498680747905354)
XLA Ops:
  0.6 1.3 %strip.2 = bf16[1280,512]{1,0:T(8,128)(2,1)S(1)} custom-call(s32[1]{0:T(128)S(6)} %sub.18.which_ref, bf16[1280,1024]{1,0:T(8,128)(2,1)} %bitcast.5), custom_call_target="tpu_custom_call" | custom-call | bytes 2621440 | tf_op jit(solution)/shard_map/strip/pallas_call | solution.py:50
  1.9 0.0 copy-start.3
  2.0 0.0 copy-start
  2.0 1.5 %collective-permute-start = (bf16[1280,512]{1,0:T(8,128)(2,1)S(1)}, bf16[1280,512]{1,0:T(8,128)(2,1)S(1)}, u32[]{:S(2)}, u32[]{:S(2)}) collective-permute-start(bf16[1280,512]{1,0:T(8,128)(2,1)S(1)} %strip.2), channel_id=1, source_target_pairs={{0,64},{64,0},{1,65},{65,1},{2,66},{66,2},{3,67},{67,3},{4,68},{68... | collective-permute-start | bytes 3932168 | tf_op jit(solution)/shard_map/ppermute | solution.py:323
  3.5 1.3 %strip.3.mine_ref = bf16[1280,512]{1,0:T(8,128)(2,1)S(1)} custom-call(s32[1]{0:T(128)} %bitcast.which_ref.rep_ref, bf16[1280,1024]{1,0:T(8,128)(2,1)} %bitcast.6), custom_call_target="tpu_custom_call" | custom-call | bytes 2621440 | tf_op jit(solution)/shard_map/strip/pallas_call | solution.py:50
  4.8 0.0 copy-done.3
  4.8 0.1 select_reduce_fusion.1
  4.9 0.0 copy-done
  4.9 0.1 select_reduce_fusion
  5.0 1.1 %collective-permute-done.theirs_ref = bf16[1280,512]{1,0:T(8,128)(2,1)S(1)} collective-permute-done((bf16[1280,512]{1,0:T(8,128)(2,1)S(1)}, bf16[1280,512]{1,0:T(8,128)(2,1)S(1)}, u32[]{:S(2)}, u32[]{:S(2)}) %collective-permute-start) | collective-permute-done | bytes 1310752 | tf_op jit(solution)/shard_map/ppermute | solution.py:323
  6.1 2.0 %pack.1 = bf16[128,16,512]{2,1,0:T(8,128)(2,1)} custom-call(s32[128]{0:T(128)S(1)} %broadcast_add_fusion.place_ref, bf16[1280,512]{1,0:T(8,128)(2,1)S(1)} %strip.3.mine_ref, bf16[1280,512]{1,0:T(8,128)(2,1)S(1)} %collective-permute-done.theirs_ref), custom_call_target="tpu_custom_call" | custom-call | flops 655360 | bytes 2097152 | tf_op jit(solution)/shard_map/pack/pallas_call | solution.py:116
  8.1 10.5 %all-to-all-start = ((bf16[128,16,512]{2,1,0:T(8,128)(2,1)}), bf16[128,16,512]{2,1,0:T(8,128)(2,1)S(1)}, u32[]{:S(2)}, u32[]{:S(2)}) async-start(bf16[128,16,512]{2,1,0:T(8,128)(2,1)} %pack.1), calls=%async_computation | async-start | bytes 4194304 | tf_op jit(solution)/shard_map/all_to_all | solution.py:336
  18.6 1.3 %constant_dynamic-slice_fusion = bf16[1,1024,512]{2,1,0:T(8,128)(2,1)S(1)} fusion(bf16[2,1024,512]{2,1,0:T(8,128)(2,1)} %right_ref.1, s32[]{:T(128)S(6)} %select_n.19), kind=kLoop, calls=%fused_computation.12 | loop fusion | bytes 2097156 | tf_op jit(solution)/shard_map/dynamic_slice | solution.py:341
  19.9 1.1 %collective-permute-start.1 = (bf16[1,1024,512]{2,1,0:T(8,128)(2,1)S(1)}, bf16[1,1024,512]{2,1,0:T(8,128)(2,1)S(1)}, u32[]{:S(2)}, u32[]{:S(2)}) collective-permute-start(bf16[1,1024,512]{2,1,0:T(8,128)(2,1)S(1)} %constant_dynamic-slice_fusion), channel_id=1, source_target_pairs={{0,64},{64,0},{1,65},{65,1},{2,66},{66,2},{3,67},{67,3},{4,68},{68... | collective-permute-start | bytes 3145736 | tf_op jit(solution)/shard_map/ppermute | solution.py:340
  21.0 2.3 %collective-permute-done.1.right_ref = bf16[1,1024,512]{2,1,0:T(8,128)(2,1)S(1)} collective-permute-done((bf16[1,1024,512]{2,1,0:T(8,128)(2,1)S(1)}, bf16[1,1024,512]{2,1,0:T(8,128)(2,1)S(1)}, u32[]{:S(2)}, u32[]{:S(2)}) %collective-permute-start.1) | collective-permute-done | bytes 1048608 | tf_op jit(solution)/shard_map/ppermute | solution.py:340
  23.3 0.0 copy-start.2
  23.3 1.0 %copy-done.2 = bf16[1,1024,512]{2,1,0:T(8,128)(2,1)} copy-done((bf16[1,1024,512]{2,1,0:T(8,128)(2,1)}, bf16[1,1024,512]{2,1,0:T(8,128)(2,1)S(1)}, u32[]{:S(2)}) %copy-start.2) | copy-done | bytes 1048600
  24.3 1.2 %fetch.1.right_oth = bf16[1024,512]{1,0:T(8,128)(2,1)S(1)} custom-call(bf16[1,1024,512]{2,1,0:T(8,128)(2,1)} %copy-done.2), custom_call_target="tpu_custom_call" | custom-call | bytes 2097152 | tf_op jit(solution)/shard_map/fetch/pallas_call | solution.py:79
  25.5 21.7 %all-to-all-done = bf16[128,16,512]{2,1,0:T(8,128)(2,1)S(1)} async-done(((bf16[128,16,512]{2,1,0:T(8,128)(2,1)}), bf16[128,16,512]{2,1,0:T(8,128)(2,1)S(1)}, u32[]{:S(2)}, u32[]{:S(2)}) %all-to-all-start) | async-done | bytes 2097184 | tf_op jit(solution)/shard_map/all_to_all | solution.py:336
  47.2 6.7 %roots.1 = (bf16[2,1024,512]{2,1,0:T(8,128)(2,1)}, bf16[2,1024,512]{2,1,0:T(8,128)(2,1)}) custom-call(s32[1]{0:T(128)} %bitcast.which_ref.rep_ref, bf16[2,1024,512]{2,1,0:T(8,128)(2,1)S(1)} %bitcast.4, bf16[2,1024,512]{2,1,0:T(8,128)(2,1)} %right_ref.1, bf16[1024,512]{1,0:T(8,128)(2,1)S(1)} %fetch.1.right_oth, bf16[2,1024,1024]{2,1,0:T(8,128)(2,1)} %left_ref.1), custom_call_target="tpu_custom_call" | custom-call | flops 4294967296 | bytes 8388608 | tf_op jit(solution)/shard_map/roots/pallas_call | solution.py:199
  53.9 1.2 %collective-permute-start.2 = (bf16[2,1024,512]{2,1,0:T(8,128)(2,1)}, bf16[2,1024,512]{2,1,0:T(8,128)(2,1)}, u32[]{:S(2)}, u32[]{:S(2)}) collective-permute-start(bf16[2,1024,512]{2,1,0:T(8,128)(2,1)} %get-tuple-element.15.own_ref), channel_id=1, source_target_pairs={{0,64},{64,0},{1,65},{65,1},{2,66},{66,2},{3,67},{67,3},{4,68},{68... | collective-permute-start | bytes 6291464 | tf_op jit(solution)/shard_map/ppermute | solution.py:348
  55.1 5.1 %all-to-all-start.1 = ((bf16[128,16,512]{2,1,0:T(8,128)(2,1)}), bf16[128,16,512]{2,1,0:T(8,128)(2,1)S(1)}, u32[]{:S(2)}, u32[]{:S(2)}) async-start(bf16[128,16,512]{2,1,0:T(8,128)(2,1)} %bitcast.7), calls=%async_computation.1 | async-start | bytes 4194304 | tf_op jit(solution)/shard_map/all_to_all | solution.py:336
  60.2 0.0 collective-permute-done.2.oth_ref
  60.2 0.0 copy-start.1
  60.2 1.6 %copy-done.1 = bf16[2,1024,512]{2,1,0:T(8,128)(2,1)S(1)} copy-done((bf16[2,1024,512]{2,1,0:T(8,128)(2,1)S(1)}, bf16[2,1024,512]{2,1,0:T(8,128)(2,1)}, u32[]{:S(2)}) %copy-start.1) | copy-done | bytes 2097176
  61.8 8.2 %grams.1 = (f32[2,512,1024]{2,1,0:T(8,128)}, f32[2,512,1024]{2,1,0:T(8,128)}) custom-call(s32[1]{0:T(128)} %bitcast.which_ref.rep_ref, bf16[2,1024,512]{2,1,0:T(8,128)(2,1)S(1)} %copy-done.1, bf16[2,1024,512]{2,1,0:T(8,128)(2,1)} %collective-permute-done.2.oth_ref), custom_call_target="tpu_custom_call" | custom-call | flops 4294967296 | bytes 12582912 | tf_op jit(solution)/shard_map/grams/pallas_call | solution.py:265
  69.9 18.8 %all-to-all-done.1.pieces_ref = bf16[128,16,512]{2,1,0:T(8,128)(2,1)S(1)} async-done(((bf16[128,16,512]{2,1,0:T(8,128)(2,1)}), bf16[128,16,512]{2,1,0:T(8,128)(2,1)S(1)}, u32[]{:S(2)}, u32[]{:S(2)}) %all-to-all-start.1) | async-done | bytes 2097184 | tf_op jit(solution)/shard_map/all_to_all | solution.py:336
  88.8 1.6 %place.1 = bf16[1280,512]{1,0:T(8,128)(2,1)} custom-call(s32[80]{0:T(128)S(1)} %get-tuple-element.17.source_ref, s32[80]{0:T(128)S(1)} %copy-done, bf16[128,16,512]{2,1,0:T(8,128)(2,1)S(1)} %all-to-all-done.1.pieces_ref), custom_call_target="tpu_custom_call" | custom-call | bytes 2621440 | tf_op jit(solution)/shard_map/place/pallas_call | solution.py:296
  (2 shorter events, 0.0 us)
Async XLA Ops:
  1.9 2.8 %copy-start.3 = (s32[80]{0:T(128)S(1)}, s32[80]{0:T(128)}, u32[]{:S(2)}) copy-start(s32[80]{0:T(128)} %param.6) | copy-start | bytes 964
  2.0 2.9 %copy-start = (s32[80]{0:T(128)S(1)}, s32[80]{0:T(128)}, u32[]{:S(2)}) copy-start(s32[80]{0:T(128)} %row_ref.1) | copy-start | bytes 964
  2.0 4.2 %collective-permute-start = (bf16[1280,512]{1,0:T(8,128)(2,1)S(1)}, bf16[1280,512]{1,0:T(8,128)(2,1)S(1)}, u32[]{:S(2)}, u32[]{:S(2)}) collective-permute-start(bf16[1280,512]{1,0:T(8,128)(2,1)S(1)} %strip.2), channel_id=1, source_target_pairs={{0,64},{64,0},{1,65},{65,1},{2,66},{66,2},{3,67},{67,3},{4,68},{68... | collective-permute-start | bytes 3932168 | tf_op jit(solution)/shard_map/ppermute | solution.py:323
  8.1 39.1 %all-to-all-start = ((bf16[128,16,512]{2,1,0:T(8,128)(2,1)}), bf16[128,16,512]{2,1,0:T(8,128)(2,1)S(1)}, u32[]{:S(2)}, u32[]{:S(2)}) async-start(bf16[128,16,512]{2,1,0:T(8,128)(2,1)} %pack.1), calls=%async_computation | async-start | bytes 4194304 | tf_op jit(solution)/shard_map/all_to_all | solution.py:336
  19.9 3.4 %collective-permute-start.1 = (bf16[1,1024,512]{2,1,0:T(8,128)(2,1)S(1)}, bf16[1,1024,512]{2,1,0:T(8,128)(2,1)S(1)}, u32[]{:S(2)}, u32[]{:S(2)}) collective-permute-start(bf16[1,1024,512]{2,1,0:T(8,128)(2,1)S(1)} %constant_dynamic-slice_fusion), channel_id=1, source_target_pairs={{0,64},{64,0},{1,65},{65,1},{2,66},{66,2},{3,67},{67,3},{4,68},{68... | collective-permute-start | bytes 3145736 | tf_op jit(solution)/shard_map/ppermute | solution.py:340
  23.3 1.0 %copy-start.2 = (bf16[1,1024,512]{2,1,0:T(8,128)(2,1)}, bf16[1,1024,512]{2,1,0:T(8,128)(2,1)S(1)}, u32[]{:S(2)}) copy-start(bf16[1,1024,512]{2,1,0:T(8,128)(2,1)S(1)} %collective-permute-done.1.right_ref) | copy-start | bytes 3145732
  53.9 6.3 %collective-permute-start.2 = (bf16[2,1024,512]{2,1,0:T(8,128)(2,1)}, bf16[2,1024,512]{2,1,0:T(8,128)(2,1)}, u32[]{:S(2)}, u32[]{:S(2)}) collective-permute-start(bf16[2,1024,512]{2,1,0:T(8,128)(2,1)} %get-tuple-element.15.own_ref), channel_id=1, source_target_pairs={{0,64},{64,0},{1,65},{65,1},{2,66},{66,2},{3,67},{67,3},{4,68},{68... | collective-permute-start | bytes 6291464 | tf_op jit(solution)/shard_map/ppermute | solution.py:348
  55.1 33.7 %all-to-all-start.1 = ((bf16[128,16,512]{2,1,0:T(8,128)(2,1)}), bf16[128,16,512]{2,1,0:T(8,128)(2,1)S(1)}, u32[]{:S(2)}, u32[]{:S(2)}) async-start(bf16[128,16,512]{2,1,0:T(8,128)(2,1)} %bitcast.7), calls=%async_computation.1 | async-start | bytes 4194304 | tf_op jit(solution)/shard_map/all_to_all | solution.py:336
  60.2 1.6 %copy-start.1 = (bf16[2,1024,512]{2,1,0:T(8,128)(2,1)S(1)}, bf16[2,1024,512]{2,1,0:T(8,128)(2,1)}, u32[]{:S(2)}) copy-start(bf16[2,1024,512]{2,1,0:T(8,128)(2,1)} %get-tuple-element.15.own_ref) | copy-start | bytes 6291460

commit v5 on v4

--- a/solution.py
+++ b/solution.py
@@ -88,48 +88,38 @@
     )(in_hbm(right))
 
 
-def pack_kernel(steps, place_ref, mine_ref, theirs_ref, out_ref, total, sems):
-    pieces, piece, _ = total.shape
-    chunk = pieces // steps
-    moves = []
-    for k in range(steps):
-
-        def step(i, carry, k=k):
-            where = place_ref[k * chunk + i]
-            rows = pl.ds(pl.multiple_of(jnp.maximum(where, 0) * piece, piece), piece)
-            both = mine_ref[rows, :] + theirs_ref[rows, :]
-            total[k * chunk + i] = jnp.where(where >= 0, both, jnp.zeros_like(both))
-            return carry
-
-        lax.fori_loop(0, chunk, step, 0, unroll=8)
-        here = pl.ds(k * chunk, chunk)
-        move = pltpu.make_async_copy(total.at[here], out_ref.at[here], sems.at[k])
-        move.start()
-        moves.append(move)
-    for move in moves:
-        move.wait()
-
-
-def pack(pieces, piece, place, mine, theirs):
+def pack_kernel(slot_ref, mine_ref, theirs_ref, out_ref, total, sem):
+    piece = out_ref.shape[1]
+
+    def step(i, carry):
+        rows = pl.ds(pl.multiple_of(i * piece, piece), piece)
+        total[rows, :] = mine_ref[rows, :] + theirs_ref[rows, :]
+        pltpu.make_async_copy(total.at[rows], out_ref.at[slot_ref[i]], sem).start()
+        return carry
+
+    lax.fori_loop(0, total.shape[0] // piece, step, 0, unroll=16)
+    pltpu.make_async_copy(total, total, sem).wait()
+
+
+def pack(pieces, piece, slot_of_row, mine, theirs):
     rows, strip = theirs.shape
-    steps = 8
-    return pl.pallas_call(
-        functools.partial(pack_kernel, steps),
+    return pl.pallas_call(
+        pack_kernel,
         grid_spec=pltpu.PrefetchScalarGridSpec(
             num_scalar_prefetch=1,
             grid=(1,),
             in_specs=[pl.BlockSpec(memory_space=pltpu.VMEM)] * 2,
             out_specs=pl.BlockSpec(memory_space=pltpu.HBM),
             scratch_shapes=[
-                pltpu.VMEM((pieces, piece, strip), theirs.dtype),
-                pltpu.SemaphoreType.DMA((steps,)),
+                pltpu.VMEM((rows, strip), theirs.dtype),
+                pltpu.SemaphoreType.DMA,
             ],
         ),
         out_shape=pltpu.HBM((pieces, piece, strip), theirs.dtype),
         compiler_params=params(),
-        cost_estimate=cost(rows * strip, 2 * pieces * piece * strip),
+        cost_estimate=cost(rows * strip, 2 * rows * strip),
         name="pack",
-    )(place, in_vmem(mine), in_vmem(theirs))
+    )(slot_of_row, in_vmem(mine), in_vmem(theirs))
 
 
 def root_kernel(
@@ -226,11 +216,12 @@
     )(rep, in_vmem(grad), in_hbm(right_root), in_vmem(right_oth), in_hbm(left_root))
 
 
-def gram_kernel(steps, rep_ref, own_ref, oth_ref, left_out, right_out):
+def gram_kernel(steps, rep_ref, held_ref, own_ref, oth_ref, left_out, right_out):
     i = pl.program_id(0)
     rep = rep_ref[0]
 
-    def form(grad_ref):
+    def form(grad_ref, slot):
+        held = held_ref[slot] != 0
         strips, _, strip = grad_ref.shape
         tile = strip // steps
         begin = pl.multiple_of((i % steps) * tile, tile)
@@ -242,39 +233,40 @@
             left += lax.dot_general(
                 grad_ref[k, rows, :], grad_ref[k], NT, preferred_element_type=jnp.float32
             )
-        left_out[0] = left
+        left_out[0] = jnp.where(held, left, 0.0)
         columns = grad_ref[rep, :, pl.ds(begin, tile)]
         for k in range(strips):
-            right_out[0, :, k * strip : (k + 1) * strip] = lax.dot_general(
+            right = lax.dot_general(
                 columns, grad_ref[k], TN, preferred_element_type=jnp.float32
             )
-
-    pl.when(i < steps)(lambda: form(own_ref))
-    pl.when(i >= steps)(lambda: form(oth_ref))
-
-
-def grams(rep, own, oth):
+            right_out[0, :, k * strip : (k + 1) * strip] = jnp.where(held, right, 0.0)
+
+    pl.when(i < steps)(lambda: form(own_ref, rep))
+    pl.when(i >= steps)(lambda: form(oth_ref, 1 - rep))
+
+
+def grams(rep, held, own, oth):
     slots, block, strip = own.shape
     steps = 2
     tile = strip // steps
     out = jax.ShapeDtypeStruct((slots, strip, block), jnp.float32)
 
-    def where(i, rep):
+    def where(i, rep, held):
         return (jnp.where(i < steps, rep[0], 1 - rep[0]), i % steps, 0)
 
     return pl.pallas_call(
         functools.partial(gram_kernel, steps),
         grid_spec=pltpu.PrefetchScalarGridSpec(
-            num_scalar_prefetch=1,
+            num_scalar_prefetch=2,
             grid=(2 * steps,),
-            in_specs=[pl.BlockSpec(own.shape, lambda i, rep: (0, 0, 0))] * 2,
+            in_specs=[pl.BlockSpec(own.shape, lambda i, rep, held: (0, 0, 0))] * 2,
             out_specs=[pl.BlockSpec((1, tile, block), where)] * 2,
         ),
         out_shape=[out, out],
         compiler_params=params(),
         cost_estimate=cost(8 * block * block * strip, 24 * block * strip),
         name="grams",
-    )(rep, own, oth)
+    )(rep, held, own, oth)
 
 
 def place_kernel(source_ref, row_ref, pieces_ref, out_ref, sem):
@@ -327,15 +319,16 @@
     before = block_ids[:, None] < block_ids[None, :]
     rank = jnp.sum(jnp.where(same_owner & before, 1, 0), axis=0).astype(jnp.int32)
     holder_id = rank * shard_count + owner_table
-    holder_ids = jnp.arange(slots * shard_count, dtype=jnp.int32)
-    held = holder_id[:, None] == holder_ids[None, :]
-    place = jnp.sum(jnp.where(held, (offsets // piece)[:, None] + 1, 0), axis=0) - 1
-    place = place.astype(jnp.int32)
+    at_row = (offsets // piece)[:, None] == block_ids[None, :]
+    slot_of_row = jnp.sum(jnp.where(at_row, holder_id[:, None], 0), axis=0).astype(jnp.int32)
+    my_slots = jnp.arange(slots, dtype=jnp.int32) * shard_count + lax.axis_index("shard")
+    held = jnp.sum(jnp.where(holder_id[:, None] == my_slots[None, :], 1, 0), axis=0)
+    held = held.astype(jnp.int32)
 
     def exchange(x):
         return lax.all_to_all(x, BOTH, split_axis=0, concat_axis=0, tiled=True)
 
-    packed = pack(slots * shard_count, piece, place, mine, theirs)
+    packed = pack(slots * shard_count, piece, slot_of_row, mine, theirs)
     packed, right_later = lax.optimization_barrier((packed, right_root))
     right_oth = lax.ppermute(
         lax.dynamic_slice_in_dim(right_later, 1 - me, 1, 0), "rep", SWAP
@@ -346,7 +339,7 @@
     update, grad = lax.optimization_barrier((update, grad))
     back = exchange(update.reshape(packed.shape))
     grad_other = lax.ppermute(grad, "rep", SWAP)
-    gram_left, gram_right = grams(rep, grad, grad_other)
+    gram_left, gram_right = grams(rep, held, grad, grad_other)
     holder_id, gram_left = lax.optimization_barrier((holder_id, gram_left))
     return place_rows(rows, holder_id, offsets, back), gram_left, gram_right
 

time: 90.8 us -> 90.4 us (level)
  transfers between devices with their start and end apart: 5 -> 5, of which waited for: 4 -> 4; matrix products, arithmetic and copies ran while one was open for 2% -> 2% of each run, Pallas kernels for 12% -> 13%
where the time goes in v5:
time: 90.4 us; the launch traced here: 90 us
  waiting for transfers between devices  43.1 us (48%)
  Pallas kernels  22.5 us (25%)
  starting transfers between devices  19.4 us (21%)
  local copies, waits for them, and re-layouts  3.87 us (4%)
    all_to_all x2, waiting for transfers between devices, exchange(): return lax.all_to_all(x, BOTH, split_axis=0, concat_axis=0, tiled=True)  39.7 us
    all_to_all x2, starting transfers between devices, exchange(): return lax.all_to_all(x, BOTH, split_axis=0, concat_axis=0, tiled=True)  15.5 us
    pallas_call x1, Pallas kernels, grams(): pl.pallas_call(functools.partial(gram_kernel, steps), grid_spec=pltpu.Pre...  8.8 us
    pallas_call x1, Pallas kernels, apply_roots(): pl.pallas_call(functools.partial(root_kernel, steps), grid_spec=pltpu.Pre...  6.67 us
    pallas_call x2, Pallas kernels, take_strip(): pl.pallas_call(functools.partial(strip_kernel, steps), grid_spec=pltpu.Pr...  2.61 us
    unnamed x8, local copies, waits for them, and re-layouts  2.57 us
    ppermute x1, waiting for transfers between devices, local(): lax.ppermute(lax.dynamic_slice_in_dim(right_later, 1 - me, 1, 0), 'rep',...  2.29 us
  transfers between devices with their start and end apart: 5, of which 4 were waited for; matrix products, arithmetic and copies ran while one was open for 2% of the time, Pallas kernels for 13%

profile of v5, /device:TPU:1, one launch (start us, length us, event | category | flops | bytes accessed | tf_op | source)
XLA Modules:
  0.0 90.0 jit_solution(12600323364022078627)
XLA Ops:
  0.6 1.3 %strip.2 = bf16[1280,512]{1,0:T(8,128)(2,1)S(1)} custom-call(s32[1]{0:T(128)S(6)} %sub.13.which_ref, bf16[1280,1024]{1,0:T(8,128)(2,1)} %bitcast.5), custom_call_target="tpu_custom_call" | custom-call | bytes 2621440 | tf_op jit(solution)/shard_map/strip/pallas_call | solution.py:50
  1.9 0.0 copy-start.3
  2.0 0.0 copy-start
  2.0 1.5 %collective-permute-start = (bf16[1280,512]{1,0:T(8,128)(2,1)S(1)}, bf16[1280,512]{1,0:T(8,128)(2,1)S(1)}, u32[]{:S(2)}, u32[]{:S(2)}) collective-permute-start(bf16[1280,512]{1,0:T(8,128)(2,1)S(1)} %strip.2), channel_id=1, source_target_pairs={{0,64},{64,0},{1,65},{65,1},{2,66},{66,2},{3,67},{67,3},{4,68},{68... | collective-permute-start | bytes 3932168 | tf_op jit(solution)/shard_map/ppermute | solution.py:315
  3.5 1.3 %strip.3.mine_ref = bf16[1280,512]{1,0:T(8,128)(2,1)S(1)} custom-call(s32[1]{0:T(128)} %bitcast.which_ref.rep_ref, bf16[1280,1024]{1,0:T(8,128)(2,1)} %bitcast.6), custom_call_target="tpu_custom_call" | custom-call | bytes 2621440 | tf_op jit(solution)/shard_map/strip/pallas_call | solution.py:50
  4.8 0.0 copy-done.3
  4.8 0.1 select_reduce_fusion.1
  4.9 0.0 copy-done
  4.9 0.1 select_reduce_fusion.slot_ref
  5.0 1.1 %collective-permute-done.theirs_ref = bf16[1280,512]{1,0:T(8,128)(2,1)S(1)} collective-permute-done((bf16[1280,512]{1,0:T(8,128)(2,1)S(1)}, bf16[1280,512]{1,0:T(8,128)(2,1)S(1)}, u32[]{:S(2)}, u32[]{:S(2)}) %collective-permute-start) | collective-permute-done | bytes 1310752 | tf_op jit(solution)/shard_map/ppermute | solution.py:315
  6.1 1.6 %pack.1 = bf16[128,16,512]{2,1,0:T(8,128)(2,1)} custom-call(s32[80]{0:T(128)S(1)} %select_reduce_fusion.slot_ref, bf16[1280,512]{1,0:T(8,128)(2,1)S(1)} %strip.3.mine_ref, bf16[1280,512]{1,0:T(8,128)(2,1)S(1)} %collective-permute-done.theirs_ref), custom_call_target="tpu_custom_call" | custom-call | flops 655360 | bytes 1310720 | tf_op jit(solution)/shard_map/pack/pallas_call | solution.py:106
  7.7 10.5 %all-to-all-start = ((bf16[128,16,512]{2,1,0:T(8,128)(2,1)}), bf16[128,16,512]{2,1,0:T(8,128)(2,1)S(1)}, u32[]{:S(2)}, u32[]{:S(2)}) async-start(bf16[128,16,512]{2,1,0:T(8,128)(2,1)} %pack.1), calls=%async_computation | async-start | bytes 4194304 | tf_op jit(solution)/shard_map/all_to_all | solution.py:329
  18.2 1.3 %constant_dynamic-slice_fusion = bf16[1,1024,512]{2,1,0:T(8,128)(2,1)S(1)} fusion(bf16[2,1024,512]{2,1,0:T(8,128)(2,1)} %right_ref.1, s32[]{:T(128)S(6)} %select_n.24), kind=kLoop, calls=%fused_computation.13 | loop fusion | bytes 2097156 | tf_op jit(solution)/shard_map/dynamic_slice | solution.py:334
  19.5 1.1 %collective-permute-start.1 = (bf16[1,1024,512]{2,1,0:T(8,128)(2,1)S(1)}, bf16[1,1024,512]{2,1,0:T(8,128)(2,1)S(1)}, u32[]{:S(2)}, u32[]{:S(2)}) collective-permute-start(bf16[1,1024,512]{2,1,0:T(8,128)(2,1)S(1)} %constant_dynamic-slice_fusion), channel_id=1, source_target_pairs={{0,64},{64,0},{1,65},{65,1},{2,66},{66,2},{3,67},{67,3},{4,68},{68... | collective-permute-start | bytes 3145736 | tf_op jit(solution)/shard_map/ppermute | solution.py:333
  20.7 2.3 %collective-permute-done.1.right_ref = bf16[1,1024,512]{2,1,0:T(8,128)(2,1)S(1)} collective-permute-done((bf16[1,1024,512]{2,1,0:T(8,128)(2,1)S(1)}, bf16[1,1024,512]{2,1,0:T(8,128)(2,1)S(1)}, u32[]{:S(2)}, u32[]{:S(2)}) %collective-permute-start.1) | collective-permute-done | bytes 1048608 | tf_op jit(solution)/shard_map/ppermute | solution.py:333
  22.9 0.0 copy-start.2
  23.0 1.0 %copy-done.2 = bf16[1,1024,512]{2,1,0:T(8,128)(2,1)} copy-done((bf16[1,1024,512]{2,1,0:T(8,128)(2,1)}, bf16[1,1024,512]{2,1,0:T(8,128)(2,1)S(1)}, u32[]{:S(2)}) %copy-start.2) | copy-done | bytes 1048600
  23.9 1.2 %fetch.1.right_oth = bf16[1024,512]{1,0:T(8,128)(2,1)S(1)} custom-call(bf16[1,1024,512]{2,1,0:T(8,128)(2,1)} %copy-done.2), custom_call_target="tpu_custom_call" | custom-call | bytes 2097152 | tf_op jit(solution)/shard_map/fetch/pallas_call | solution.py:79
  25.1 21.7 %all-to-all-done = bf16[128,16,512]{2,1,0:T(8,128)(2,1)S(1)} async-done(((bf16[128,16,512]{2,1,0:T(8,128)(2,1)}), bf16[128,16,512]{2,1,0:T(8,128)(2,1)S(1)}, u32[]{:S(2)}, u32[]{:S(2)}) %all-to-all-start) | async-done | bytes 2097184 | tf_op jit(solution)/shard_map/all_to_all | solution.py:329
  46.8 6.7 %roots.1 = (bf16[2,1024,512]{2,1,0:T(8,128)(2,1)}, bf16[2,1024,512]{2,1,0:T(8,128)(2,1)}) custom-call(s32[1]{0:T(128)} %bitcast.which_ref.rep_ref, bf16[2,1024,512]{2,1,0:T(8,128)(2,1)S(1)} %bitcast.4, bf16[2,1024,512]{2,1,0:T(8,128)(2,1)} %right_ref.1, bf16[1024,512]{1,0:T(8,128)(2,1)S(1)} %fetch.1.right_oth, bf16[2,1024,1024]{2,1,0:T(8,128)(2,1)} %left_ref.1), custom_call_target="tpu_custom_call" | custom-call | flops 4294967296 | bytes 8388608 | tf_op jit(solution)/shard_map/roots/pallas_call | solution.py:189
  53.5 1.2 %collective-permute-start.2 = (bf16[2,1024,512]{2,1,0:T(8,128)(2,1)}, bf16[2,1024,512]{2,1,0:T(8,128)(2,1)}, u32[]{:S(2)}, u32[]{:S(2)}) collective-permute-start(bf16[2,1024,512]{2,1,0:T(8,128)(2,1)} %get-tuple-element.15.own_ref), channel_id=1, source_target_pairs={{0,64},{64,0},{1,65},{65,1},{2,66},{66,2},{3,67},{67,3},{4,68},{68... | collective-permute-start | bytes 6291464 | tf_op jit(solution)/shard_map/ppermute | solution.py:341
  54.7 5.1 %all-to-all-start.1 = ((bf16[128,16,512]{2,1,0:T(8,128)(2,1)}), bf16[128,16,512]{2,1,0:T(8,128)(2,1)S(1)}, u32[]{:S(2)}, u32[]{:S(2)}) async-start(bf16[128,16,512]{2,1,0:T(8,128)(2,1)} %bitcast.7), calls=%async_computation.1 | async-start | bytes 4194304 | tf_op jit(solution)/shard_map/all_to_all | solution.py:329
  59.8 0.2 fusion.1.held_ref
  60.0 0.0 collective-permute-done.2.oth_ref
  60.0 0.0 copy-start.1
  60.0 1.6 %copy-done.1 = bf16[2,1024,512]{2,1,0:T(8,128)(2,1)S(1)} copy-done((bf16[2,1024,512]{2,1,0:T(8,128)(2,1)S(1)}, bf16[2,1024,512]{2,1,0:T(8,128)(2,1)}, u32[]{:S(2)}) %copy-start.1) | copy-done | bytes 2097176
  61.6 8.8 %grams.1 = (f32[2,512,1024]{2,1,0:T(8,128)}, f32[2,512,1024]{2,1,0:T(8,128)}) custom-call(s32[1]{0:T(128)} %bitcast.which_ref.rep_ref, s32[2]{0:T(128)S(1)} %fusion.1.held_ref, bf16[2,1024,512]{2,1,0:T(8,128)(2,1)S(1)} %copy-done.1, bf16[2,1024,512]{2,1,0:T(8,128)(2,1)} %collective-permute-done.2.oth_ref), custom_call_target="tpu_custom_call" | custom-call | flops 4294967296 | bytes 12582912 | tf_op jit(solution)/shard_map/grams/pallas_call | solution.py:257
  70.4 18.0 %all-to-all-done.1.pieces_ref = bf16[128,16,512]{2,1,0:T(8,128)(2,1)S(1)} async-done(((bf16[128,16,512]{2,1,0:T(8,128)(2,1)}), bf16[128,16,512]{2,1,0:T(8,128)(2,1)S(1)}, u32[]{:S(2)}, u32[]{:S(2)}) %all-to-all-start.1) | async-done | bytes 2097184 | tf_op jit(solution)/shard_map/all_to_all | solution.py:329
  88.4 1.6 %place.1 = bf16[1280,512]{1,0:T(8,128)(2,1)} custom-call(s32[80]{0:T(128)S(1)} %get-tuple-element.17.source_ref, s32[80]{0:T(128)S(1)} %copy-done, bf16[128,16,512]{2,1,0:T(8,128)(2,1)S(1)} %all-to-all-done.1.pieces_ref), custom_call_target="tpu_custom_call" | custom-call | bytes 2621440 | tf_op jit(solution)/shard_map/place/pallas_call | solution.py:288
  (2 shorter events, 0.0 us)
Async XLA Ops:
  1.9 2.8 %copy-start.3 = (s32[80]{0:T(128)S(1)}, s32[80]{0:T(128)}, u32[]{:S(2)}) copy-start(s32[80]{0:T(128)} %param.6) | copy-start | bytes 964
  2.0 2.9 %copy-start = (s32[80]{0:T(128)S(1)}, s32[80]{0:T(128)}, u32[]{:S(2)}) copy-start(s32[80]{0:T(128)} %row_ref.1) | copy-start | bytes 964
  2.0 4.2 %collective-permute-start = (bf16[1280,512]{1,0:T(8,128)(2,1)S(1)}, bf16[1280,512]{1,0:T(8,128)(2,1)S(1)}, u32[]{:S(2)}, u32[]{:S(2)}) collective-permute-start(bf16[1280,512]{1,0:T(8,128)(2,1)S(1)} %strip.2), channel_id=1, source_target_pairs={{0,64},{64,0},{1,65},{65,1},{2,66},{66,2},{3,67},{67,3},{4,68},{68... | collective-permute-start | bytes 3932168 | tf_op jit(solution)/shard_map/ppermute | solution.py:315
  7.7 39.1 %all-to-all-start = ((bf16[128,16,512]{2,1,0:T(8,128)(2,1)}), bf16[128,16,512]{2,1,0:T(8,128)(2,1)S(1)}, u32[]{:S(2)}, u32[]{:S(2)}) async-start(bf16[128,16,512]{2,1,0:T(8,128)(2,1)} %pack.1), calls=%async_computation | async-start | bytes 4194304 | tf_op jit(solution)/shard_map/all_to_all | solution.py:329
  19.5 3.4 %collective-permute-start.1 = (bf16[1,1024,512]{2,1,0:T(8,128)(2,1)S(1)}, bf16[1,1024,512]{2,1,0:T(8,128)(2,1)S(1)}, u32[]{:S(2)}, u32[]{:S(2)}) collective-permute-start(bf16[1,1024,512]{2,1,0:T(8,128)(2,1)S(1)} %constant_dynamic-slice_fusion), channel_id=1, source_target_pairs={{0,64},{64,0},{1,65},{65,1},{2,66},{66,2},{3,67},{67,3},{4,68},{68... | collective-permute-start | bytes 3145736 | tf_op jit(solution)/shard_map/ppermute | solution.py:333
  22.9 1.0 %copy-start.2 = (bf16[1,1024,512]{2,1,0:T(8,128)(2,1)}, bf16[1,1024,512]{2,1,0:T(8,128)(2,1)S(1)}, u32[]{:S(2)}) copy-start(bf16[1,1024,512]{2,1,0:T(8,128)(2,1)S(1)} %collective-permute-done.1.right_ref) | copy-start | bytes 3145732
  53.5 6.5 %collective-permute-start.2 = (bf16[2,1024,512]{2,1,0:T(8,128)(2,1)}, bf16[2,1024,512]{2,1,0:T(8,128)(2,1)}, u32[]{:S(2)}, u32[]{:S(2)}) collective-permute-start(bf16[2,1024,512]{2,1,0:T(8,128)(2,1)} %get-tuple-element.15.own_ref), channel_id=1, source_target_pairs={{0,64},{64,0},{1,65},{65,1},{2,66},{66,2},{3,67},{67,3},{4,68},{68... | collective-permute-start | bytes 6291464 | tf_op jit(solution)/shard_map/ppermute | solution.py:341
  54.7 33.7 %all-to-all-start.1 = ((bf16[128,16,512]{2,1,0:T(8,128)(2,1)}), bf16[128,16,512]{2,1,0:T(8,128)(2,1)S(1)}, u32[]{:S(2)}, u32[]{:S(2)}) async-start(bf16[128,16,512]{2,1,0:T(8,128)(2,1)} %bitcast.7), calls=%async_computation.1 | async-start | bytes 4194304 | tf_op jit(solution)/shard_map/all_to_all | solution.py:329
  60.0 1.6 %copy-start.1 = (bf16[2,1024,512]{2,1,0:T(8,128)(2,1)S(1)}, bf16[2,1024,512]{2,1,0:T(8,128)(2,1)}, u32[]{:S(2)}) copy-start(bf16[2,1024,512]{2,1,0:T(8,128)(2,1)} %get-tuple-element.15.own_ref) | copy-start | bytes 6291460

commit v6 on v5

--- a/solution.py
+++ b/solution.py
@@ -216,57 +216,55 @@
     )(rep, in_vmem(grad), in_hbm(right_root), in_vmem(right_oth), in_hbm(left_root))
 
 
-def gram_kernel(steps, rep_ref, held_ref, own_ref, oth_ref, left_out, right_out):
-    i = pl.program_id(0)
+def gram_kernel(steps, rep_ref, slot_ref, held_ref, grad_ref, *rest):
+    left_out, right_out = rest[-2:]
+    strips, _, strip = grad_ref.shape
+    tile = strip // steps
     rep = rep_ref[0]
-
-    def form(grad_ref, slot):
-        held = held_ref[slot] != 0
-        strips, _, strip = grad_ref.shape
-        tile = strip // steps
-        begin = pl.multiple_of((i % steps) * tile, tile)
-        rows = pl.ds(pl.multiple_of(rep * strip + begin, tile), tile)
-        left = lax.dot_general(
-            grad_ref[0, rows, :], grad_ref[0], NT, preferred_element_type=jnp.float32
+    held = held_ref[slot_ref[0]] != 0
+    begin = pl.multiple_of(pl.program_id(0) * tile, tile)
+    rows = pl.ds(pl.multiple_of(rep * strip + begin, tile), tile)
+    left = lax.dot_general(
+        grad_ref[0, rows, :], grad_ref[0], NT, preferred_element_type=jnp.float32
+    )
+    for k in range(1, strips):
+        left += lax.dot_general(
+            grad_ref[k, rows, :], grad_ref[k], NT, preferred_element_type=jnp.float32
         )
-        for k in range(1, strips):
-            left += lax.dot_general(
-                grad_ref[k, rows, :], grad_ref[k], NT, preferred_element_type=jnp.float32
-            )
-        left_out[0] = jnp.where(held, left, 0.0)
-        columns = grad_ref[rep, :, pl.ds(begin, tile)]
-        for k in range(strips):
-            right = lax.dot_general(
-                columns, grad_ref[k], TN, preferred_element_type=jnp.float32
-            )
-            right_out[0, :, k * strip : (k + 1) * strip] = jnp.where(held, right, 0.0)
-
-    pl.when(i < steps)(lambda: form(own_ref, rep))
-    pl.when(i >= steps)(lambda: form(oth_ref, 1 - rep))
-
-
-def grams(rep, held, own, oth):
-    slots, block, strip = own.shape
+    left_out[0] = jnp.where(held, left, 0.0)
+    columns = grad_ref[rep, :, pl.ds(begin, tile)]
+    for k in range(strips):
+        right = lax.dot_general(columns, grad_ref[k], TN, preferred_element_type=jnp.float32)
+        right_out[0, :, k * strip : (k + 1) * strip] = jnp.where(held, right, 0.0)
+
+
+def grams(slots, rep, slot, held, grad, previous):
+    strips, block, strip = grad.shape
     steps = 2
     tile = strip // steps
     out = jax.ShapeDtypeStruct((slots, strip, block), jnp.float32)
 
-    def where(i, rep, held):
-        return (jnp.where(i < steps, rep[0], 1 - rep[0]), i % steps, 0)
+    def whole(i, rep, slot, held):
+        return (0, 0, 0)
+
+    def where(i, rep, slot, held):
+        return (slot[0], i, 0)
 
     return pl.pallas_call(
         functools.partial(gram_kernel, steps),
         grid_spec=pltpu.PrefetchScalarGridSpec(
-            num_scalar_prefetch=2,
-            grid=(2 * steps,),
-            in_specs=[pl.BlockSpec(own.shape, lambda i, rep, held: (0, 0, 0))] * 2,
+            num_scalar_prefetch=3,
+            grid=(steps,),
+            in_specs=[pl.BlockSpec(grad.shape, whole)]
+            + [pl.BlockSpec(memory_space=pl.ANY)] * len(previous),
             out_specs=[pl.BlockSpec((1, tile, block), where)] * 2,
         ),
         out_shape=[out, out],
-        compiler_params=params(),
-        cost_estimate=cost(8 * block * block * strip, 24 * block * strip),
+        input_output_aliases={4 + k: k for k in range(len(previous))},
+        compiler_params=params(),
+        cost_estimate=cost(4 * block * block * strip, 12 * block * strip),
         name="grams",
-    )(rep, held, own, oth)
+    )(rep, slot, held, grad, *previous)
 
 
 def place_kernel(source_ref, row_ref, pieces_ref, out_ref, sem):
@@ -339,7 +337,8 @@
     update, grad = lax.optimization_barrier((update, grad))
     back = exchange(update.reshape(packed.shape))
     grad_other = lax.ppermute(grad, "rep", SWAP)
-    gram_left, gram_right = grams(rep, held, grad, grad_other)
+    gram = grams(slots, rep, rep, held, grad, ())
+    gram_left, gram_right = grams(slots, rep, 1 - rep, held, grad_other, tuple(gram))
     holder_id, gram_left = lax.optimization_barrier((holder_id, gram_left))
     return place_rows(rows, holder_id, offsets, back), gram_left, gram_right
 

time: 90.4 us -> 90.4 us (level)
  Pallas kernels: 22.5 us -> 23.6 us
  waiting for transfers between devices: 43.1 us -> 42 us
    pallas_call x1 -> x2, Pallas kernels: 8.8 us -> 9.86 us  [grams(): pl.pallas_call(functools.partial(gram_kernel, steps), grid_spec=pltpu.Pre...]
    all_to_all x2, waiting for transfers between devices: 39.7 us -> 38.6 us  [exchange(): return lax.all_to_all(x, BOTH, split_axis=0, concat_axis=0, tiled=True)]
  transfers between devices with their start and end apart: 5 -> 5, of which waited for: 4 -> 4; matrix products, arithmetic and copies ran while one was open for 2% -> 2% of each run, Pallas kernels for 13% -> 14%
where the time goes in v6:
time: 90.4 us; the launch traced here: 90 us
  waiting for transfers between devices  42 us (46%)
  Pallas kernels  23.6 us (26%)
  starting transfers between devices  19.4 us (21%)
  local copies, waits for them, and re-layouts  3.87 us (4%)
    all_to_all x2, waiting for transfers between devices, exchange(): return lax.all_to_all(x, BOTH, split_axis=0, concat_axis=0, tiled=True)  38.6 us
    all_to_all x2, starting transfers between devices, exchange(): return lax.all_to_all(x, BOTH, split_axis=0, concat_axis=0, tiled=True)  15.5 us
    pallas_call x2, Pallas kernels, grams(): pl.pallas_call(functools.partial(gram_kernel, steps), grid_spec=pltpu.Pre...  9.86 us
    pallas_call x1, Pallas kernels, apply_roots(): pl.pallas_call(functools.partial(root_kernel, steps), grid_spec=pltpu.Pre...  6.7 us
    pallas_call x2, Pallas kernels, take_strip(): pl.pallas_call(functools.partial(strip_kernel, steps), grid_spec=pltpu.Pr...  2.61 us
    unnamed x8, local copies, waits for them, and re-layouts  2.57 us
    ppermute x1, waiting for transfers between devices, local(): lax.ppermute(lax.dynamic_slice_in_dim(right_later, 1 - me, 1, 0), 'rep',...  2.29 us
  transfers between devices with their start and end apart: 5, of which 4 were waited for; matrix products, arithmetic and copies ran while one was open for 2% of the time, Pallas kernels for 14%

profile of v6, /device:TPU:1, one launch (start us, length us, event | category | flops | bytes accessed | tf_op | source)
XLA Modules:
  0.0 90.0 jit_solution(11724394115038529199)
XLA Ops:
  0.6 1.3 %strip.2 = bf16[1280,512]{1,0:T(8,128)(2,1)S(1)} custom-call(s32[1]{0:T(128)S(6)} %sub.13.which_ref.slot_ref, bf16[1280,1024]{1,0:T(8,128)(2,1)} %bitcast.5), custom_call_target="tpu_custom_call" | custom-call | bytes 2621440 | tf_op jit(solution)/shard_map/strip/pallas_call | solution.py:50
  1.9 0.0 copy-start.3
  2.0 0.0 copy-start
  2.0 1.5 %collective-permute-start = (bf16[1280,512]{1,0:T(8,128)(2,1)S(1)}, bf16[1280,512]{1,0:T(8,128)(2,1)S(1)}, u32[]{:S(2)}, u32[]{:S(2)}) collective-permute-start(bf16[1280,512]{1,0:T(8,128)(2,1)S(1)} %strip.2), channel_id=1, source_target_pairs={{0,64},{64,0},{1,65},{65,1},{2,66},{66,2},{3,67},{67,3},{4,68},{68... | collective-permute-start | bytes 3932168 | tf_op jit(solution)/shard_map/ppermute | solution.py:313
  3.5 1.3 %strip.3.mine_ref = bf16[1280,512]{1,0:T(8,128)(2,1)S(1)} custom-call(s32[1]{0:T(128)} %bitcast.which_ref.rep_ref.slot_ref, bf16[1280,1024]{1,0:T(8,128)(2,1)} %bitcast.6), custom_call_target="tpu_custom_call" | custom-call | bytes 2621440 | tf_op jit(solution)/shard_map/strip/pallas_call | solution.py:50
  4.8 0.0 copy-done.3
  4.8 0.1 select_reduce_fusion.1
  4.9 0.0 copy-done
  4.9 0.1 select_reduce_fusion.slot_ref
  5.0 1.1 %collective-permute-done.theirs_ref = bf16[1280,512]{1,0:T(8,128)(2,1)S(1)} collective-permute-done((bf16[1280,512]{1,0:T(8,128)(2,1)S(1)}, bf16[1280,512]{1,0:T(8,128)(2,1)S(1)}, u32[]{:S(2)}, u32[]{:S(2)}) %collective-permute-start) | collective-permute-done | bytes 1310752 | tf_op jit(solution)/shard_map/ppermute | solution.py:313
  6.1 1.6 %pack.1 = bf16[128,16,512]{2,1,0:T(8,128)(2,1)} custom-call(s32[80]{0:T(128)S(1)} %select_reduce_fusion.slot_ref, bf16[1280,512]{1,0:T(8,128)(2,1)S(1)} %strip.3.mine_ref, bf16[1280,512]{1,0:T(8,128)(2,1)S(1)} %collective-permute-done.theirs_ref), custom_call_target="tpu_custom_call" | custom-call | flops 655360 | bytes 1310720 | tf_op jit(solution)/shard_map/pack/pallas_call | solution.py:106
  7.7 10.5 %all-to-all-start = ((bf16[128,16,512]{2,1,0:T(8,128)(2,1)}), bf16[128,16,512]{2,1,0:T(8,128)(2,1)S(1)}, u32[]{:S(2)}, u32[]{:S(2)}) async-start(bf16[128,16,512]{2,1,0:T(8,128)(2,1)} %pack.1), calls=%async_computation | async-start | bytes 4194304 | tf_op jit(solution)/shard_map/all_to_all | solution.py:327
  18.2 1.3 %constant_dynamic-slice_fusion = bf16[1,1024,512]{2,1,0:T(8,128)(2,1)S(1)} fusion(bf16[2,1024,512]{2,1,0:T(8,128)(2,1)} %right_ref.1, s32[]{:T(128)S(6)} %select_n.24), kind=kLoop, calls=%fused_computation.13 | loop fusion | bytes 2097156 | tf_op jit(solution)/shard_map/dynamic_slice | solution.py:332
  19.5 1.1 %collective-permute-start.1 = (bf16[1,1024,512]{2,1,0:T(8,128)(2,1)S(1)}, bf16[1,1024,512]{2,1,0:T(8,128)(2,1)S(1)}, u32[]{:S(2)}, u32[]{:S(2)}) collective-permute-start(bf16[1,1024,512]{2,1,0:T(8,128)(2,1)S(1)} %constant_dynamic-slice_fusion), channel_id=1, source_target_pairs={{0,64},{64,0},{1,65},{65,1},{2,66},{66,2},{3,67},{67,3},{4,68},{68... | collective-permute-start | bytes 3145736 | tf_op jit(solution)/shard_map/ppermute | solution.py:331
  20.7 2.3 %collective-permute-done.1.right_ref = bf16[1,1024,512]{2,1,0:T(8,128)(2,1)S(1)} collective-permute-done((bf16[1,1024,512]{2,1,0:T(8,128)(2,1)S(1)}, bf16[1,1024,512]{2,1,0:T(8,128)(2,1)S(1)}, u32[]{:S(2)}, u32[]{:S(2)}) %collective-permute-start.1) | collective-permute-done | bytes 1048608 | tf_op jit(solution)/shard_map/ppermute | solution.py:331
  22.9 0.0 copy-start.2
  23.0 1.0 %copy-done.2 = bf16[1,1024,512]{2,1,0:T(8,128)(2,1)} copy-done((bf16[1,1024,512]{2,1,0:T(8,128)(2,1)}, bf16[1,1024,512]{2,1,0:T(8,128)(2,1)S(1)}, u32[]{:S(2)}) %copy-start.2) | copy-done | bytes 1048600
  23.9 1.2 %fetch.1.right_oth = bf16[1024,512]{1,0:T(8,128)(2,1)S(1)} custom-call(bf16[1,1024,512]{2,1,0:T(8,128)(2,1)} %copy-done.2), custom_call_target="tpu_custom_call" | custom-call | bytes 2097152 | tf_op jit(solution)/shard_map/fetch/pallas_call | solution.py:79
  25.1 21.7 %all-to-all-done = bf16[128,16,512]{2,1,0:T(8,128)(2,1)S(1)} async-done(((bf16[128,16,512]{2,1,0:T(8,128)(2,1)}), bf16[128,16,512]{2,1,0:T(8,128)(2,1)S(1)}, u32[]{:S(2)}, u32[]{:S(2)}) %all-to-all-start) | async-done | bytes 2097184 | tf_op jit(solution)/shard_map/all_to_all | solution.py:327
  46.8 6.7 %roots.1 = (bf16[2,1024,512]{2,1,0:T(8,128)(2,1)}, bf16[2,1024,512]{2,1,0:T(8,128)(2,1)}) custom-call(s32[1]{0:T(128)} %bitcast.which_ref.rep_ref.slot_ref, bf16[2,1024,512]{2,1,0:T(8,128)(2,1)S(1)} %bitcast.4, bf16[2,1024,512]{2,1,0:T(8,128)(2,1)} %right_ref.1, bf16[1024,512]{1,0:T(8,128)(2,1)S(1)} %fetch.1.right_oth, bf16[2,1024,1024]{2,1,0:T(8,128)(2,1)} %left_ref.1), custom_call_target="tpu_custom_call" | custom-call | flops 4294967296 | bytes 8388608 | tf_op jit(solution)/shard_map/roots/pallas_call | solution.py:189
  53.5 1.2 %collective-permute-start.2 = (bf16[2,1024,512]{2,1,0:T(8,128)(2,1)}, bf16[2,1024,512]{2,1,0:T(8,128)(2,1)}, u32[]{:S(2)}, u32[]{:S(2)}) collective-permute-start(bf16[2,1024,512]{2,1,0:T(8,128)(2,1)} %get-tuple-element.17.grad_ref), channel_id=1, source_target_pairs={{0,64},{64,0},{1,65},{65,1},{2,66},{66,2},{3,67},{67,3},{4,68},{68... | collective-permute-start | bytes 6291464 | tf_op jit(solution)/shard_map/ppermute | solution.py:339
  54.7 5.1 %all-to-all-start.1 = ((bf16[128,16,512]{2,1,0:T(8,128)(2,1)}), bf16[128,16,512]{2,1,0:T(8,128)(2,1)S(1)}, u32[]{:S(2)}, u32[]{:S(2)}) async-start(bf16[128,16,512]{2,1,0:T(8,128)(2,1)} %bitcast.7), calls=%async_computation.1 | async-start | bytes 4194304 | tf_op jit(solution)/shard_map/all_to_all | solution.py:327
  59.8 0.2 fusion.1.held_ref
  60.0 0.0 copy-start.1
  60.0 1.6 %copy-done.1 = bf16[2,1024,512]{2,1,0:T(8,128)(2,1)S(1)} copy-done((bf16[2,1024,512]{2,1,0:T(8,128)(2,1)S(1)}, bf16[2,1024,512]{2,1,0:T(8,128)(2,1)}, u32[]{:S(2)}) %copy-start.1) | copy-done | bytes 2097176
  61.6 4.1 %grams.2 = (f32[2,512,1024]{2,1,0:T(8,128)}, f32[2,512,1024]{2,1,0:T(8,128)}) custom-call(s32[1]{0:T(128)} %bitcast.which_ref.rep_ref.slot_ref, s32[1]{0:T(128)} %bitcast.which_ref.rep_ref.slot_ref, s32[2]{0:T(128)S(1)} %fusion.1.held_ref, bf16[2,1024,512]{2,1,0:T(8,128)(2,1)S(1)} %copy-done.1), custom_call_target="tpu_custom_call" | custom-call | flops 2147483648 | bytes 6291456 | tf_op jit(solution)/shard_map/grams/pallas_call | solution.py:253
  65.7 0.0 collective-permute-done.2.grad_ref
  65.7 5.7 %grams.3 = (f32[2,512,1024]{2,1,0:T(8,128)}, f32[2,512,1024]{2,1,0:T(8,128)}) custom-call(s32[1]{0:T(128)} %bitcast.which_ref.rep_ref.slot_ref, s32[1]{0:T(128)S(6)} %sub.13.which_ref.slot_ref, s32[2]{0:T(128)S(1)} %fusion.1.held_ref, bf16[2,1024,512]{2,1,0:T(8,128)(2,1)} %collective-permute-done.2.grad_ref, ...), custom_call_target="tpu_custom_call", output_to_operand_aliasing={{0}: (4, {}), {1}: (5, {})} | custom-call | flops 2147483648 | bytes 6291456 | tf_op jit(solution)/shard_map/grams/pallas_call | solution.py:253
  71.4 16.9 %all-to-all-done.1.pieces_ref = bf16[128,16,512]{2,1,0:T(8,128)(2,1)S(1)} async-done(((bf16[128,16,512]{2,1,0:T(8,128)(2,1)}), bf16[128,16,512]{2,1,0:T(8,128)(2,1)S(1)}, u32[]{:S(2)}, u32[]{:S(2)}) %all-to-all-start.1) | async-done | bytes 2097184 | tf_op jit(solution)/shard_map/all_to_all | solution.py:327
  88.4 1.6 %place.1 = bf16[1280,512]{1,0:T(8,128)(2,1)} custom-call(s32[80]{0:T(128)S(1)} %get-tuple-element.21.source_ref, s32[80]{0:T(128)S(1)} %copy-done, bf16[128,16,512]{2,1,0:T(8,128)(2,1)S(1)} %all-to-all-done.1.pieces_ref), custom_call_target="tpu_custom_call" | custom-call | bytes 2621440 | tf_op jit(solution)/shard_map/place/pallas_call | solution.py:286
  (2 shorter events, 0.0 us)
Async XLA Ops:
  1.9 2.8 %copy-start.3 = (s32[80]{0:T(128)S(1)}, s32[80]{0:T(128)}, u32[]{:S(2)}) copy-start(s32[80]{0:T(128)} %param.6) | copy-start | bytes 964
  2.0 2.9 %copy-start = (s32[80]{0:T(128)S(1)}, s32[80]{0:T(128)}, u32[]{:S(2)}) copy-start(s32[80]{0:T(128)} %row_ref.1) | copy-start | bytes 964
  2.0 4.2 %collective-permute-start = (bf16[1280,512]{1,0:T(8,128)(2,1)S(1)}, bf16[1280,512]{1,0:T(8,128)(2,1)S(1)}, u32[]{:S(2)}, u32[]{:S(2)}) collective-permute-start(bf16[1280,512]{1,0:T(8,128)(2,1)S(1)} %strip.2), channel_id=1, source_target_pairs={{0,64},{64,0},{1,65},{65,1},{2,66},{66,2},{3,67},{67,3},{4,68},{68... | collective-permute-start | bytes 3932168 | tf_op jit(solution)/shard_map/ppermute | solution.py:313
  7.7 39.1 %all-to-all-start = ((bf16[128,16,512]{2,1,0:T(8,128)(2,1)}), bf16[128,16,512]{2,1,0:T(8,128)(2,1)S(1)}, u32[]{:S(2)}, u32[]{:S(2)}) async-start(bf16[128,16,512]{2,1,0:T(8,128)(2,1)} %pack.1), calls=%async_computation | async-start | bytes 4194304 | tf_op jit(solution)/shard_map/all_to_all | solution.py:327
  19.5 3.4 %collective-permute-start.1 = (bf16[1,1024,512]{2,1,0:T(8,128)(2,1)S(1)}, bf16[1,1024,512]{2,1,0:T(8,128)(2,1)S(1)}, u32[]{:S(2)}, u32[]{:S(2)}) collective-permute-start(bf16[1,1024,512]{2,1,0:T(8,128)(2,1)S(1)} %constant_dynamic-slice_fusion), channel_id=1, source_target_pairs={{0,64},{64,0},{1,65},{65,1},{2,66},{66,2},{3,67},{67,3},{4,68},{68... | collective-permute-start | bytes 3145736 | tf_op jit(solution)/shard_map/ppermute | solution.py:331
  22.9 1.0 %copy-start.2 = (bf16[1,1024,512]{2,1,0:T(8,128)(2,1)}, bf16[1,1024,512]{2,1,0:T(8,128)(2,1)S(1)}, u32[]{:S(2)}) copy-start(bf16[1,1024,512]{2,1,0:T(8,128)(2,1)S(1)} %collective-permute-done.1.right_ref) | copy-start | bytes 3145732
  53.5 12.2 %collective-permute-start.2 = (bf16[2,1024,512]{2,1,0:T(8,128)(2,1)}, bf16[2,1024,512]{2,1,0:T(8,128)(2,1)}, u32[]{:S(2)}, u32[]{:S(2)}) collective-permute-start(bf16[2,1024,512]{2,1,0:T(8,128)(2,1)} %get-tuple-element.17.grad_ref), channel_id=1, source_target_pairs={{0,64},{64,0},{1,65},{65,1},{2,66},{66,2},{3,67},{67,3},{4,68},{68... | collective-permute-start | bytes 6291464 | tf_op jit(solution)/shard_map/ppermute | solution.py:339
  54.7 33.7 %all-to-all-start.1 = ((bf16[128,16,512]{2,1,0:T(8,128)(2,1)}), bf16[128,16,512]{2,1,0:T(8,128)(2,1)S(1)}, u32[]{:S(2)}, u32[]{:S(2)}) async-start(bf16[128,16,512]{2,1,0:T(8,128)(2,1)} %bitcast.7), calls=%async_computation.1 | async-start | bytes 4194304 | tf_op jit(solution)/shard_map/all_to_all | solution.py:327
  60.0 1.6 %copy-start.1 = (bf16[2,1024,512]{2,1,0:T(8,128)(2,1)S(1)}, bf16[2,1024,512]{2,1,0:T(8,128)(2,1)}, u32[]{:S(2)}) copy-start(bf16[2,1024,512]{2,1,0:T(8,128)(2,1)} %get-tuple-element.17.grad_ref) | copy-start | bytes 6291460

commit v7 on v5

--- a/solution.py
+++ b/solution.py
@@ -149,14 +149,14 @@
     fetch_left.start()
     for k, right in ((1, right_oth), (0, right_own)):
         if k == 0:
+            grad_sq = jnp.zeros((1, strip), jnp.float32)
+            for j in range(strips):
+                value = grad_ref[j].astype(jnp.float32)
+                grad_sq += jnp.sum(value * value, axis=0, keepdims=True)
             fetch_right.wait()
         wide = jnp.concatenate([grad_ref[j] for j in range(strips)], axis=1)
         acc = jnp.dot(wide, right[...], preferred_element_type=jnp.float32)
         half[k] = acc.astype(half.dtype)
-    grad_sq = jnp.zeros((1, strip), jnp.float32)
-    for k in range(strips):
-        value = grad_ref[k].astype(jnp.float32)
-        grad_sq += jnp.sum(value * value, axis=0, keepdims=True)
     fetch_left.wait()
     keep.start()
     pre_sq = jnp.zeros((1, strip), jnp.float32)

time: 90.4 us -> 90.4 us (level)
  no operation moved by 1% of the time
where the time goes in v7:
time: 90.4 us; the launch traced here: 89.9 us
  waiting for transfers between devices  43.1 us (48%)
  Pallas kernels  22.5 us (25%)
  starting transfers between devices  19.4 us (21%)
  local copies, waits for them, and re-layouts  3.87 us (4%)
    all_to_all x2, waiting for transfers between devices, exchange(): return lax.all_to_all(x, BOTH, split_axis=0, concat_axis=0, tiled=True)  39.7 us
    all_to_all x2, starting transfers between devices, exchange(): return lax.all_to_all(x, BOTH, split_axis=0, concat_axis=0, tiled=True)  15.5 us
    pallas_call x1, Pallas kernels, grams(): pl.pallas_call(functools.partial(gram_kernel, steps), grid_spec=pltpu.Pre...  8.8 us
    pallas_call x1, Pallas kernels, apply_roots(): pl.pallas_call(functools.partial(root_kernel, steps), grid_spec=pltpu.Pre...  6.67 us
    pallas_call x2, Pallas kernels, take_strip(): pl.pallas_call(functools.partial(strip_kernel, steps), grid_spec=pltpu.Pr...  2.61 us
    unnamed x8, local copies, waits for them, and re-layouts  2.57 us
    ppermute x1, waiting for transfers between devices, local(): lax.ppermute(lax.dynamic_slice_in_dim(right_later, 1 - me, 1, 0), 'rep',...  2.29 us
  transfers between devices with their start and end apart: 5, of which 4 were waited for; matrix products, arithmetic and copies ran while one was open for 2% of the time, Pallas kernels for 13%

profile of v7, /device:TPU:1, one launch (start us, length us, event | category | flops | bytes accessed | tf_op | source)
XLA Modules:
  0.0 89.9 jit_solution(16339088196335145871)
XLA Ops:
  0.6 1.3 %strip.2 = bf16[1280,512]{1,0:T(8,128)(2,1)S(1)} custom-call(s32[1]{0:T(128)S(6)} %sub.13.which_ref, bf16[1280,1024]{1,0:T(8,128)(2,1)} %bitcast.5), custom_call_target="tpu_custom_call" | custom-call | bytes 2621440 | tf_op jit(solution)/shard_map/strip/pallas_call | solution.py:50
  1.9 0.0 copy-start.3
  2.0 0.0 copy-start
  2.0 1.5 %collective-permute-start = (bf16[1280,512]{1,0:T(8,128)(2,1)S(1)}, bf16[1280,512]{1,0:T(8,128)(2,1)S(1)}, u32[]{:S(2)}, u32[]{:S(2)}) collective-permute-start(bf16[1280,512]{1,0:T(8,128)(2,1)S(1)} %strip.2), channel_id=1, source_target_pairs={{0,64},{64,0},{1,65},{65,1},{2,66},{66,2},{3,67},{67,3},{4,68},{68... | collective-permute-start | bytes 3932168 | tf_op jit(solution)/shard_map/ppermute | solution.py:315
  3.5 1.3 %strip.3.mine_ref = bf16[1280,512]{1,0:T(8,128)(2,1)S(1)} custom-call(s32[1]{0:T(128)} %bitcast.which_ref.rep_ref, bf16[1280,1024]{1,0:T(8,128)(2,1)} %bitcast.6), custom_call_target="tpu_custom_call" | custom-call | bytes 2621440 | tf_op jit(solution)/shard_map/strip/pallas_call | solution.py:50
  4.8 0.0 copy-done.3
  4.8 0.1 select_reduce_fusion.1
  4.9 0.0 copy-done
  4.9 0.1 select_reduce_fusion.slot_ref
  5.0 1.1 %collective-permute-done.theirs_ref = bf16[1280,512]{1,0:T(8,128)(2,1)S(1)} collective-permute-done((bf16[1280,512]{1,0:T(8,128)(2,1)S(1)}, bf16[1280,512]{1,0:T(8,128)(2,1)S(1)}, u32[]{:S(2)}, u32[]{:S(2)}) %collective-permute-start) | collective-permute-done | bytes 1310752 | tf_op jit(solution)/shard_map/ppermute | solution.py:315
  6.1 1.6 %pack.1 = bf16[128,16,512]{2,1,0:T(8,128)(2,1)} custom-call(s32[80]{0:T(128)S(1)} %select_reduce_fusion.slot_ref, bf16[1280,512]{1,0:T(8,128)(2,1)S(1)} %strip.3.mine_ref, bf16[1280,512]{1,0:T(8,128)(2,1)S(1)} %collective-permute-done.theirs_ref), custom_call_target="tpu_custom_call" | custom-call | flops 655360 | bytes 1310720 | tf_op jit(solution)/shard_map/pack/pallas_call | solution.py:106
  7.7 10.5 %all-to-all-start = ((bf16[128,16,512]{2,1,0:T(8,128)(2,1)}), bf16[128,16,512]{2,1,0:T(8,128)(2,1)S(1)}, u32[]{:S(2)}, u32[]{:S(2)}) async-start(bf16[128,16,512]{2,1,0:T(8,128)(2,1)} %pack.1), calls=%async_computation | async-start | bytes 4194304 | tf_op jit(solution)/shard_map/all_to_all | solution.py:329
  18.2 1.3 %constant_dynamic-slice_fusion = bf16[1,1024,512]{2,1,0:T(8,128)(2,1)S(1)} fusion(bf16[2,1024,512]{2,1,0:T(8,128)(2,1)} %right_ref.1, s32[]{:T(128)S(6)} %select_n.24), kind=kLoop, calls=%fused_computation.13 | loop fusion | bytes 2097156 | tf_op jit(solution)/shard_map/dynamic_slice | solution.py:334
  19.5 1.1 %collective-permute-start.1 = (bf16[1,1024,512]{2,1,0:T(8,128)(2,1)S(1)}, bf16[1,1024,512]{2,1,0:T(8,128)(2,1)S(1)}, u32[]{:S(2)}, u32[]{:S(2)}) collective-permute-start(bf16[1,1024,512]{2,1,0:T(8,128)(2,1)S(1)} %constant_dynamic-slice_fusion), channel_id=1, source_target_pairs={{0,64},{64,0},{1,65},{65,1},{2,66},{66,2},{3,67},{67,3},{4,68},{68... | collective-permute-start | bytes 3145736 | tf_op jit(solution)/shard_map/ppermute | solution.py:333
  20.7 2.3 %collective-permute-done.1.right_ref = bf16[1,1024,512]{2,1,0:T(8,128)(2,1)S(1)} collective-permute-done((bf16[1,1024,512]{2,1,0:T(8,128)(2,1)S(1)}, bf16[1,1024,512]{2,1,0:T(8,128)(2,1)S(1)}, u32[]{:S(2)}, u32[]{:S(2)}) %collective-permute-start.1) | collective-permute-done | bytes 1048608 | tf_op jit(solution)/shard_map/ppermute | solution.py:333
  22.9 0.0 copy-start.2
  23.0 1.0 %copy-done.2 = bf16[1,1024,512]{2,1,0:T(8,128)(2,1)} copy-done((bf16[1,1024,512]{2,1,0:T(8,128)(2,1)}, bf16[1,1024,512]{2,1,0:T(8,128)(2,1)S(1)}, u32[]{:S(2)}) %copy-start.2) | copy-done | bytes 1048600
  23.9 1.2 %fetch.1.right_oth = bf16[1024,512]{1,0:T(8,128)(2,1)S(1)} custom-call(bf16[1,1024,512]{2,1,0:T(8,128)(2,1)} %copy-done.2), custom_call_target="tpu_custom_call" | custom-call | bytes 2097152 | tf_op jit(solution)/shard_map/fetch/pallas_call | solution.py:79
  25.1 21.7 %all-to-all-done = bf16[128,16,512]{2,1,0:T(8,128)(2,1)S(1)} async-done(((bf16[128,16,512]{2,1,0:T(8,128)(2,1)}), bf16[128,16,512]{2,1,0:T(8,128)(2,1)S(1)}, u32[]{:S(2)}, u32[]{:S(2)}) %all-to-all-start) | async-done | bytes 2097184 | tf_op jit(solution)/shard_map/all_to_all | solution.py:329
  46.8 6.7 %roots.1 = (bf16[2,1024,512]{2,1,0:T(8,128)(2,1)}, bf16[2,1024,512]{2,1,0:T(8,128)(2,1)}) custom-call(s32[1]{0:T(128)} %bitcast.which_ref.rep_ref, bf16[2,1024,512]{2,1,0:T(8,128)(2,1)S(1)} %bitcast.4, bf16[2,1024,512]{2,1,0:T(8,128)(2,1)} %right_ref.1, bf16[1024,512]{1,0:T(8,128)(2,1)S(1)} %fetch.1.right_oth, bf16[2,1024,1024]{2,1,0:T(8,128)(2,1)} %left_ref.1), custom_call_target="tpu_custom_call" | custom-call | flops 4294967296 | bytes 8388608 | tf_op jit(solution)/shard_map/roots/pallas_call | solution.py:189
  53.5 1.2 %collective-permute-start.2 = (bf16[2,1024,512]{2,1,0:T(8,128)(2,1)}, bf16[2,1024,512]{2,1,0:T(8,128)(2,1)}, u32[]{:S(2)}, u32[]{:S(2)}) collective-permute-start(bf16[2,1024,512]{2,1,0:T(8,128)(2,1)} %get-tuple-element.15.own_ref), channel_id=1, source_target_pairs={{0,64},{64,0},{1,65},{65,1},{2,66},{66,2},{3,67},{67,3},{4,68},{68... | collective-permute-start | bytes 6291464 | tf_op jit(solution)/shard_map/ppermute | solution.py:341
  54.7 5.1 %all-to-all-start.1 = ((bf16[128,16,512]{2,1,0:T(8,128)(2,1)}), bf16[128,16,512]{2,1,0:T(8,128)(2,1)S(1)}, u32[]{:S(2)}, u32[]{:S(2)}) async-start(bf16[128,16,512]{2,1,0:T(8,128)(2,1)} %bitcast.7), calls=%async_computation.1 | async-start | bytes 4194304 | tf_op jit(solution)/shard_map/all_to_all | solution.py:329
  59.8 0.2 fusion.1.held_ref
  60.0 0.0 collective-permute-done.2.oth_ref
  60.0 0.0 copy-start.1
  60.0 1.6 %copy-done.1 = bf16[2,1024,512]{2,1,0:T(8,128)(2,1)S(1)} copy-done((bf16[2,1024,512]{2,1,0:T(8,128)(2,1)S(1)}, bf16[2,1024,512]{2,1,0:T(8,128)(2,1)}, u32[]{:S(2)}) %copy-start.1) | copy-done | bytes 2097176
  61.6 8.8 %grams.1 = (f32[2,512,1024]{2,1,0:T(8,128)}, f32[2,512,1024]{2,1,0:T(8,128)}) custom-call(s32[1]{0:T(128)} %bitcast.which_ref.rep_ref, s32[2]{0:T(128)S(1)} %fusion.1.held_ref, bf16[2,1024,512]{2,1,0:T(8,128)(2,1)S(1)} %copy-done.1, bf16[2,1024,512]{2,1,0:T(8,128)(2,1)} %collective-permute-done.2.oth_ref), custom_call_target="tpu_custom_call" | custom-call | flops 4294967296 | bytes 12582912 | tf_op jit(solution)/shard_map/grams/pallas_call | solution.py:257
  70.4 18.0 %all-to-all-done.1.pieces_ref = bf16[128,16,512]{2,1,0:T(8,128)(2,1)S(1)} async-done(((bf16[128,16,512]{2,1,0:T(8,128)(2,1)}), bf16[128,16,512]{2,1,0:T(8,128)(2,1)S(1)}, u32[]{:S(2)}, u32[]{:S(2)}) %all-to-all-start.1) | async-done | bytes 2097184 | tf_op jit(solution)/shard_map/all_to_all | solution.py:329
  88.4 1.6 %place.1 = bf16[1280,512]{1,0:T(8,128)(2,1)} custom-call(s32[80]{0:T(128)S(1)} %get-tuple-element.17.source_ref, s32[80]{0:T(128)S(1)} %copy-done, bf16[128,16,512]{2,1,0:T(8,128)(2,1)S(1)} %all-to-all-done.1.pieces_ref), custom_call_target="tpu_custom_call" | custom-call | bytes 2621440 | tf_op jit(solution)/shard_map/place/pallas_call | solution.py:288
  (2 shorter events, 0.0 us)
Async XLA Ops:
  1.9 2.8 %copy-start.3 = (s32[80]{0:T(128)S(1)}, s32[80]{0:T(128)}, u32[]{:S(2)}) copy-start(s32[80]{0:T(128)} %param.6) | copy-start | bytes 964
  2.0 2.9 %copy-start = (s32[80]{0:T(128)S(1)}, s32[80]{0:T(128)}, u32[]{:S(2)}) copy-start(s32[80]{0:T(128)} %row_ref.1) | copy-start | bytes 964
  2.0 4.2 %collective-permute-start = (bf16[1280,512]{1,0:T(8,128)(2,1)S(1)}, bf16[1280,512]{1,0:T(8,128)(2,1)S(1)}, u32[]{:S(2)}, u32[]{:S(2)}) collective-permute-start(bf16[1280,512]{1,0:T(8,128)(2,1)S(1)} %strip.2), channel_id=1, source_target_pairs={{0,64},{64,0},{1,65},{65,1},{2,66},{66,2},{3,67},{67,3},{4,68},{68... | collective-permute-start | bytes 3932168 | tf_op jit(solution)/shard_map/ppermute | solution.py:315
  7.7 39.1 %all-to-all-start = ((bf16[128,16,512]{2,1,0:T(8,128)(2,1)}), bf16[128,16,512]{2,1,0:T(8,128)(2,1)S(1)}, u32[]{:S(2)}, u32[]{:S(2)}) async-start(bf16[128,16,512]{2,1,0:T(8,128)(2,1)} %pack.1), calls=%async_computation | async-start | bytes 4194304 | tf_op jit(solution)/shard_map/all_to_all | solution.py:329
  19.5 3.4 %collective-permute-start.1 = (bf16[1,1024,512]{2,1,0:T(8,128)(2,1)S(1)}, bf16[1,1024,512]{2,1,0:T(8,128)(2,1)S(1)}, u32[]{:S(2)}, u32[]{:S(2)}) collective-permute-start(bf16[1,1024,512]{2,1,0:T(8,128)(2,1)S(1)} %constant_dynamic-slice_fusion), channel_id=1, source_target_pairs={{0,64},{64,0},{1,65},{65,1},{2,66},{66,2},{3,67},{67,3},{4,68},{68... | collective-permute-start | bytes 3145736 | tf_op jit(solution)/shard_map/ppermute | solution.py:333
  22.9 1.0 %copy-start.2 = (bf16[1,1024,512]{2,1,0:T(8,128)(2,1)}, bf16[1,1024,512]{2,1,0:T(8,128)(2,1)S(1)}, u32[]{:S(2)}) copy-start(bf16[1,1024,512]{2,1,0:T(8,128)(2,1)S(1)} %collective-permute-done.1.right_ref) | copy-start | bytes 3145732
  53.5 6.5 %collective-permute-start.2 = (bf16[2,1024,512]{2,1,0:T(8,128)(2,1)}, bf16[2,1024,512]{2,1,0:T(8,128)(2,1)}, u32[]{:S(2)}, u32[]{:S(2)}) collective-permute-start(bf16[2,1024,512]{2,1,0:T(8,128)(2,1)} %get-tuple-element.15.own_ref), channel_id=1, source_target_pairs={{0,64},{64,0},{1,65},{65,1},{2,66},{66,2},{3,67},{67,3},{4,68},{68... | collective-permute-start | bytes 6291464 | tf_op jit(solution)/shard_map/ppermute | solution.py:341
  54.7 33.7 %all-to-all-start.1 = ((bf16[128,16,512]{2,1,0:T(8,128)(2,1)}), bf16[128,16,512]{2,1,0:T(8,128)(2,1)S(1)}, u32[]{:S(2)}, u32[]{:S(2)}) async-start(bf16[128,16,512]{2,1,0:T(8,128)(2,1)} %bitcast.7), calls=%async_computation.1 | async-start | bytes 4194304 | tf_op jit(solution)/shard_map/all_to_all | solution.py:329
  60.0 1.6 %copy-start.1 = (bf16[2,1024,512]{2,1,0:T(8,128)(2,1)S(1)}, bf16[2,1024,512]{2,1,0:T(8,128)(2,1)}, u32[]{:S(2)}) copy-start(bf16[2,1024,512]{2,1,0:T(8,128)(2,1)} %get-tuple-element.15.own_ref) | copy-start | bytes 6291460
